TPU v7x, 256 devices: a whole 4x4x8 slice. The times are simulated.
256 devices in a mesh: section: 2 (over x_lo), group: 4 (over x_hi, core), mp: 32 (over y, z).
Axes of the slice: x: 4 (x_hi: 2, x_lo: 2; x = x_hi * 2 + x_lo), y: 4, z: 8, core: 2. Of those that a mesh axis runs over, the one named last changes fastest.
Arguments:
- hidden: bfloat16 [2, 3072, 28672], P('section', 'group', 'mp'), may hold values from -6 to 6
- down_weight: bfloat16 [2, 28672, 8192], P('section', 'mp', 'group'), may hold values from -0.0625 to 0.0625
- residual: bfloat16 [2, 3072, 8192], P('section', ('group', 'mp')), may hold values from -12 to 12
- norm_gain: float32 [2, 8192], P('section', 'mp'), may hold values from 0.25 to 1.75
Outputs:
- handed: bfloat16 [2, 3072, 8192], P('section', 'group', 'mp')
- normed: bfloat16 [2, 3072, 8192], P('section', 'group', 'mp')
All inputs are finite; a program needn't handle non-finite values.
Results may differ from a plain program's by a relative error of at most 0.017.
Values may be sent and summed in bfloat16 or wider, within the bound.
No kernel may reach another device: no remote copies, remote signals or barrier semaphores. Data moves between devices by JAX's collectives and lax.ppermute only.
A program may use at most 128 MiB of HBM per device.

v0:
```python
import jax
import jax.numpy as jnp
from jax import lax
from jax.sharding import PartitionSpec as P

D = 8192


def passed_along(x, axis, by):
    length = lax.axis_size(axis)
    return lax.ppermute(x, axis, [(i, (i + by) % length) for i in range(length)])


def shards(hidden, down_weight, residual, norm_gain):
    local_hidden = hidden[0]
    local_weight = down_weight[0]
    term = jnp.dot(
        local_hidden,
        lax.all_gather(local_weight, "group", axis=1, tiled=True),
        preferred_element_type=jnp.float32,
    )
    summed = lax.psum_scatter(
        term.astype(jnp.bfloat16), "mp", scatter_dimension=0, tiled=True
    ).astype(jnp.float32)
    stream = (residual[0].astype(jnp.float32) + summed).astype(jnp.bfloat16)
    regrouped = lax.all_to_all(stream, "mp", split_axis=1, concat_axis=0, tiled=True)
    handed = passed_along(regrouped, "section", 1)
    values = handed.astype(jnp.float32)
    squares = lax.psum(jnp.sum(values * values, axis=1), "mp")
    scale = lax.rsqrt(squares / D + 1e-05)
    normed = (values * scale[:, None] * norm_gain[0][None, :]).astype(jnp.bfloat16)
    return (handed[None], normed[None])


def solution(mesh):
    placed = (
        P("section", "group", "mp"),
        P("section", "mp", "group"),
        P("section", ("group", "mp"), None),
        P("section", "mp"),
    )
    return jax.shard_map(
        shards,
        mesh=mesh,
        in_specs=placed,
        out_specs=(P("section", "group", "mp"), P("section", "group", "mp")),
        check_vma=False,
    )
```

profile of v0, /device:TPU:2, one launch (start us, length us, event | category | flops | bytes accessed | tf_op | source)
XLA Modules:
  0.0 479.8 jit_solution(16720687751090415899)
XLA Ops:
  7.2 0.0 copy-start
  7.2 0.0 all-gather.3.cloned.1.call-start
  7.2 0.7 all-gather.3.cloned.1.call-update
  7.9 0.0 reduce-scatter.2.cloned.1.call-start
  8.0 104.6 %all-gather.3.cloned.1.call-done = bf16[1,896,8192]{2,1,0:T(8,128)(2,1)} async-done(((bf16[1,896,2048]{2,1,0:T(8,128)(2,1)}), bf16[1,896,8192]{2,1,0:T(8,128)(2,1)}) %all-gather.3.cloned.1.call-update) | async-done | bytes 14680080 | tf_op jit(solution)/shard_map/all_gather | solution.py:19
  112.5 0.0 copy-done
  112.5 20.6 %fusion.2 = bf16[768,8192]{1,0:T(8,128)(2,1)} fusion(bf16[1,896,8192]{2,1,0:T(8,128)(2,1)} %all-gather.3.cloned.1.call-done, bf16[1,768,896]{2,1,0:T(8,128)(2,1)S(1)} %copy-done), kind=kOutput, calls=%fused_computation.2 | convolution fusion | flops 11280580608 | bytes 28639232 | tf_op jit(solution)/shard_map/dot_general | solution.py:17
  133.2 0.0 copy-start.1
  133.2 0.0 copy-start.2
  133.2 0.0 reduce-scatter.2.cloned.1.call-update
  133.2 238.1 %reduce-scatter.2.cloned.1.call-done = bf16[24,8192]{1,0:T(8,128)(2,1)} async-done(((bf16[768,8192]{1,0:T(8,128)(2,1)}), bf16[24,8192]{1,0:T(8,128)(2,1)}) %reduce-scatter.2.cloned.1.call-update) | async-done | bytes 393232 | tf_op jit(solution)/shard_map/reduce_scatter | solution.py:22
  371.3 0.0 copy-done.1
  371.3 1.1 fusion.9
  372.5 18.4 %all_to_all.19 = bf16[24,32,256]{2,0,1:T(8,128)(2,1)S(1)} all-to-all(bf16[24,32,256]{2,0,1:T(8,128)(2,1)S(1)} %bitcast.23), channel_id=1, replica_groups=mesh['section'=2,'group'=4,'mp'=32] {'mp'}, dimensions={1} | all-to-all | bytes 786432 | tf_op jit(solution)/shard_map/all_to_all | solution.py:26
  390.9 0.6 collective-permute-start
  391.4 7.2 %collective-permute-done = bf16[768,256]{1,0:T(8,128)(2,1)S(1)} collective-permute-done((bf16[768,256]{1,0:T(8,128)(2,1)S(1)}, bf16[768,256]{1,0:T(8,128)(2,1)S(1)}, u32[]{:S(2)}, u32[]{:S(2)}) %collective-permute-start) | collective-permute-done | bytes 393248 | tf_op jit(solution)/shard_map/ppermute | solution.py:11
  398.7 0.2 fusion.6
  398.8 72.5 %psum.7 = f32[768]{0:T(1024)S(1)} all-reduce(f32[768]{0:T(1024)S(1)} %fusion.6), channel_id=1, replica_groups=mesh['section'=2,'group'=4,'mp'=32] {'mp'}, use_global_device_ids=true, to_apply=%region_2.0 | all-reduce | flops 768 | bytes 6144 | tf_op jit(solution)/shard_map/psum | solution.py:29
  471.3 0.0 copy-done.2
  471.3 0.9 fusion.10
  472.3 0.7 copy.12
  (2 shorter events, 0.0 us)
Async XLA Ops:
  7.2 105.3 %copy-start = (bf16[1,768,896]{2,1,0:T(8,128)(2,1)S(1)}, bf16[1,768,896]{2,1,0:T(8,128)(2,1)}, u32[]{:S(2)}) copy-start(bf16[1,768,896]{2,1,0:T(8,128)(2,1)} %param.4) | copy-start | bytes 4128772
  7.2 105.3 %all-gather.3.cloned.1.call-start = ((), (), s32[]{:S(2)}) async-start(), calls=%async_computation.3 | async-start | bytes 18350080 | tf_op jit(solution)/shard_map/all_gather | solution.py:19
  7.9 363.4 %reduce-scatter.2.cloned.1.call-start = ((), (), s32[]{:S(2)}) async-start(), calls=%async_computation.2 | async-start | bytes 12976128 | tf_op jit(solution)/shard_map/reduce_scatter | solution.py:22
  133.2 238.2 %copy-start.1 = (bf16[1,24,8192]{2,1,0:T(8,128)(2,1)S(1)}, bf16[1,24,8192]{2,1,0:T(8,128)(2,1)}, u32[]{:S(2)}) copy-start(bf16[1,24,8192]{2,1,0:T(8,128)(2,1)} %param.6) | copy-start | bytes 1179652
  133.2 338.2 %copy-start.2 = (f32[1,256]{1,0:T(1,128)S(1)}, f32[1,256]{1,0:T(1,128)}, u32[]{:S(2)}) copy-start(f32[1,256]{1,0:T(1,128)} %param.7) | copy-start | bytes 3076
  390.9 7.8 %collective-permute-start = (bf16[768,256]{1,0:T(8,128)(2,1)S(1)}, bf16[768,256]{1,0:T(8,128)(2,1)S(1)}, u32[]{:S(2)}, u32[]{:S(2)}) collective-permute-start(bf16[768,256]{1,0:T(8,128)(2,1)S(1)} %bitcast.25), channel_id=1, source_target_pairs={{0,128},{128,0},{1,129},{129,1},{2,130},{130,2},{3,131},{131,3},{4... | collective-permute-start | bytes 1179656 | tf_op jit(solution)/shard_map/ppermute | solution.py:11
Sparse Core Ops, SparseCore 0:
  9.8 102.6 all-gather.2
  133.3 237.9 reduce-scatter.1
where the time goes:
time: 480 us
  waiting for transfers between devices  351 us (73%)
  blocking collectives  90.9 us (19%)
  matrix products  20.6 us (4%)
  between operations  14.1 us (3%)
    reduce_scatter x1, waiting for transfers between devices, shards(): lax.psum_scatter(term.astype(jnp.bfloat16), 'mp', scatter_dimension=0, ti...  238 us
    all_gather x1, waiting for transfers between devices, shards(): lax.all_gather(local_weight, 'group', axis=1, tiled=True)  105 us
    psum x1, blocking collectives, shards(): squares = lax.psum(jnp.sum(values * values, axis=1), 'mp')  72.5 us
    dot_general x1, matrix products, shards(): jnp.dot(local_hidden, lax.all_gather(local_weight, 'group', axis=1, tiled...  20.6 us
    all_to_all x1, blocking collectives, shards(): lax.all_to_all(stream, 'mp', split_axis=1, concat_axis=0, tiled=True)  18.4 us
  transfers between devices with their start and end apart: 3, of which 3 were waited for; matrix products, arithmetic and copies ran while one was open for 0% of the time, Pallas kernels for 0%

commit v1 on v0

v1 whole, which is shorter than its diff:
```python
import jax
import jax.numpy as jnp
from jax import lax
from jax.sharding import Mesh
from jax.sharding import PartitionSpec as P

D = 8192
NZ, NY = 8, 4
ROWS, COLS = 768, 256
ZROWS = 320
AXES = ("s", "xh", "c", "y", "z")
F32, BF16 = jnp.float32, jnp.bfloat16


def shifted(x, axis, n, by):
    return lax.ppermute(x, axis, [(i, (i + by) % n) for i in range(n)])


def flipped(x, *axes):
    n = 2 ** len(axes)
    return lax.ppermute(x, axes, [(i, n - 1 - i) for i in range(n)])


def ring_sum(piece, axis, n, cut):
    far = piece(n // 2)
    half = far.shape[cut] // 2
    low, high = (lax.slice_in_dim(far, i * half, (i + 1) * half, axis=cut) for i in (0, 1))
    up, down = shifted(low, axis, n, 1), shifted(high, axis, n, -1)
    for j in range(n // 2 - 1, 0, -1):
        ahead, behind = piece(j), piece(-j)
        if up.shape != ahead.shape:
            parts = [lax.slice_in_dim(ahead, i * half, (i + 1) * half, axis=cut) for i in (0, 1)]
            ahead = jnp.concatenate([parts[0] + up, parts[1]], axis=cut)
            parts = [lax.slice_in_dim(behind, i * half, (i + 1) * half, axis=cut) for i in (0, 1)]
            behind = jnp.concatenate([parts[0], parts[1] + down], axis=cut)
        else:
            ahead, behind = ahead + up, behind + down
        up, down = shifted(ahead, axis, n, 1), shifted(behind, axis, n, -1)
    return piece(0).astype(F32) + up.astype(F32) + down.astype(F32)


def by_columns(x, z):
    return lambda j: lax.dynamic_slice_in_dim(x, (z + j) % NZ * COLS, COLS, axis=1)


def by_rows(x, y):
    rows = x.shape[0] // NY
    return lambda j: lax.dynamic_slice_in_dim(x, (y + j) % NY * rows, rows, axis=0)


def scattered(h, w, res, y, z):
    partial = jnp.dot(h, w, preferred_element_type=F32).astype(BF16)
    at = (y * NZ + z) * res.shape[0]
    slab = lax.dynamic_slice_in_dim(partial, at, res.shape[0], axis=0)
    partial = lax.dynamic_update_slice_in_dim(partial, slab + res, at, axis=0)
    z_sum = ring_sum(by_columns(partial[:ZROWS], z), "z", NZ, 0).astype(BF16)
    y_sum = ring_sum(by_rows(partial[ZROWS:], y), "y", NY, 1).astype(BF16)
    z_first = ring_sum(by_rows(z_sum, y), "y", NY, 1)
    y_first = ring_sum(by_columns(y_sum, z), "z", NZ, 1)
    return jnp.concatenate([z_first, y_first], axis=0).astype(BF16)


def across(by):
    pairs = []
    for i in range(2 * 4 * NY * NZ):
        s, g, y, z = i // 128, i // 32 % 4, i // 8 % 4, i % 8
        pairs.append((i, (1 - s) * 128 + (y + by) % 4 * 32 + g * 8 + z))
    return pairs


def shards(hidden, down_weight, residual, norm_gain):
    h, w, gain = hidden[0], down_weight[0], norm_gain[0]
    xh, c, y, z = (lax.axis_index(a) for a in AXES[1:])
    group = xh * 2 + c
    h_core = flipped(h, "c")
    zero = c == 0
    got = [
        lax.ppermute(h, ("xh", "c"), [(k, 2 + k), (2 + k, k)]) for k in (0, 1)
    ]
    h_far = [
        jnp.where(c == k, got[k], lax.ppermute(got[k], "c", [(k, 1 - k)])) for k in (0, 1)
    ]
    res = residual[0].reshape(24, 4, 2048)
    part = lambda r: lax.dynamic_index_in_dim(res, group ^ r, axis=1, keepdims=False)
    res_near = [part(0), flipped(part(1), "c")]
    far = [flipped(part(2), "xh"), flipped(part(3), "xh", "c")]
    res_far = [jnp.where(zero, far[0], far[1]), jnp.where(zero, far[1], far[0])]
    blocks = [
        scattered(a, w, r, y, z)
        for a, r in zip([h, h_core] + h_far, res_near + res_far)
    ]
    stack = jnp.stack(blocks)
    place = [jnp.where(xh == g // 2, (c + g) % 2, 2 + g % 2) for g in range(4)]
    stream = jnp.stack(
        [lax.dynamic_index_in_dim(stack, p, axis=0, keepdims=False) for p in place]
    )
    wide = stream.astype(F32)
    squares = jnp.sum(wide * wide, axis=2)
    squares = squares + flipped(squares, "c") + flipped(squares, "xh") + flipped(squares, "xh", "c")
    squares = sum([shifted(squares, "z", NZ, j) for j in range(1, NZ)], squares)

    def hand(x):
        sent = [
            lax.ppermute(
                lax.dynamic_index_in_dim(x, (y + by) % 4, axis=0, keepdims=False),
                AXES,
                across(by),
            )
            for by in range(4)
        ]
        sent = jnp.stack(sent)
        quarters = [
            lax.dynamic_index_in_dim(sent, (group - q) % 4, axis=0, keepdims=False)
            for q in range(4)
        ]
        cut = ZROWS // 4
        return jnp.concatenate([q[:cut] for q in quarters] + [q[cut:] for q in quarters])

    handed = hand(stream)
    scale = lax.rsqrt(hand(squares) / D + 1e-05)
    normed = (handed.astype(F32) * scale[:, None] * gain[None, :]).astype(BF16)
    return (handed[None], normed[None])


def solution(mesh):
    fine = Mesh(mesh.devices.reshape(2, 2, 2, NY, NZ), AXES)
    group, mp = ("xh", "c"), ("y", "z")
    return jax.shard_map(
        shards,
        mesh=fine,
        in_specs=(P("s", group, mp), P("s", mp, group), P("s", group + mp, None), P("s", mp)),
        out_specs=(P("s", group, mp), P("s", group, mp)),
        check_vma=False,
    )
```

time: 480 us -> 356 us (0.74); the launches traced: 480 us -> 349 us
  waiting for transfers between devices: 351 us -> 126 us
  starting transfers between devices: 0.64 us -> 178 us
  blocking collectives: 90.9 us -> 0 us
  between operations: 14.1 us -> 2.71 us
  local copies, waits for them, and re-layouts: 0.79 us -> 11.7 us
  other arithmetic: 2.22 us -> 12.7 us
    reduce_scatter x1 -> x0, waiting for transfers between devices: 238 us -> none  [shards(): lax.psum_scatter(term.astype(jnp.bfloat16), 'mp', scatter_dimension=0, ti...]
    ppermute x1 -> x122, starting transfers between devices: 0.56 us -> 178 us  [the longest x103 150 us: shifted(): return lax.ppermute(x, axis, [(i, (i + by) % n) for i in range(n)])]
    ppermute x1 -> x122, waiting for transfers between devices: 7.22 us -> 126 us  [the longest x103 117 us: shifted(): return lax.ppermute(x, axis, [(i, (i + by) % n) for i in range(n)])]
    all_gather x1 -> x0, waiting for transfers between devices: 105 us -> none  [shards(): lax.all_gather(local_weight, 'group', axis=1, tiled=True)]
    psum x1 -> x0, blocking collectives: 72.5 us -> none  [shards(): squares = lax.psum(jnp.sum(values * values, axis=1), 'mp')]
    all_to_all x1 -> x0, blocking collectives: 18.4 us -> none  [shards(): lax.all_to_all(stream, 'mp', split_axis=1, concat_axis=0, tiled=True)]
    add x0 -> x42, other arithmetic: none -> 6.08 us  [the longest x16 3.21 us: ring_sum(): ahead = jnp.concatenate([parts[0] + up, parts[1]], axis=cut)]
    dot_general x1 -> x4, matrix products: 20.6 us -> 18.1 us  [scattered(): partial = jnp.dot(h, w, preferred_element_type=F32).astype(BF16)]
  transfers between devices with their start and end apart: 3 -> 122, of which waited for: 3 -> 48; matrix products, arithmetic and copies ran while one was open for 0% -> 8% of each run, Pallas kernels for 0% -> 0%
where the time goes in v1:
time: 356 us; the launch traced here: 349 us
  starting transfers between devices  178 us (50%)
  waiting for transfers between devices  126 us (35%)
  matrix products  18.1 us (5%)
  other arithmetic  12.7 us (4%)
  local copies, waits for them, and re-layouts  11.7 us (3%)
    ppermute x103, starting transfers between devices, shifted(): return lax.ppermute(x, axis, [(i, (i + by) % n) for i in range(n)])  150 us
    ppermute x103, waiting for transfers between devices, shifted(): return lax.ppermute(x, axis, [(i, (i + by) % n) for i in range(n)])  117 us
    dot_general x4, matrix products, scattered(): partial = jnp.dot(h, w, preferred_element_type=F32).astype(BF16)  18.1 us
    ppermute x8, starting transfers between devices, hand(): lax.ppermute(lax.dynamic_index_in_dim(x, (y + by) % 4, axis=0, keepdims=F...  14.6 us
  transfers between devices with their start and end apart: 122, of which 48 were waited for; matrix products, arithmetic and copies ran while one was open for 8% of the time, Pallas kernels for 0%

profile of v1, /device:TPU:2, one launch (start us, length us, event | category | flops | bytes accessed | tf_op | source)
XLA Modules:
  0.0 348.7 jit_solution(8209224911085230413)
XLA Ops:
  2.0 5.9 %fusion.8 = bf16[768,2048]{1,0:T(8,128)(2,1)S(1)} fusion(bf16[1,896,2048]{2,1,0:T(8,128)(2,1)} %param.5, bf16[1,768,896]{2,1,0:T(8,128)(2,1)} %param.4), kind=kOutput, calls=%fused_computation.8 | convolution fusion | flops 2820145152 | bytes 8192000 | tf_op jit(solution)/shard_map/dot_general | solution.py:52
  13.9 3.9 %collective-permute-start.4 = (bf16[160,256]{1,0:T(8,128)(2,1)}, bf16[160,256]{1,0:T(8,128)(2,1)}, u32[]{:S(2)}, u32[]{:S(2)}) collective-permute-start(bf16[160,256]{1,0:T(8,128)(2,1)} %get-tuple-element.35), channel_id=1, source_target_pairs={{0,7},{1,0},{2,1},{3,2},{4,3},{5,4},{6,5},{7,6},{8,15},{9,8},{10,9... | collective-permute-start | bytes 245768 | tf_op jit(solution)/shard_map/ppermute | solution.py:16
  38.7 4.0 %collective-permute-start.50 = (bf16[768,896]{1,0:T(8,128)(2,1)}, bf16[768,896]{1,0:T(8,128)(2,1)S(1)}, u32[]{:S(2)}, u32[]{:S(2)}) collective-permute-start(bf16[768,896]{1,0:T(8,128)(2,1)} %bitcast), channel_id=1, source_target_pairs={{0,64},{64,0},{1,65},{65,1},{2,66},{66,2},{3,67},{67,3},{4,68},{68... | collective-permute-start | bytes 4128776 | tf_op jit(solution)/shard_map/ppermute | solution.py:78
  51.6 3.7 %collective-permute-start.20 = (bf16[112,128]{1,0:T(8,128)(2,1)S(1)}, bf16[112,128]{1,0:T(8,128)(2,1)S(1)}, u32[]{:S(2)}, u32[]{:S(2)}) collective-permute-start(bf16[112,128]{1,0:T(8,128)(2,1)S(1)} %get-tuple-element.67), channel_id=1, source_target_pairs={{0,7},{1,0},{2,1},{3,2},{4,3},{5,4},{6,5},{7,6},{8,15},{9,8},{10,9... | collective-permute-start | bytes 86024 | tf_op jit(solution)/shard_map/ppermute | solution.py:16
  56.8 3.5 %collective-permute-start.7 = (bf16[320,256]{1,0:T(8,128)(2,1)S(1)}, bf16[320,256]{1,0:T(8,128)(2,1)S(1)}, u32[]{:S(2)}, u32[]{:S(2)}) collective-permute-start(bf16[320,256]{1,0:T(8,128)(2,1)S(1)} %dynamic-slice_add_fusion.21), channel_id=1, source_target_pairs={{0,7},{1,0},{2,1},{3,2},{4,3},{5,4},{6,5},{7,6},{8,15},{9,8},{10,9... | collective-permute-start | bytes 491528 | tf_op jit(solution)/shard_map/ppermute | solution.py:16
  67.2 3.7 %collective-permute-start.21 = (bf16[112,256]{1,0:T(8,128)(2,1)S(1)}, bf16[112,256]{1,0:T(8,128)(2,1)S(1)}, u32[]{:S(2)}, u32[]{:S(2)}) collective-permute-start(bf16[112,256]{1,0:T(8,128)(2,1)S(1)} %pad_maximum_fusion.19), channel_id=1, source_target_pairs={{0,7},{1,0},{2,1},{3,2},{4,3},{5,4},{6,5},{7,6},{8,15},{9,8},{10,9... | collective-permute-start | bytes 172040 | tf_op jit(solution)/shard_map/ppermute | solution.py:16
  70.9 5.5 %collective-permute-done.17 = bf16[112,256]{1,0:T(8,128)(2,1)S(1)} collective-permute-done((bf16[112,256]{1,0:T(8,128)(2,1)S(1)}, bf16[112,256]{1,0:T(8,128)(2,1)S(1)}, u32[]{:S(2)}, u32[]{:S(2)}) %collective-permute-start.17) | collective-permute-done | bytes 57376 | tf_op jit(solution)/shard_map/ppermute | solution.py:16
  77.0 4.9 %collective-permute-done.18 = bf16[112,256]{1,0:T(8,128)(2,1)S(1)} collective-permute-done((bf16[112,256]{1,0:T(8,128)(2,1)S(1)}, bf16[112,256]{1,0:T(8,128)(2,1)S(1)}, u32[]{:S(2)}, u32[]{:S(2)}) %collective-permute-start.18) | collective-permute-done | bytes 57376 | tf_op jit(solution)/shard_map/ppermute | solution.py:16
  86.4 4.2 %collective-permute-done.22 = bf16[112,256]{1,0:T(8,128)(2,1)S(1)} collective-permute-done((bf16[112,256]{1,0:T(8,128)(2,1)S(1)}, bf16[112,256]{1,0:T(8,128)(2,1)S(1)}, u32[]{:S(2)}, u32[]{:S(2)}) %collective-permute-start.22) | collective-permute-done | bytes 57376 | tf_op jit(solution)/shard_map/ppermute | solution.py:16
  90.5 8.6 %collective-permute-start.19 = (bf16[112,256]{1,0:T(8,128)(2,1)S(1)}, bf16[112,256]{1,0:T(8,128)(2,1)S(1)}, u32[]{:S(2)}, u32[]{:S(2)}) collective-permute-start(bf16[112,256]{1,0:T(8,128)(2,1)S(1)} %get-tuple-element.60), channel_id=1, source_target_pairs={{0,1},{1,2},{2,3},{3,4},{4,5},{5,6},{6,7},{7,0},{8,9},{9,10},{10,1... | collective-permute-start | bytes 172040 | tf_op jit(solution)/shard_map/ppermute | solution.py:16
  99.2 5.0 %fusion.11 = bf16[768,2048]{1,0:T(8,128)(2,1)S(1)} fusion(bf16[768,896]{1,0:T(8,128)(2,1)} %collective-permute-done.24, bf16[1,896,2048]{2,1,0:T(8,128)(2,1)S(1)} %copy-done.5), kind=kOutput, calls=%fused_computation.9 | convolution fusion | flops 2820145152 | bytes 8192000 | tf_op jit(solution)/shard_map/dot_general | solution.py:52
  111.0 3.5 %collective-permute-start.40 = (bf16[112,1024]{1,0:T(8,128)(2,1)S(1)}, bf16[112,1024]{1,0:T(8,128)(2,1)S(1)}, u32[]{:S(2)}, u32[]{:S(2)}) collective-permute-start(bf16[112,1024]{1,0:T(8,128)(2,1)S(1)} %get-tuple-element.15), channel_id=1, source_target_pairs={{0,24},{8,0},{16,8},{24,16},{1,25},{9,1},{17,9},{25,17},{2,26},{10... | collective-permute-start | bytes 688136 | tf_op jit(solution)/shard_map/ppermute | solution.py:16
  120.4 6.0 %collective-permute-done.27 = bf16[320,256]{1,0:T(8,128)(2,1)S(1)} collective-permute-done((bf16[320,256]{1,0:T(8,128)(2,1)S(1)}, bf16[320,256]{1,0:T(8,128)(2,1)S(1)}, u32[]{:S(2)}, u32[]{:S(2)}) %collective-permute-start.27) | collective-permute-done | bytes 163872 | tf_op jit(solution)/shard_map/ppermute | solution.py:16
  141.3 4.3 %collective-permute-done.32 = bf16[320,256]{1,0:T(8,128)(2,1)S(1)} collective-permute-done((bf16[320,256]{1,0:T(8,128)(2,1)S(1)}, bf16[320,256]{1,0:T(8,128)(2,1)S(1)}, u32[]{:S(2)}, u32[]{:S(2)}) %collective-permute-start.32) | collective-permute-done | bytes 163872 | tf_op jit(solution)/shard_map/ppermute | solution.py:16
  160.1 3.7 %collective-permute-start.47 = (bf16[112,256]{1,0:T(8,128)(2,1)S(1)}, bf16[112,256]{1,0:T(8,128)(2,1)S(1)}, u32[]{:S(2)}, u32[]{:S(2)}) collective-permute-start(bf16[112,256]{1,0:T(8,128)(2,1)S(1)} %pad_maximum_fusion.21), channel_id=1, source_target_pairs={{0,7},{1,0},{2,1},{3,2},{4,3},{5,4},{6,5},{7,6},{8,15},{9,8},{10,9... | collective-permute-start | bytes 172040 | tf_op jit(solution)/shard_map/ppermute | solution.py:16
  163.8 5.7 %collective-permute-done.43 = bf16[112,256]{1,0:T(8,128)(2,1)S(1)} collective-permute-done((bf16[112,256]{1,0:T(8,128)(2,1)S(1)}, bf16[112,256]{1,0:T(8,128)(2,1)S(1)}, u32[]{:S(2)}, u32[]{:S(2)}) %collective-permute-start.43) | collective-permute-done | bytes 57376 | tf_op jit(solution)/shard_map/ppermute | solution.py:16
  169.8 5.3 %collective-permute-done.44 = bf16[112,256]{1,0:T(8,128)(2,1)S(1)} collective-permute-done((bf16[112,256]{1,0:T(8,128)(2,1)S(1)}, bf16[112,256]{1,0:T(8,128)(2,1)S(1)}, u32[]{:S(2)}, u32[]{:S(2)}) %collective-permute-start.44) | collective-permute-done | bytes 57376 | tf_op jit(solution)/shard_map/ppermute | solution.py:16
  175.2 4.1 %collective-permute-done.48 = bf16[112,256]{1,0:T(8,128)(2,1)S(1)} collective-permute-done((bf16[112,256]{1,0:T(8,128)(2,1)S(1)}, bf16[112,256]{1,0:T(8,128)(2,1)S(1)}, u32[]{:S(2)}, u32[]{:S(2)}) %collective-permute-start.48) | collective-permute-done | bytes 57376 | tf_op jit(solution)/shard_map/ppermute | solution.py:16
  187.5 3.6 %fusion.14 = bf16[768,2048]{1,0:T(8,128)(2,1)S(1)} fusion(bf16[1,896,2048]{2,1,0:T(8,128)(2,1)S(1)} %copy-done.5, bf16[768,896]{1,0:T(8,128)(2,1)S(1)} %collective-permute-done.50, bf16[768,896]{1,0:T(8,128)(2,1)S(1)} %collective-permute-done.51, pred[]{:T(512)S(6)} %eq.132), kind=kOutput, calls=%fused_computation.10 | convolution fusion | flops 2820833280 | bytes 9568257 | tf_op jit(solution)/shard_map/dot_general | solution.py:52
  191.2 3.6 %fusion.17 = bf16[768,2048]{1,0:T(8,128)(2,1)S(1)} fusion(bf16[1,896,2048]{2,1,0:T(8,128)(2,1)S(1)} %copy-done.5, bf16[768,896]{1,0:T(8,128)(2,1)S(1)} %collective-permute-done.78, bf16[768,896]{1,0:T(8,128)(2,1)S(1)} %collective-permute-done.79, pred[]{:T(512)S(6)} %eq.133), kind=kOutput, calls=%fused_computation.11 | convolution fusion | flops 2820833280 | bytes 9568257 | tf_op jit(solution)/shard_map/dot_general | solution.py:52
  215.5 3.8 %collective-permute-done.55 = bf16[320,256]{1,0:T(8,128)(2,1)S(1)} collective-permute-done((bf16[320,256]{1,0:T(8,128)(2,1)S(1)}, bf16[320,256]{1,0:T(8,128)(2,1)S(1)}, u32[]{:S(2)}, u32[]{:S(2)}) %collective-permute-start.55) | collective-permute-done | bytes 163872 | tf_op jit(solution)/shard_map/ppermute | solution.py:16
  221.8 6.4 %collective-permute-done.56 = bf16[320,256]{1,0:T(8,128)(2,1)S(1)} collective-permute-done((bf16[320,256]{1,0:T(8,128)(2,1)S(1)}, bf16[320,256]{1,0:T(8,128)(2,1)S(1)}, u32[]{:S(2)}, u32[]{:S(2)}) %collective-permute-start.56) | collective-permute-done | bytes 163872 | tf_op jit(solution)/shard_map/ppermute | solution.py:16
  229.3 5.4 %collective-permute-done.82 = bf16[320,256]{1,0:T(8,128)(2,1)S(1)} collective-permute-done((bf16[320,256]{1,0:T(8,128)(2,1)S(1)}, bf16[320,256]{1,0:T(8,128)(2,1)S(1)}, u32[]{:S(2)}, u32[]{:S(2)}) %collective-permute-start.82) | collective-permute-done | bytes 163872 | tf_op jit(solution)/shard_map/ppermute | solution.py:16
  234.8 6.2 %collective-permute-done.60 = bf16[320,256]{1,0:T(8,128)(2,1)S(1)} collective-permute-done((bf16[320,256]{1,0:T(8,128)(2,1)S(1)}, bf16[320,256]{1,0:T(8,128)(2,1)S(1)}, u32[]{:S(2)}, u32[]{:S(2)}) %collective-permute-start.60) | collective-permute-done | bytes 163872 | tf_op jit(solution)/shard_map/ppermute | solution.py:16
  242.3 4.9 %collective-permute-done.86 = bf16[320,256]{1,0:T(8,128)(2,1)S(1)} collective-permute-done((bf16[320,256]{1,0:T(8,128)(2,1)S(1)}, bf16[320,256]{1,0:T(8,128)(2,1)S(1)}, u32[]{:S(2)}, u32[]{:S(2)}) %collective-permute-start.86) | collective-permute-done | bytes 163872 | tf_op jit(solution)/shard_map/ppermute | solution.py:16
  283.0 3.3 collective-permute-start.91
  288.4 3.3 collective-permute-done.72
  303.4 3.3 collective-permute-start.109
  311.3 4.8 %collective-permute-start.112 = (f32[4,192]{1,0:T(4,128)S(1)}, f32[4,192]{1,0:T(4,128)S(1)}, u32[]{:S(2)}, u32[]{:S(2)}) collective-permute-start(f32[4,192]{1,0:T(4,128)S(1)} %add_add_fusion.1), channel_id=1, source_target_pairs={{0,2},{1,3},{2,4},{3,5},{4,6},{5,7},{6,0},{7,1},{8,10},{9,11},{10,... | collective-permute-start | bytes 9224 | tf_op jit(solution)/shard_map/ppermute | solution.py:16
  319.3 4.0 %collective-permute-start.115 = (f32[4,192]{1,0:T(4,128)S(1)}, f32[4,192]{1,0:T(4,128)S(1)}, u32[]{:S(2)}, u32[]{:S(2)}) collective-permute-start(f32[4,192]{1,0:T(4,128)S(1)} %add_add_fusion.1), channel_id=1, source_target_pairs={{0,5},{1,6},{2,7},{3,0},{4,1},{5,2},{6,3},{7,4},{8,13},{9,14},{10,... | collective-permute-start | bytes 9224 | tf_op jit(solution)/shard_map/ppermute | solution.py:16
  332.7 3.3 collective-permute-start.121
  338.5 4.5 %collective-permute-start.107 = (bf16[192,256]{1,0:T(8,128)(2,1)S(1)}, bf16[192,256]{1,0:T(8,128)(2,1)S(1)}, u32[]{:S(2)}, u32[]{:S(2)}) collective-permute-start(bf16[192,256]{1,0:T(8,128)(2,1)S(1)} %get-tuple-element.93), channel_id=1, source_target_pairs={{0,224},{1,225},{2,226},{3,227},{4,228},{5,229},{6,230},{7,231},{8... | collective-permute-start | bytes 294920 | tf_op jit(solution)/shard_map/ppermute | solution.py:104
  (378 shorter events, 199.9 us)
Async XLA Ops:
  12.0 11.5 %collective-permute-start = (bf16[160,256]{1,0:T(8,128)(2,1)}, bf16[160,256]{1,0:T(8,128)(2,1)}, u32[]{:S(2)}, u32[]{:S(2)}) collective-permute-start(bf16[160,256]{1,0:T(8,128)(2,1)} %get-tuple-element.34), channel_id=1, source_target_pairs={{0,1},{1,2},{2,3},{3,4},{4,5},{5,6},{6,7},{7,0},{8,9},{9,10},{10,1... | collective-permute-start | bytes 245768 | tf_op jit(solution)/shard_map/ppermute | solution.py:16
  24.5 10.5 %collective-permute-start.1 = (bf16[320,256]{1,0:T(8,128)(2,1)S(1)}, bf16[320,256]{1,0:T(8,128)(2,1)S(1)}, u32[]{:S(2)}, u32[]{:S(2)}) collective-permute-start(bf16[320,256]{1,0:T(8,128)(2,1)S(1)} %pad_maximum_fusion.10), channel_id=1, source_target_pairs={{0,1},{1,2},{2,3},{3,4},{4,5},{5,6},{6,7},{7,0},{8,9},{9,10},{10,1... | collective-permute-start | bytes 491528 | tf_op jit(solution)/shard_map/ppermute | solution.py:16
  25.3 13.4 %collective-permute-start.5 = (bf16[320,256]{1,0:T(8,128)(2,1)}, bf16[320,256]{1,0:T(8,128)(2,1)}, u32[]{:S(2)}, u32[]{:S(2)}) collective-permute-start(bf16[320,256]{1,0:T(8,128)(2,1)} %pad_maximum_fusion.11), channel_id=1, source_target_pairs={{0,7},{1,0},{2,1},{3,2},{4,3},{5,4},{6,5},{7,6},{8,15},{9,8},{10,9... | collective-permute-start | bytes 491528 | tf_op jit(solution)/shard_map/ppermute | solution.py:16
  31.0 13.6 %collective-permute-start.13 = (bf16[112,2048]{1,0:T(8,128)(2,1)}, bf16[112,2048]{1,0:T(8,128)(2,1)}, u32[]{:S(2)}, u32[]{:S(2)}) collective-permute-start(bf16[112,2048]{1,0:T(8,128)(2,1)} %pad_maximum_fusion), channel_id=1, source_target_pairs={{0,8},{8,16},{16,24},{24,0},{1,9},{9,17},{17,25},{25,1},{2,10},{10... | collective-permute-start | bytes 1376264 | tf_op jit(solution)/shard_map/ppermute | solution.py:16
  33.4 14.5 %collective-permute-start.15 = (bf16[112,2048]{1,0:T(8,128)(2,1)}, bf16[112,2048]{1,0:T(8,128)(2,1)}, u32[]{:S(2)}, u32[]{:S(2)}) collective-permute-start(bf16[112,2048]{1,0:T(8,128)(2,1)} %pad_maximum_fusion.1), channel_id=1, source_target_pairs={{0,24},{8,0},{16,8},{24,16},{1,25},{9,1},{17,9},{25,17},{2,26},{10... | collective-permute-start | bytes 1376264 | tf_op jit(solution)/shard_map/ppermute | solution.py:16
  35.8 63.4 %collective-permute-start.24 = (bf16[768,896]{1,0:T(8,128)(2,1)}, bf16[768,896]{1,0:T(8,128)(2,1)}, u32[]{:S(2)}, u32[]{:S(2)}) collective-permute-start(bf16[768,896]{1,0:T(8,128)(2,1)} %bitcast), channel_id=1, source_target_pairs={{0,32},{32,0},{1,33},{33,1},{2,34},{34,2},{3,35},{35,3},{4,36},{36... | collective-permute-start | bytes 4128776 | tf_op jit(solution)/shard_map/ppermute | solution.py:21
  38.7 92.0 %collective-permute-start.50 = (bf16[768,896]{1,0:T(8,128)(2,1)}, bf16[768,896]{1,0:T(8,128)(2,1)S(1)}, u32[]{:S(2)}, u32[]{:S(2)}) collective-permute-start(bf16[768,896]{1,0:T(8,128)(2,1)} %bitcast), channel_id=1, source_target_pairs={{0,64},{64,0},{1,65},{65,1},{2,66},{66,2},{3,67},{67,3},{4,68},{68... | collective-permute-start | bytes 4128776 | tf_op jit(solution)/shard_map/ppermute | solution.py:78
  42.7 89.1 %collective-permute-start.78 = (bf16[768,896]{1,0:T(8,128)(2,1)}, bf16[768,896]{1,0:T(8,128)(2,1)S(1)}, u32[]{:S(2)}, u32[]{:S(2)}) collective-permute-start(bf16[768,896]{1,0:T(8,128)(2,1)} %bitcast), channel_id=1, source_target_pairs={{32,96},{96,32},{33,97},{97,33},{34,98},{98,34},{35,99},{99,35},{3... | collective-permute-start | bytes 4128776 | tf_op jit(solution)/shard_map/ppermute | solution.py:78
  84.7 19.5 %collective-permute-start.25 = (bf16[24,2048]{1,0:T(8,128)(2,1)S(1)}, bf16[24,2048]{1,0:T(8,128)(2,1)S(1)}, u32[]{:S(2)}, u32[]{:S(2)}) collective-permute-start(bf16[24,2048]{1,0:T(8,128)(2,1)S(1)} %bitcast.112), channel_id=1, source_target_pairs={{0,32},{32,0},{1,33},{33,1},{2,34},{34,2},{3,35},{35,3},{4,36},{36... | collective-permute-start | bytes 294920 | tf_op jit(solution)/shard_map/ppermute | solution.py:21
  90.5 35.9 %collective-permute-start.19 = (bf16[112,256]{1,0:T(8,128)(2,1)S(1)}, bf16[112,256]{1,0:T(8,128)(2,1)S(1)}, u32[]{:S(2)}, u32[]{:S(2)}) collective-permute-start(bf16[112,256]{1,0:T(8,128)(2,1)S(1)} %get-tuple-element.60), channel_id=1, source_target_pairs={{0,1},{1,2},{2,3},{3,4},{4,5},{5,6},{6,7},{7,0},{8,9},{9,10},{10,1... | collective-permute-start | bytes 172040 | tf_op jit(solution)/shard_map/ppermute | solution.py:16
  126.5 12.2 %collective-permute-start.39 = (bf16[112,2048]{1,0:T(8,128)(2,1)S(1)}, bf16[112,2048]{1,0:T(8,128)(2,1)S(1)}, u32[]{:S(2)}, u32[]{:S(2)}) collective-permute-start(bf16[112,2048]{1,0:T(8,128)(2,1)S(1)} %pad_maximum_fusion.2), channel_id=1, source_target_pairs={{0,8},{8,16},{16,24},{24,0},{1,9},{9,17},{17,25},{25,1},{2,10},{10... | collective-permute-start | bytes 1376264 | tf_op jit(solution)/shard_map/ppermute | solution.py:16
  127.9 11.1 %collective-permute-start.41 = (bf16[112,2048]{1,0:T(8,128)(2,1)S(1)}, bf16[112,2048]{1,0:T(8,128)(2,1)S(1)}, u32[]{:S(2)}, u32[]{:S(2)}) collective-permute-start(bf16[112,2048]{1,0:T(8,128)(2,1)S(1)} %pad_maximum_fusion.3), channel_id=1, source_target_pairs={{0,24},{8,0},{16,8},{24,16},{1,25},{9,1},{17,9},{25,17},{2,26},{10... | collective-permute-start | bytes 1376264 | tf_op jit(solution)/shard_map/ppermute | solution.py:16
  131.9 62.9 %collective-permute-start.52 = (bf16[24,2048]{1,0:T(8,128)(2,1)S(1)}, bf16[24,2048]{1,0:T(8,128)(2,1)S(1)}, u32[]{:S(2)}, u32[]{:S(2)}) collective-permute-start(bf16[24,2048]{1,0:T(8,128)(2,1)S(1)} %bitcast.111), channel_id=1, source_target_pairs={{0,64},{64,0},{1,65},{65,1},{2,66},{66,2},{3,67},{67,3},{4,68},{68... | collective-permute-start | bytes 294920 | tf_op jit(solution)/shard_map/ppermute | solution.py:21
  134.0 53.6 %collective-permute-start.51 = (bf16[768,896]{1,0:T(8,128)(2,1)S(1)}, bf16[768,896]{1,0:T(8,128)(2,1)S(1)}, u32[]{:S(2)}, u32[]{:S(2)}) collective-permute-start(bf16[768,896]{1,0:T(8,128)(2,1)S(1)} %collective-permute-done.50), channel_id=1, source_target_pairs={{0,32},{1,33},{2,34},{3,35},{4,36},{5,37},{6,38},{7,39},{8,40},{9,... | collective-permute-start | bytes 4128776 | tf_op jit(solution)/shard_map/ppermute | solution.py:81
  137.2 53.9 %collective-permute-start.79 = (bf16[768,896]{1,0:T(8,128)(2,1)S(1)}, bf16[768,896]{1,0:T(8,128)(2,1)S(1)}, u32[]{:S(2)}, u32[]{:S(2)}) collective-permute-start(bf16[768,896]{1,0:T(8,128)(2,1)S(1)} %collective-permute-done.78), channel_id=1, source_target_pairs={{32,0},{33,1},{34,2},{35,3},{36,4},{37,5},{38,6},{39,7},{40,8},{41... | collective-permute-start | bytes 4128776 | tf_op jit(solution)/shard_map/ppermute | solution.py:81
  169.7 10.6 %collective-permute-start.35 = (bf16[80,256]{1,0:T(8,128)(2,1)S(1)}, bf16[80,256]{1,0:T(8,128)(2,1)S(1)}, u32[]{:S(2)}, u32[]{:S(2)}) collective-permute-start(bf16[80,256]{1,0:T(8,128)(2,1)S(1)} %pad_maximum_fusion.28), channel_id=1, source_target_pairs={{0,8},{8,16},{16,24},{24,0},{1,9},{9,17},{17,25},{25,1},{2,10},{10... | collective-permute-start | bytes 122888 | tf_op jit(solution)/shard_map/ppermute | solution.py:16
  198.7 12.5 %collective-permute-start.66 = (bf16[112,1024]{1,0:T(8,128)(2,1)S(1)}, bf16[112,1024]{1,0:T(8,128)(2,1)S(1)}, u32[]{:S(2)}, u32[]{:S(2)}) collective-permute-start(bf16[112,1024]{1,0:T(8,128)(2,1)S(1)} %get-tuple-element.20), channel_id=1, source_target_pairs={{0,8},{8,16},{16,24},{24,0},{1,9},{9,17},{17,25},{25,1},{2,10},{10... | collective-permute-start | bytes 688136 | tf_op jit(solution)/shard_map/ppermute | solution.py:16
  198.8 12.6 %collective-permute-start.68 = (bf16[112,1024]{1,0:T(8,128)(2,1)S(1)}, bf16[112,1024]{1,0:T(8,128)(2,1)S(1)}, u32[]{:S(2)}, u32[]{:S(2)}) collective-permute-start(bf16[112,1024]{1,0:T(8,128)(2,1)S(1)} %get-tuple-element.21), channel_id=1, source_target_pairs={{0,24},{8,0},{16,8},{24,16},{1,25},{9,1},{17,9},{25,17},{2,26},{10... | collective-permute-start | bytes 688136 | tf_op jit(solution)/shard_map/ppermute | solution.py:16
  208.9 12.8 %collective-permute-start.59 = (bf16[320,256]{1,0:T(8,128)(2,1)S(1)}, bf16[320,256]{1,0:T(8,128)(2,1)S(1)}, u32[]{:S(2)}, u32[]{:S(2)}) collective-permute-start(bf16[320,256]{1,0:T(8,128)(2,1)S(1)} %pad_maximum_fusion.15), channel_id=1, source_target_pairs={{0,7},{1,0},{2,1},{3,2},{4,3},{5,4},{6,5},{7,6},{8,15},{9,8},{10,9... | collective-permute-start | bytes 491528 | tf_op jit(solution)/shard_map/ppermute | solution.py:16
  211.4 16.9 %collective-permute-start.85 = (bf16[320,256]{1,0:T(8,128)(2,1)S(1)}, bf16[320,256]{1,0:T(8,128)(2,1)S(1)}, u32[]{:S(2)}, u32[]{:S(2)}) collective-permute-start(bf16[320,256]{1,0:T(8,128)(2,1)S(1)} %pad_maximum_fusion.17), channel_id=1, source_target_pairs={{0,7},{1,0},{2,1},{3,2},{4,3},{5,4},{6,5},{7,6},{8,15},{9,8},{10,9... | collective-permute-start | bytes 491528 | tf_op jit(solution)/shard_map/ppermute | solution.py:16
  215.1 32.2 %collective-permute-start.67 = (bf16[112,2048]{1,0:T(8,128)(2,1)S(1)}, bf16[112,2048]{1,0:T(8,128)(2,1)S(1)}, u32[]{:S(2)}, u32[]{:S(2)}) collective-permute-start(bf16[112,2048]{1,0:T(8,128)(2,1)S(1)} %pad_maximum_fusion.4), channel_id=1, source_target_pairs={{0,8},{8,16},{16,24},{24,0},{1,9},{9,17},{17,25},{25,1},{2,10},{10... | collective-permute-start | bytes 1376264 | tf_op jit(solution)/shard_map/ppermute | solution.py:16
  219.3 28.7 %collective-permute-start.69 = (bf16[112,2048]{1,0:T(8,128)(2,1)S(1)}, bf16[112,2048]{1,0:T(8,128)(2,1)S(1)}, u32[]{:S(2)}, u32[]{:S(2)}) collective-permute-start(bf16[112,2048]{1,0:T(8,128)(2,1)S(1)} %pad_maximum_fusion.5), channel_id=1, source_target_pairs={{0,24},{8,0},{16,8},{24,16},{1,25},{9,1},{17,9},{25,17},{2,26},{10... | collective-permute-start | bytes 1376264 | tf_op jit(solution)/shard_map/ppermute | solution.py:16
  221.7 29.2 %collective-permute-start.93 = (bf16[112,2048]{1,0:T(8,128)(2,1)S(1)}, bf16[112,2048]{1,0:T(8,128)(2,1)S(1)}, u32[]{:S(2)}, u32[]{:S(2)}) collective-permute-start(bf16[112,2048]{1,0:T(8,128)(2,1)S(1)} %pad_maximum_fusion.6), channel_id=1, source_target_pairs={{0,8},{8,16},{16,24},{24,0},{1,9},{9,17},{17,25},{25,1},{2,10},{10... | collective-permute-start | bytes 1376264 | tf_op jit(solution)/shard_map/ppermute | solution.py:16
  228.3 24.8 %collective-permute-start.95 = (bf16[112,2048]{1,0:T(8,128)(2,1)S(1)}, bf16[112,2048]{1,0:T(8,128)(2,1)S(1)}, u32[]{:S(2)}, u32[]{:S(2)}) collective-permute-start(bf16[112,2048]{1,0:T(8,128)(2,1)S(1)} %pad_maximum_fusion.7), channel_id=1, source_target_pairs={{0,24},{8,0},{16,8},{24,16},{1,25},{9,1},{17,9},{25,17},{2,26},{10... | collective-permute-start | bytes 1376264 | tf_op jit(solution)/shard_map/ppermute | solution.py:16
  247.2 16.9 %collective-permute-start.57 = (bf16[320,256]{1,0:T(8,128)(2,1)S(1)}, bf16[320,256]{1,0:T(8,128)(2,1)S(1)}, u32[]{:S(2)}, u32[]{:S(2)}) collective-permute-start(bf16[320,256]{1,0:T(8,128)(2,1)S(1)} %get-tuple-element.44), channel_id=1, source_target_pairs={{0,1},{1,2},{2,3},{3,4},{4,5},{5,6},{6,7},{7,0},{8,9},{9,10},{10,1... | collective-permute-start | bytes 491528 | tf_op jit(solution)/shard_map/ppermute | solution.py:16
  247.3 20.2 %collective-permute-start.83 = (bf16[320,256]{1,0:T(8,128)(2,1)S(1)}, bf16[320,256]{1,0:T(8,128)(2,1)S(1)}, u32[]{:S(2)}, u32[]{:S(2)}) collective-permute-start(bf16[320,256]{1,0:T(8,128)(2,1)S(1)} %get-tuple-element.52), channel_id=1, source_target_pairs={{0,1},{1,2},{2,3},{3,4},{4,5},{5,6},{6,7},{7,0},{8,9},{9,10},{10,1... | collective-permute-start | bytes 491528 | tf_op jit(solution)/shard_map/ppermute | solution.py:16
  248.1 17.5 %collective-permute-start.61 = (bf16[320,256]{1,0:T(8,128)(2,1)S(1)}, bf16[320,256]{1,0:T(8,128)(2,1)S(1)}, u32[]{:S(2)}, u32[]{:S(2)}) collective-permute-start(bf16[320,256]{1,0:T(8,128)(2,1)S(1)} %dynamic-slice_add_fusion.13), channel_id=1, source_target_pairs={{0,7},{1,0},{2,1},{3,2},{4,3},{5,4},{6,5},{7,6},{8,15},{9,8},{10,9... | collective-permute-start | bytes 491528 | tf_op jit(solution)/shard_map/ppermute | solution.py:16
  263.4 25.0 %collective-permute-start.75 = (bf16[112,256]{1,0:T(8,128)(2,1)S(1)}, bf16[112,256]{1,0:T(8,128)(2,1)S(1)}, u32[]{:S(2)}, u32[]{:S(2)}) collective-permute-start(bf16[112,256]{1,0:T(8,128)(2,1)S(1)} %pad_maximum_fusion.23), channel_id=1, source_target_pairs={{0,7},{1,0},{2,1},{3,2},{4,3},{5,4},{6,5},{7,6},{8,15},{9,8},{10,9... | collective-permute-start | bytes 172040 | tf_op jit(solution)/shard_map/ppermute | solution.py:16
  264.1 13.7 %collective-permute-start.71 = (bf16[112,256]{1,0:T(8,128)(2,1)S(1)}, bf16[112,256]{1,0:T(8,128)(2,1)S(1)}, u32[]{:S(2)}, u32[]{:S(2)}) collective-permute-start(bf16[112,256]{1,0:T(8,128)(2,1)S(1)} %pad_maximum_fusion.22), channel_id=1, source_target_pairs={{0,1},{1,2},{2,3},{3,4},{4,5},{5,6},{6,7},{7,0},{8,9},{9,10},{10,1... | collective-permute-start | bytes 172040 | tf_op jit(solution)/shard_map/ppermute | solution.py:16
  265.6 28.3 %collective-permute-start.101 = (bf16[112,256]{1,0:T(8,128)(2,1)S(1)}, bf16[112,256]{1,0:T(8,128)(2,1)S(1)}, u32[]{:S(2)}, u32[]{:S(2)}) collective-permute-start(bf16[112,256]{1,0:T(8,128)(2,1)S(1)} %pad_maximum_fusion.25), channel_id=1, source_target_pairs={{0,7},{1,0},{2,1},{3,2},{4,3},{5,4},{6,5},{7,6},{8,15},{9,8},{10,9... | collective-permute-start | bytes 172040 | tf_op jit(solution)/shard_map/ppermute | solution.py:16
  311.3 12.1 %collective-permute-start.111 = (f32[4,192]{1,0:T(4,128)S(1)}, f32[4,192]{1,0:T(4,128)S(1)}, u32[]{:S(2)}, u32[]{:S(2)}) collective-permute-start(f32[4,192]{1,0:T(4,128)S(1)} %add_add_fusion.1), channel_id=1, source_target_pairs={{0,1},{1,2},{2,3},{3,4},{4,5},{5,6},{6,7},{7,0},{8,9},{9,10},{10,1... | collective-permute-start | bytes 9224 | tf_op jit(solution)/shard_map/ppermute | solution.py:16
  311.3 13.4 %collective-permute-start.112 = (f32[4,192]{1,0:T(4,128)S(1)}, f32[4,192]{1,0:T(4,128)S(1)}, u32[]{:S(2)}, u32[]{:S(2)}) collective-permute-start(f32[4,192]{1,0:T(4,128)S(1)} %add_add_fusion.1), channel_id=1, source_target_pairs={{0,2},{1,3},{2,4},{3,5},{4,6},{5,7},{6,0},{7,1},{8,10},{9,11},{10,... | collective-permute-start | bytes 9224 | tf_op jit(solution)/shard_map/ppermute | solution.py:16
  (96 other events, 729.3 us)

commit v2 on v0

v2 whole, which is shorter than its diff:
```python
import functools

import jax
import jax.numpy as jnp
from jax import lax
from jax.experimental import pallas as pl
from jax.experimental.pallas import tpu as pltpu
from jax.sharding import Mesh
from jax.sharding import PartitionSpec as P

D = 8192
NZ, NY = 8, 4
COLS = 256
HALF = 384
ORDER = ((0, 192), (192, HALF))
SCALE, FAR = 1, 100
VMEM = 58 * 2**20
AXES = ("s", "xh", "c", "y", "z")
F32, BF16 = jnp.float32, jnp.bfloat16


def shifted(x, axis, n, by):
    return lax.ppermute(x, axis, [(i, (i + by) % n) for i in range(n)])


def flipped(x, *axes):
    n = 2 ** len(axes)
    return lax.ppermute(x, axes, [(i, n - 1 - i) for i in range(n)])


def product_kernel(first, rows, y_major, m_ref, h0_ref, h1_ref, w_ref, r0_ref, r1_ref, *refs):
    out_ref = refs[-1]

    def block(i, half):
        return (i * 2 + half, 0) if y_major else (0, i * 2 + half)

    for i, h_ref in enumerate((h0_ref, h1_ref)):
        for half in range(2):
            at = half * rows
            acc = jnp.dot(h_ref[at : at + rows], w_ref[...], preferred_element_type=F32)
            out_ref[block(i, half)] = acc.astype(BF16)

    m = m_ref[0]
    row = m % 16 * 24

    @pl.when((row >= first) & (row < first + rows))
    def _():
        window = pl.ds(pl.multiple_of(row // 16 * 16 - first, 16), 32)
        for i, r_ref in enumerate((r0_ref, r1_ref)):
            at = block(i, m // 16) + (window, slice(None))
            out_ref[at] = (out_ref[at].astype(F32) + r_ref[...].astype(F32)).astype(BF16)


def product(m, h, w, res, first, rows, y_major, scale=1, after=()):
    whole = lambda j: (0, 0)
    columns = lambda j: (0, j)
    if y_major:
        shape, block, place = (NY, NZ, rows, COLS), (NY, 1, rows, COLS), lambda j: (0, j, 0, 0)
    else:
        shape, block, place = (NZ, NY, rows, COLS), (1, NY, rows, COLS), lambda j: (j, 0, 0, 0)
    return pl.pallas_call(
        functools.partial(product_kernel, first, rows, y_major),
        out_shape=jax.ShapeDtypeStruct(shape, BF16),
        grid=(NZ,),
        in_specs=[
            pl.BlockSpec(memory_space=pltpu.SMEM),
            pl.BlockSpec(h[0].shape, whole),
            pl.BlockSpec(h[1].shape, whole),
            pl.BlockSpec((w.shape[0], COLS), columns),
            pl.BlockSpec((32, COLS), columns),
            pl.BlockSpec((32, COLS), columns),
        ]
        + [pl.BlockSpec(memory_space=pl.ANY)] * len(after),
        out_specs=pl.BlockSpec(block, place),
        compiler_params=pltpu.CompilerParams(vmem_limit_bytes=VMEM),
        cost_estimate=pl.CostEstimate(
            flops=scale * 2 * NY * rows * w.size,
            bytes_accessed=2 * (NY * rows * NZ * COLS + w.size + 2 * h[0].size),
            transcendentals=0,
        ),
    )(m, h[0], h[1], w, res[0], res[1], *after)


def tied(x, *after):
    anywhere = pl.BlockSpec(memory_space=pl.ANY)
    return pl.pallas_call(
        lambda *refs: None,
        out_shape=jax.ShapeDtypeStruct(x.shape, x.dtype),
        in_specs=[anywhere] * (1 + len(after)),
        out_specs=anywhere,
        input_output_aliases={0: 0},
    )(x, *after)


def summed_along_y(x, y):
    half = x.shape[1] // 2
    take = lambda j: lax.dynamic_index_in_dim(x, (y + j) % NY, axis=0, keepdims=False)
    far, ahead, behind = take(2), take(1), take(-1)
    up, down = shifted(far[:half], "y", NY, 1), shifted(far[half:], "y", NY, -1)
    ahead = jnp.concatenate([ahead[:half] + up, ahead[half:]])
    behind = jnp.concatenate([behind[:half], behind[half:] + down])
    up, down = shifted(ahead, "y", NY, 1), shifted(behind, "y", NY, -1)
    return take(0).astype(F32) + up.astype(F32) + down.astype(F32)


def summed_along_z(x):
    return lax.psum_scatter(x, "z", scatter_dimension=0, tiled=False)


def handing(odd):
    pairs = []
    for i in range(2 * 4 * NY * NZ):
        s, g, y, z = i // 128, i // 32 % 4, i // 8 % 4, i % 8
        pairs.append((i, (1 - s) * 128 + (g ^ (y // 2) ^ (2 * ((y + odd) % 2))) * 32 + g * 8 + z))
    return pairs


def handed_over(pair, group, y):
    swapped = y % 2 == 1
    one = jnp.where(swapped, pair[1], pair[0])
    two = jnp.where(swapped, pair[0], pair[1])
    one = lax.ppermute(one, AXES, handing(0))
    two = lax.ppermute(two, AXES, handing(1))
    turned = (group ^ y) >= 2
    return jnp.concatenate([jnp.where(turned, two, one), jnp.where(turned, one, two)])


def shards(hidden, down_weight, residual, norm_gain):
    h, w, gain = hidden[0], down_weight[0], norm_gain[0]
    xh, c, y, z = (lax.axis_index(a) for a in AXES[1:])
    group = xh * 2 + c
    res = residual[0].reshape(24, 4, 2048)
    part = lambda x, r: lax.dynamic_index_in_dim(x, group ^ r, axis=1, keepdims=False)
    got = flipped(jnp.stack([part(res, 1), part(res, 3)]), "c")
    far = flipped(jnp.stack([part(res, 2), got[1]]), "xh")
    m = y * NZ + z
    pad = lambda x: jnp.where(m % 2 == 0, jnp.pad(x, ((0, 8), (0, 0))), jnp.pad(x, ((8, 0), (0, 0))))
    near_res = (pad(part(res, 0)), pad(got[0]))
    far_res = (pad(far[0]), pad(far[1]))
    m = m.reshape(1)
    core = flipped(h, "c")
    product_near = product(m, (h, core), w, near_res, 0, HALF, False, SCALE)
    near = summed_along_y(summed_along_z(product_near), y).astype(BF16)
    sums, last = [], product_near
    for a, b in ORDER:
        x = h.reshape(2, HALF, -1)[:, a:b].reshape(2 * (b - a), -1)
        x = flipped(tied(x, near_res[1]) if a else x, "xh")
        x = tied(x, last)
        x = last = product(m, (x, flipped(x, "c")), w, far_res, a, b - a, True, 1 if a else FAR)
        x = summed_along_y(x, y).astype(BF16)
        x = lax.all_to_all(x, "z", split_axis=0, concat_axis=0, tiled=True)
        sums.append(jnp.sum(x.astype(F32), axis=0).astype(BF16))
    handed = handed_over((near, jnp.concatenate(sums)), group, y)
    wide = handed.astype(F32)
    squares = jnp.sum(wide * wide, axis=1)
    squares = lax.all_to_all(
        jnp.broadcast_to(squares, (NY * NZ, 768)), ("y", "z"), split_axis=0, concat_axis=0, tiled=True
    )
    scale = lax.rsqrt(jnp.sum(squares, axis=0) / D + 1e-05)
    normed = (wide * scale[:, None] * gain[None, :]).astype(BF16)
    return (handed[None], normed[None])


def solution(mesh):
    fine = Mesh(mesh.devices.reshape(2, 2, 2, NY, NZ), AXES)
    group, mp = ("xh", "c"), ("y", "z")
    return jax.shard_map(
        shards,
        mesh=fine,
        in_specs=(P("s", group, mp), P("s", mp, group), P("s", group + mp, None), P("s", mp)),
        out_specs=(P("s", group, mp), P("s", group, mp)),
        check_vma=False,
    )
```

time: 480 us -> 198 us (0.41)
  waiting for transfers between devices: 351 us -> 70.3 us
  blocking collectives: 90.9 us -> 0 us
  starting transfers between devices: 0.64 us -> 51.1 us
  Pallas kernels: 0 us -> 29.9 us
  matrix products: 20.6 us -> 0 us
  other arithmetic: 2.22 us -> 17.4 us
  local copies, waits for them, and re-layouts: 0.79 us -> 12.6 us
    reduce_scatter x1, waiting for transfers between devices: 238 us -> 6.57 us  [summed_along_z(): return lax.psum_scatter(x, 'z', scatter_dimension=0, tiled=False)]
    all_gather x1 -> x0, waiting for transfers between devices: 105 us -> none  [shards(): lax.all_gather(local_weight, 'group', axis=1, tiled=True)]
    psum x1 -> x0, blocking collectives: 72.5 us -> none  [shards(): squares = lax.psum(jnp.sum(values * values, axis=1), 'mp')]
    ppermute x1 -> x21, waiting for transfers between devices: 7.22 us -> 43.7 us  [the longest x12 35.1 us: shifted(): return lax.ppermute(x, axis, [(i, (i + by) % n) for i in range(n)])]
    ppermute x1 -> x21, starting transfers between devices: 0.56 us -> 31.8 us  [the longest x12 22.2 us: shifted(): return lax.ppermute(x, axis, [(i, (i + by) % n) for i in range(n)])]
    pallas_call x0 -> x6, Pallas kernels: none -> 29.9 us  [the longest x3 29.9 us: product(): pl.pallas_call(functools.partial(product_kernel, first, rows, y_major), o...]
    dot_general x1 -> x0, matrix products: 20.6 us -> none  [shards(): jnp.dot(local_hidden, lax.all_gather(local_weight, 'group', axis=1, tiled...]
    all_to_all x0 -> x3, waiting for transfers between devices: none -> 20.1 us  [the longest x2 10.4 us: shards(): x = lax.all_to_all(x, 'z', split_axis=0, concat_axis=0, tiled=True)]
  transfers between devices with their start and end apart: 3 -> 25, of which waited for: 3 -> 14; matrix products, arithmetic and copies ran while one was open for 0% -> 11% of each run, Pallas kernels for 0% -> 15%
where the time goes in v2:
time: 198 us; the launch traced here: 196 us
  waiting for transfers between devices  70.3 us (36%)
  starting transfers between devices  51.1 us (26%)
  Pallas kernels  29.9 us (15%)
  other arithmetic  17.4 us (9%)
  between operations  14.4 us (7%)
  local copies, waits for them, and re-layouts  12.6 us (6%)
    ppermute x12, waiting for transfers between devices, shifted(): return lax.ppermute(x, axis, [(i, (i + by) % n) for i in range(n)])  35.1 us
    pallas_call x3, Pallas kernels, product(): pl.pallas_call(functools.partial(product_kernel, first, rows, y_major), o...  29.9 us
    ppermute x12, starting transfers between devices, shifted(): return lax.ppermute(x, axis, [(i, (i + by) % n) for i in range(n)])  22.2 us
    all_to_all x2, starting transfers between devices, shards(): x = lax.all_to_all(x, 'z', split_axis=0, concat_axis=0, tiled=True)  12.1 us
    all_to_all x2, waiting for transfers between devices, shards(): x = lax.all_to_all(x, 'z', split_axis=0, concat_axis=0, tiled=True)  10.4 us
    all_to_all x1, waiting for transfers between devices, shards(): lax.all_to_all(jnp.broadcast_to(squares, (NY * NZ, 768)), ('y', 'z'), spl...  9.65 us
    all_to_all x1, starting transfers between devices, shards(): lax.all_to_all(jnp.broadcast_to(squares, (NY * NZ, 768)), ('y', 'z'), spl...  7.27 us
    reduce_scatter x1, waiting for transfers between devices, summed_along_z(): return lax.psum_scatter(x, 'z', scatter_dimension=0, tiled=False)  6.57 us
  transfers between devices with their start and end apart: 25, of which 14 were waited for; matrix products, arithmetic and copies ran while one was open for 11% of the time, Pallas kernels for 15%

profile of v2, /device:TPU:2, one launch (start us, length us, event | category | flops | bytes accessed | tf_op | source)
XLA Modules:
  0.0 195.8 jit_solution(12337236625720401144)
XLA Ops:
  11.8 2.1 %collective-permute-start.6 = (bf16[384,896]{1,0:T(8,128)(2,1)S(1)}, bf16[384,896]{1,0:T(8,128)(2,1)S(1)}, u32[]{:S(2)}, u32[]{:S(2)}) collective-permute-start(bf16[384,896]{1,0:T(8,128)(2,1)S(1)} %bitcast.91), channel_id=1, source_target_pairs={{0,64},{64,0},{1,65},{65,1},{2,66},{66,2},{3,67},{67,3},{4,68},{68... | collective-permute-start | bytes 2064392 | tf_op jit(solution)/shard_map/ppermute | solution.py:28
  17.0 2.1 %collective-permute-start.13 = (bf16[384,896]{1,0:T(8,128)(2,1)}, bf16[384,896]{1,0:T(8,128)(2,1)}, u32[]{:S(2)}, u32[]{:S(2)}) collective-permute-start(bf16[384,896]{1,0:T(8,128)(2,1)} %shard_map.62), channel_id=1, source_target_pairs={{0,64},{64,0},{1,65},{65,1},{2,66},{66,2},{3,67},{67,3},{4,68},{68... | collective-permute-start | bytes 2064392 | tf_op jit(solution)/shard_map/ppermute | solution.py:28
  19.1 12.0 %shard_map.59.refs_1_ = bf16[8,4,384,256]{3,2,1,0:T(8,128)(2,1)} custom-call(s32[1]{0:T(128)} %bitcast.m_ref, bf16[768,896]{1,0:T(8,128)(2,1)} %bitcast.88, bf16[768,896]{1,0:T(8,128)(2,1)} %collective-permute-done.h1_ref, bf16[896,2048]{1,0:T(8,128)(2,1)} %bitcast.95, bf16[32,2048]{1,0:T(8,128)(2,1)} %pad_select_fusion.3.r0_ref, ...), custom_call_target="tpu_custom_call" | custom-call | flops 5637144576 | bytes 12713984 | tf_op jit(solution)/shard_map/pallas_call | solution.py:61
  32.5 3.4 %collective-permute-done.8 = bf16[2,24,2048]{2,1,0:T(8,128)(2,1)S(1)} collective-permute-done((bf16[2,24,2048]{2,1,0:T(8,128)(2,1)S(1)}, bf16[2,24,2048]{2,1,0:T(8,128)(2,1)S(1)}, u32[]{:S(2)}, u32[]{:S(2)}) %collective-permute-start.8) | collective-permute-done | bytes 196640 | tf_op jit(solution)/shard_map/ppermute | solution.py:28
  38.1 9.0 %shard_map.61.refs_1_ = bf16[4,8,192,256]{3,2,1,0:T(8,128)(2,1)} custom-call(s32[1]{0:T(128)} %bitcast.m_ref, bf16[384,896]{1,0:T(8,128)(2,1)} %shard_map.60.h0_ref, bf16[384,896]{1,0:T(8,128)(2,1)} %copy-done.7, bf16[896,2048]{1,0:T(8,128)(2,1)} %bitcast.96, bf16[32,2048]{1,0:T(8,128)(2,1)} %pad_select_fusion.1.r0_ref, bf16[32,2048]{1,0:T(8,128)(2,1)} %pad_select_fusion.r1_ref), custom_call_target="tpu_custom_call" | custom-call | flops 281857228800 | bytes 8192000 | tf_op jit(solution)/shard_map/pallas_call | solution.py:61
  47.1 2.4 %dynamic-slice_bitcast_fusion.10 = (bf16[4,192,256]{2,1,0:T(8,128)(2,1)}, bf16[4,192,256]{2,1,0:T(8,128)(2,1)}, bf16[4,192,256]{2,1,0:T(8,128)(2,1)}, bf16[4,192,256]{2,1,0:T(8,128)(2,1)S(1)}) fusion(bf16[4,8,192,256]{3,2,1,0:T(8,128)(2,1)} %shard_map.61.refs_1_, s32[]{:T(128)S(6)} %select_n.141, s32[]{:T(128)S(6)} %select_n.143, s32[]{:T(128)S(6)} %add.186, ...), kind=kLoop, calls=%fused_computation.25 | loop fusion | bytes 3145744 | tf_op jit(solution)/shard_map/slice | solution.py:99
  51.0 1.7 collective-permute-start.11
  52.7 7.5 %collective-permute-done.9 = bf16[4,192,256]{2,1,0:T(8,128)(2,1)} collective-permute-done((bf16[4,192,256]{2,1,0:T(8,128)(2,1)}, bf16[4,192,256]{2,1,0:T(8,128)(2,1)}, u32[]{:S(2)}, u32[]{:S(2)}) %collective-permute-start.9) | collective-permute-done | bytes 393248 | tf_op jit(solution)/shard_map/ppermute | solution.py:23
  62.4 3.0 %collective-permute-start.12 = (bf16[8,192,256]{2,1,0:T(8,128)(2,1)}, bf16[8,192,256]{2,1,0:T(8,128)(2,1)}, u32[]{:S(2)}, u32[]{:S(2)}) collective-permute-start(bf16[8,192,256]{2,1,0:T(8,128)(2,1)} %pad_maximum_fusion.1), channel_id=1, source_target_pairs={{0,24},{8,0},{16,8},{24,16},{1,25},{9,1},{17,9},{25,17},{2,26},{10... | collective-permute-start | bytes 2359304 | tf_op jit(solution)/shard_map/ppermute | solution.py:23
  67.2 8.9 %shard_map.64 = bf16[4,8,192,256]{3,2,1,0:T(8,128)(2,1)} custom-call(s32[1]{0:T(128)} %bitcast.m_ref, bf16[384,896]{1,0:T(8,128)(2,1)} %shard_map.63.h0_ref, bf16[384,896]{1,0:T(8,128)(2,1)} %copy-done.6, bf16[896,2048]{1,0:T(8,128)(2,1)} %bitcast.97, bf16[32,2048]{1,0:T(8,128)(2,1)} %pad_select_fusion.1.r0_ref, bf16[32,2048]{1,0:T(8,128)(2,1)} %pad_select_fusion.r1_ref), custom_call_target="tpu_custom_call" | custom-call | flops 2818572288 | bytes 8192000 | tf_op jit(solution)/shard_map/pallas_call | solution.py:61
  76.2 2.4 %dynamic-slice_bitcast_fusion.4 = (bf16[4,192,256]{2,1,0:T(8,128)(2,1)}, bf16[4,192,256]{2,1,0:T(8,128)(2,1)}, bf16[4,192,256]{2,1,0:T(8,128)(2,1)}, bf16[4,192,256]{2,1,0:T(8,128)(2,1)S(1)}) fusion(bf16[4,8,192,256]{3,2,1,0:T(8,128)(2,1)} %shard_map.64, s32[]{:T(128)S(6)} %select_n.141, s32[]{:T(128)S(6)} %select_n.143, s32[]{:T(128)S(6)} %add.186, ...), kind=kLoop, calls=%fused_computation.17 | loop fusion | bytes 3145744 | tf_op jit(solution)/shard_map/slice | solution.py:99
  79.5 2.5 %collective-permute-start.17 = (bf16[4,192,256]{2,1,0:T(8,128)(2,1)}, bf16[4,192,256]{2,1,0:T(8,128)(2,1)}, u32[]{:S(2)}, u32[]{:S(2)}) collective-permute-start(bf16[4,192,256]{2,1,0:T(8,128)(2,1)} %get-tuple-element.14), channel_id=1, source_target_pairs={{0,24},{8,0},{16,8},{24,16},{1,25},{9,1},{17,9},{25,17},{2,26},{10... | collective-permute-start | bytes 1179656 | tf_op jit(solution)/shard_map/ppermute | solution.py:23
  81.9 6.3 %collective-permute-done.10 = bf16[8,192,256]{2,1,0:T(8,128)(2,1)} collective-permute-done((bf16[8,192,256]{2,1,0:T(8,128)(2,1)}, bf16[8,192,256]{2,1,0:T(8,128)(2,1)}, u32[]{:S(2)}, u32[]{:S(2)}) %collective-permute-start.10) | collective-permute-done | bytes 786464 | tf_op jit(solution)/shard_map/ppermute | solution.py:23
  88.3 2.6 %fusion.3 = bf16[8,192,256]{2,1,0:T(8,128)(2,1)} fusion(bf16[8,192,256]{2,1,0:T(8,128)(2,1)} %collective-permute-done.12, bf16[8,192,256]{2,1,0:T(8,128)(2,1)} %collective-permute-done.10, bf16[4,8,192,256]{3,2,1,0:T(8,128)(2,1)S(1)} %copy-done, s32[]{:T(128)S(6)} %select_n.137), kind=kLoop, calls=%fused_computation.5 | loop fusion | flops 2359296 | bytes 3145732 | tf_op jit(solution)/shard_map/convert_element_type | solution.py:150
  90.8 8.5 %all-to-all-start = ((bf16[8,192,256]{2,1,0:T(8,128)(2,1)}), bf16[8,192,256]{2,1,0:T(8,128)(2,1)S(1)}, u32[]{:S(2)}, u32[]{:S(2)}) async-start(bf16[8,192,256]{2,1,0:T(8,128)(2,1)} %fusion.3), calls=%async_computation.1 | async-start | bytes 1572864 | tf_op jit(solution)/shard_map/all_to_all | solution.py:151
  101.1 2.1 %collective-permute-start.16 = (bf16[8,192,256]{2,1,0:T(8,128)(2,1)S(1)}, bf16[8,192,256]{2,1,0:T(8,128)(2,1)S(1)}, u32[]{:S(2)}, u32[]{:S(2)}) collective-permute-start(bf16[8,192,256]{2,1,0:T(8,128)(2,1)S(1)} %pad_maximum_fusion.2), channel_id=1, source_target_pairs={{0,8},{8,16},{16,24},{24,0},{1,9},{9,17},{17,25},{25,1},{2,10},{10... | collective-permute-start | bytes 2359304 | tf_op jit(solution)/shard_map/ppermute | solution.py:23
  103.2 9.8 %collective-permute-done.18 = bf16[8,192,256]{2,1,0:T(8,128)(2,1)S(1)} collective-permute-done((bf16[8,192,256]{2,1,0:T(8,128)(2,1)S(1)}, bf16[8,192,256]{2,1,0:T(8,128)(2,1)S(1)}, u32[]{:S(2)}, u32[]{:S(2)}) %collective-permute-start.18) | collective-permute-done | bytes 786464 | tf_op jit(solution)/shard_map/ppermute | solution.py:23
  114.4 2.3 %fusion.1 = bf16[8,192,256]{2,1,0:T(8,128)(2,1)} fusion(bf16[8,192,256]{2,1,0:T(8,128)(2,1)S(1)} %collective-permute-done.18, bf16[8,192,256]{2,1,0:T(8,128)(2,1)S(1)} %collective-permute-done.16, bf16[4,8,192,256]{3,2,1,0:T(8,128)(2,1)} %shard_map.64, s32[]{:T(128)S(6)} %select_n.137), kind=kLoop, calls=%fused_computation.2 | loop fusion | flops 2359296 | bytes 3145732 | tf_op jit(solution)/shard_map/convert_element_type | solution.py:150
  116.7 10.4 %all-to-all-done = bf16[8,192,256]{2,1,0:T(8,128)(2,1)S(1)} async-done(((bf16[8,192,256]{2,1,0:T(8,128)(2,1)}), bf16[8,192,256]{2,1,0:T(8,128)(2,1)S(1)}, u32[]{:S(2)}, u32[]{:S(2)}) %all-to-all-start) | async-done | bytes 786464 | tf_op jit(solution)/shard_map/all_to_all | solution.py:151
  127.2 3.5 %all-to-all-start.1 = ((bf16[8,192,256]{2,1,0:T(8,128)(2,1)}), bf16[8,192,256]{2,1,0:T(8,128)(2,1)S(1)}, u32[]{:S(2)}, u32[]{:S(2)}) async-start(bf16[8,192,256]{2,1,0:T(8,128)(2,1)} %fusion.1), calls=%async_computation.2 | async-start | bytes 1572864 | tf_op jit(solution)/shard_map/all_to_all | solution.py:151
  130.7 6.6 %reduce-scatter.2.cloned.1.call-done = bf16[1,4,384,256]{3,2,1,0:T(8,128)(2,1)} async-done(((bf16[8,4,384,256]{3,2,1,0:T(8,128)(2,1)}), bf16[1,4,384,256]{3,2,1,0:T(8,128)(2,1)}) %reduce-scatter.2.cloned.1.call-update) | async-done | bytes 786448 | tf_op jit(solution)/shard_map/reduce_scatter | solution.py:107
  138.4 5.8 %collective-permute-start.2 = (bf16[192,256]{1,0:T(8,128)(2,1)S(1)}, bf16[192,256]{1,0:T(8,128)(2,1)S(1)}, u32[]{:S(2)}, u32[]{:S(2)}) collective-permute-start(bf16[192,256]{1,0:T(8,128)(2,1)S(1)} %get-tuple-element.20), channel_id=1, source_target_pairs={{0,8},{8,16},{16,24},{24,0},{1,9},{9,17},{17,25},{25,1},{2,10},{10... | collective-permute-start | bytes 294920 | tf_op jit(solution)/shard_map/ppermute | solution.py:23
  144.1 2.2 %collective-permute-start.4 = (bf16[192,256]{1,0:T(8,128)(2,1)S(1)}, bf16[192,256]{1,0:T(8,128)(2,1)S(1)}, u32[]{:S(2)}, u32[]{:S(2)}) collective-permute-start(bf16[192,256]{1,0:T(8,128)(2,1)S(1)} %get-tuple-element.22), channel_id=1, source_target_pairs={{0,24},{8,0},{16,8},{24,16},{1,25},{9,1},{17,9},{25,17},{2,26},{10... | collective-permute-start | bytes 294920 | tf_op jit(solution)/shard_map/ppermute | solution.py:23
  146.3 2.5 %collective-permute-done.2 = bf16[192,256]{1,0:T(8,128)(2,1)S(1)} collective-permute-done((bf16[192,256]{1,0:T(8,128)(2,1)S(1)}, bf16[192,256]{1,0:T(8,128)(2,1)S(1)}, u32[]{:S(2)}, u32[]{:S(2)}) %collective-permute-start.2) | collective-permute-done | bytes 98336 | tf_op jit(solution)/shard_map/ppermute | solution.py:23
  150.8 2.4 %collective-permute-start.5 = (bf16[384,256]{1,0:T(8,128)(2,1)S(1)}, bf16[384,256]{1,0:T(8,128)(2,1)S(1)}, u32[]{:S(2)}, u32[]{:S(2)}) collective-permute-start(bf16[384,256]{1,0:T(8,128)(2,1)S(1)} %pad_maximum_fusion.7), channel_id=1, source_target_pairs={{0,24},{8,0},{16,8},{24,16},{1,25},{9,1},{17,9},{25,17},{2,26},{10... | collective-permute-start | bytes 589832 | tf_op jit(solution)/shard_map/ppermute | solution.py:23
  153.6 3.0 %collective-permute-done.5 = bf16[384,256]{1,0:T(8,128)(2,1)S(1)} collective-permute-done((bf16[384,256]{1,0:T(8,128)(2,1)S(1)}, bf16[384,256]{1,0:T(8,128)(2,1)S(1)}, u32[]{:S(2)}, u32[]{:S(2)}) %collective-permute-start.5) | collective-permute-done | bytes 196640 | tf_op jit(solution)/shard_map/ppermute | solution.py:23
  156.6 3.6 %collective-permute-done.3 = bf16[384,256]{1,0:T(8,128)(2,1)S(1)} collective-permute-done((bf16[384,256]{1,0:T(8,128)(2,1)S(1)}, bf16[384,256]{1,0:T(8,128)(2,1)S(1)}, u32[]{:S(2)}, u32[]{:S(2)}) %collective-permute-start.3) | collective-permute-done | bytes 196640 | tf_op jit(solution)/shard_map/ppermute | solution.py:23
  161.3 1.5 collective-permute-start.19
  162.9 1.8 collective-permute-start.20
  164.6 4.7 %collective-permute-done.19 = bf16[384,256]{1,0:T(8,128)(2,1)S(1)} collective-permute-done((bf16[384,256]{1,0:T(8,128)(2,1)S(1)}, bf16[384,256]{1,0:T(8,128)(2,1)S(1)}, u32[]{:S(2)}, u32[]{:S(2)}) %collective-permute-start.19) | collective-permute-done | bytes 196640 | tf_op jit(solution)/shard_map/ppermute | solution.py:123
  170.2 7.3 %all-to-all-start.2 = ((f32[32,1,768]{2,1,0:T(1,128)}), f32[32,1,768]{2,1,0:T(1,128)S(1)}, u32[]{:S(2)}, u32[]{:S(2)}) async-start(f32[32,1,768]{2,1,0:T(1,128)} %broadcast_in_dim.9), calls=%async_computation.3 | async-start | bytes 196608 | tf_op jit(solution)/shard_map/all_to_all | solution.py:156
  178.3 9.7 %all-to-all-done.2 = f32[32,1,768]{2,1,0:T(1,128)S(1)} async-done(((f32[32,1,768]{2,1,0:T(1,128)}), f32[32,1,768]{2,1,0:T(1,128)S(1)}, u32[]{:S(2)}, u32[]{:S(2)}) %all-to-all-start.2) | async-done | bytes 98336 | tf_op jit(solution)/shard_map/all_to_all | solution.py:156
  (80 shorter events, 27.8 us)
Async XLA Ops:
  7.2 130.1 %reduce-scatter.2.cloned.1.call-start = ((), (), s32[]{:S(2)}) async-start(), calls=%async_computation.4 | async-start | bytes 7077888 | tf_op jit(solution)/shard_map/reduce_scatter | solution.py:107
  7.2 3.1 %copy-start.3 = (bf16[1,768,896]{2,1,0:T(8,128)(2,1)S(1)}, bf16[1,768,896]{2,1,0:T(8,128)(2,1)}, u32[]{:S(2)}) copy-start(bf16[1,768,896]{2,1,0:T(8,128)(2,1)} %param.4) | copy-start | bytes 4128772
  10.3 4.5 %collective-permute-start.1 = (bf16[2,24,2048]{2,1,0:T(8,128)(2,1)}, bf16[2,24,2048]{2,1,0:T(8,128)(2,1)S(1)}, u32[]{:S(2)}, u32[]{:S(2)}) collective-permute-start(bf16[2,24,2048]{2,1,0:T(8,128)(2,1)} %pad_maximum_fusion.5), channel_id=1, source_target_pairs={{0,32},{32,0},{1,33},{33,1},{2,34},{34,2},{3,35},{35,3},{4,36},{36... | collective-permute-start | bytes 589832 | tf_op jit(solution)/shard_map/ppermute | solution.py:28
  10.3 8.8 %collective-permute-start = (bf16[768,896]{1,0:T(8,128)(2,1)S(1)}, bf16[768,896]{1,0:T(8,128)(2,1)}, u32[]{:S(2)}, u32[]{:S(2)}) collective-permute-start(bf16[768,896]{1,0:T(8,128)(2,1)S(1)} %bitcast.89), channel_id=1, source_target_pairs={{0,32},{32,0},{1,33},{33,1},{2,34},{34,2},{3,35},{35,3},{4,36},{36... | collective-permute-start | bytes 4128776 | tf_op jit(solution)/shard_map/ppermute | solution.py:28
  11.8 19.8 %collective-permute-start.6 = (bf16[384,896]{1,0:T(8,128)(2,1)S(1)}, bf16[384,896]{1,0:T(8,128)(2,1)S(1)}, u32[]{:S(2)}, u32[]{:S(2)}) collective-permute-start(bf16[384,896]{1,0:T(8,128)(2,1)S(1)} %bitcast.91), channel_id=1, source_target_pairs={{0,64},{64,0},{1,65},{65,1},{2,66},{66,2},{3,67},{67,3},{4,68},{68... | collective-permute-start | bytes 2064392 | tf_op jit(solution)/shard_map/ppermute | solution.py:28
  14.8 21.0 %collective-permute-start.8 = (bf16[2,24,2048]{2,1,0:T(8,128)(2,1)S(1)}, bf16[2,24,2048]{2,1,0:T(8,128)(2,1)S(1)}, u32[]{:S(2)}, u32[]{:S(2)}) collective-permute-start(bf16[2,24,2048]{2,1,0:T(8,128)(2,1)S(1)} %pad_maximum_fusion.8), channel_id=1, source_target_pairs={{0,64},{64,0},{1,65},{65,1},{2,66},{66,2},{3,67},{67,3},{4,68},{68... | collective-permute-start | bytes 589832 | tf_op jit(solution)/shard_map/ppermute | solution.py:28
  17.0 35.7 %collective-permute-start.13 = (bf16[384,896]{1,0:T(8,128)(2,1)}, bf16[384,896]{1,0:T(8,128)(2,1)}, u32[]{:S(2)}, u32[]{:S(2)}) collective-permute-start(bf16[384,896]{1,0:T(8,128)(2,1)} %shard_map.62), channel_id=1, source_target_pairs={{0,64},{64,0},{1,65},{65,1},{2,66},{66,2},{3,67},{67,3},{4,68},{68... | collective-permute-start | bytes 2064392 | tf_op jit(solution)/shard_map/ppermute | solution.py:28
  31.6 0.9 copy-start.4
  32.5 4.7 %collective-permute-start.7 = (bf16[384,896]{1,0:T(8,128)(2,1)}, bf16[384,896]{1,0:T(8,128)(2,1)S(1)}, u32[]{:S(2)}, u32[]{:S(2)}) collective-permute-start(bf16[384,896]{1,0:T(8,128)(2,1)} %shard_map.60.h0_ref), channel_id=1, source_target_pairs={{0,32},{32,0},{1,33},{33,1},{2,34},{34,2},{3,35},{35,3},{4,36},{36... | collective-permute-start | bytes 2064392 | tf_op jit(solution)/shard_map/ppermute | solution.py:28
  49.5 10.7 %collective-permute-start.9 = (bf16[4,192,256]{2,1,0:T(8,128)(2,1)}, bf16[4,192,256]{2,1,0:T(8,128)(2,1)}, u32[]{:S(2)}, u32[]{:S(2)}) collective-permute-start(bf16[4,192,256]{2,1,0:T(8,128)(2,1)} %get-tuple-element.6), channel_id=1, source_target_pairs={{0,8},{8,16},{16,24},{24,0},{1,9},{9,17},{17,25},{25,1},{2,10},{10... | collective-permute-start | bytes 1179656 | tf_op jit(solution)/shard_map/ppermute | solution.py:23
  51.0 9.3 %copy-start = (bf16[4,8,192,256]{3,2,1,0:T(8,128)(2,1)S(1)}, bf16[4,8,192,256]{3,2,1,0:T(8,128)(2,1)}, u32[]{:S(2)}) copy-start(bf16[4,8,192,256]{3,2,1,0:T(8,128)(2,1)} %shard_map.61.refs_1_) | copy-start | bytes 9437188
  51.0 9.2 %collective-permute-start.11 = (bf16[4,192,256]{2,1,0:T(8,128)(2,1)}, bf16[4,192,256]{2,1,0:T(8,128)(2,1)}, u32[]{:S(2)}, u32[]{:S(2)}) collective-permute-start(bf16[4,192,256]{2,1,0:T(8,128)(2,1)} %get-tuple-element.8), channel_id=1, source_target_pairs={{0,24},{8,0},{16,8},{24,16},{1,25},{9,1},{17,9},{25,17},{2,26},{10... | collective-permute-start | bytes 1179656 | tf_op jit(solution)/shard_map/ppermute | solution.py:23
  52.7 8.7 %copy-start.2 = (bf16[4,192,256]{2,1,0:T(8,128)(2,1)S(1)}, bf16[4,192,256]{2,1,0:T(8,128)(2,1)}, u32[]{:S(2)}) copy-start(bf16[4,192,256]{2,1,0:T(8,128)(2,1)} %get-tuple-element.7) | copy-start | bytes 1179652
  52.7 13.7 %collective-permute-start.14 = (bf16[384,896]{1,0:T(8,128)(2,1)}, bf16[384,896]{1,0:T(8,128)(2,1)S(1)}, u32[]{:S(2)}, u32[]{:S(2)}) collective-permute-start(bf16[384,896]{1,0:T(8,128)(2,1)} %shard_map.63.h0_ref), channel_id=1, source_target_pairs={{0,32},{32,0},{1,33},{33,1},{2,34},{34,2},{3,35},{35,3},{4,36},{36... | collective-permute-start | bytes 2064392 | tf_op jit(solution)/shard_map/ppermute | solution.py:28
  62.4 19.5 %collective-permute-start.12 = (bf16[8,192,256]{2,1,0:T(8,128)(2,1)}, bf16[8,192,256]{2,1,0:T(8,128)(2,1)}, u32[]{:S(2)}, u32[]{:S(2)}) collective-permute-start(bf16[8,192,256]{2,1,0:T(8,128)(2,1)} %pad_maximum_fusion.1), channel_id=1, source_target_pairs={{0,24},{8,0},{16,8},{24,16},{1,25},{9,1},{17,9},{25,17},{2,26},{10... | collective-permute-start | bytes 2359304 | tf_op jit(solution)/shard_map/ppermute | solution.py:23
  66.4 21.9 %collective-permute-start.10 = (bf16[8,192,256]{2,1,0:T(8,128)(2,1)}, bf16[8,192,256]{2,1,0:T(8,128)(2,1)}, u32[]{:S(2)}, u32[]{:S(2)}) collective-permute-start(bf16[8,192,256]{2,1,0:T(8,128)(2,1)} %pad_maximum_fusion), channel_id=1, source_target_pairs={{0,8},{8,16},{16,24},{24,0},{1,9},{9,17},{17,25},{25,1},{2,10},{10... | collective-permute-start | bytes 2359304 | tf_op jit(solution)/shard_map/ppermute | solution.py:23
  66.4 0.9 copy-start.6
  78.6 20.8 %collective-permute-start.15 = (bf16[4,192,256]{2,1,0:T(8,128)(2,1)}, bf16[4,192,256]{2,1,0:T(8,128)(2,1)}, u32[]{:S(2)}, u32[]{:S(2)}) collective-permute-start(bf16[4,192,256]{2,1,0:T(8,128)(2,1)} %get-tuple-element.12), channel_id=1, source_target_pairs={{0,8},{8,16},{16,24},{24,0},{1,9},{9,17},{17,25},{25,1},{2,10},{10... | collective-permute-start | bytes 1179656 | tf_op jit(solution)/shard_map/ppermute | solution.py:23
  79.5 19.9 %collective-permute-start.17 = (bf16[4,192,256]{2,1,0:T(8,128)(2,1)}, bf16[4,192,256]{2,1,0:T(8,128)(2,1)}, u32[]{:S(2)}, u32[]{:S(2)}) collective-permute-start(bf16[4,192,256]{2,1,0:T(8,128)(2,1)} %get-tuple-element.14), channel_id=1, source_target_pairs={{0,24},{8,0},{16,8},{24,16},{1,25},{9,1},{17,9},{25,17},{2,26},{10... | collective-permute-start | bytes 1179656 | tf_op jit(solution)/shard_map/ppermute | solution.py:23
  90.8 36.3 %all-to-all-start = ((bf16[8,192,256]{2,1,0:T(8,128)(2,1)}), bf16[8,192,256]{2,1,0:T(8,128)(2,1)S(1)}, u32[]{:S(2)}, u32[]{:S(2)}) async-start(bf16[8,192,256]{2,1,0:T(8,128)(2,1)} %fusion.3), calls=%async_computation.1 | async-start | bytes 1572864 | tf_op jit(solution)/shard_map/all_to_all | solution.py:151
  99.3 1.5 copy-start.1
  100.9 12.1 %collective-permute-start.18 = (bf16[8,192,256]{2,1,0:T(8,128)(2,1)S(1)}, bf16[8,192,256]{2,1,0:T(8,128)(2,1)S(1)}, u32[]{:S(2)}, u32[]{:S(2)}) collective-permute-start(bf16[8,192,256]{2,1,0:T(8,128)(2,1)S(1)} %pad_maximum_fusion.3), channel_id=1, source_target_pairs={{0,24},{8,0},{16,8},{24,16},{1,25},{9,1},{17,9},{25,17},{2,26},{10... | collective-permute-start | bytes 2359304 | tf_op jit(solution)/shard_map/ppermute | solution.py:23
  101.1 13.3 %collective-permute-start.16 = (bf16[8,192,256]{2,1,0:T(8,128)(2,1)S(1)}, bf16[8,192,256]{2,1,0:T(8,128)(2,1)S(1)}, u32[]{:S(2)}, u32[]{:S(2)}) collective-permute-start(bf16[8,192,256]{2,1,0:T(8,128)(2,1)S(1)} %pad_maximum_fusion.2), channel_id=1, source_target_pairs={{0,8},{8,16},{16,24},{24,0},{1,9},{9,17},{17,25},{25,1},{2,10},{10... | collective-permute-start | bytes 2359304 | tf_op jit(solution)/shard_map/ppermute | solution.py:23
  127.2 26.3 %all-to-all-start.1 = ((bf16[8,192,256]{2,1,0:T(8,128)(2,1)}), bf16[8,192,256]{2,1,0:T(8,128)(2,1)S(1)}, u32[]{:S(2)}, u32[]{:S(2)}) async-start(bf16[8,192,256]{2,1,0:T(8,128)(2,1)} %fusion.1), calls=%async_computation.2 | async-start | bytes 1572864 | tf_op jit(solution)/shard_map/all_to_all | solution.py:151
  138.4 10.5 %collective-permute-start.2 = (bf16[192,256]{1,0:T(8,128)(2,1)S(1)}, bf16[192,256]{1,0:T(8,128)(2,1)S(1)}, u32[]{:S(2)}, u32[]{:S(2)}) collective-permute-start(bf16[192,256]{1,0:T(8,128)(2,1)S(1)} %get-tuple-element.20), channel_id=1, source_target_pairs={{0,8},{8,16},{16,24},{24,0},{1,9},{9,17},{17,25},{25,1},{2,10},{10... | collective-permute-start | bytes 294920 | tf_op jit(solution)/shard_map/ppermute | solution.py:23
  144.1 5.7 %collective-permute-start.4 = (bf16[192,256]{1,0:T(8,128)(2,1)S(1)}, bf16[192,256]{1,0:T(8,128)(2,1)S(1)}, u32[]{:S(2)}, u32[]{:S(2)}) collective-permute-start(bf16[192,256]{1,0:T(8,128)(2,1)S(1)} %get-tuple-element.22), channel_id=1, source_target_pairs={{0,24},{8,0},{16,8},{24,16},{1,25},{9,1},{17,9},{25,17},{2,26},{10... | collective-permute-start | bytes 294920 | tf_op jit(solution)/shard_map/ppermute | solution.py:23
  150.8 5.8 %collective-permute-start.5 = (bf16[384,256]{1,0:T(8,128)(2,1)S(1)}, bf16[384,256]{1,0:T(8,128)(2,1)S(1)}, u32[]{:S(2)}, u32[]{:S(2)}) collective-permute-start(bf16[384,256]{1,0:T(8,128)(2,1)S(1)} %pad_maximum_fusion.7), channel_id=1, source_target_pairs={{0,24},{8,0},{16,8},{24,16},{1,25},{9,1},{17,9},{25,17},{2,26},{10... | collective-permute-start | bytes 589832 | tf_op jit(solution)/shard_map/ppermute | solution.py:23
  153.3 7.0 %collective-permute-start.3 = (bf16[384,256]{1,0:T(8,128)(2,1)S(1)}, bf16[384,256]{1,0:T(8,128)(2,1)S(1)}, u32[]{:S(2)}, u32[]{:S(2)}) collective-permute-start(bf16[384,256]{1,0:T(8,128)(2,1)S(1)} %pad_maximum_fusion.6), channel_id=1, source_target_pairs={{0,8},{8,16},{16,24},{24,0},{1,9},{9,17},{17,25},{25,1},{2,10},{10... | collective-permute-start | bytes 589832 | tf_op jit(solution)/shard_map/ppermute | solution.py:23
  161.3 26.8 %copy-start.5 = (f32[1,256]{1,0:T(1,128)S(1)}, f32[1,256]{1,0:T(1,128)}, u32[]{:S(2)}) copy-start(f32[1,256]{1,0:T(1,128)} %param.7) | copy-start | bytes 3076
  161.3 8.0 %collective-permute-start.19 = (bf16[384,256]{1,0:T(8,128)(2,1)S(1)}, bf16[384,256]{1,0:T(8,128)(2,1)S(1)}, u32[]{:S(2)}, u32[]{:S(2)}) collective-permute-start(bf16[384,256]{1,0:T(8,128)(2,1)S(1)} %get-tuple-element.2), channel_id=1, source_target_pairs={{0,192},{1,193},{2,194},{3,195},{4,196},{5,197},{6,198},{7,199},{8... | collective-permute-start | bytes 589832 | tf_op jit(solution)/shard_map/ppermute | solution.py:123
  162.9 6.5 %collective-permute-start.20 = (bf16[384,256]{1,0:T(8,128)(2,1)S(1)}, bf16[384,256]{1,0:T(8,128)(2,1)S(1)}, u32[]{:S(2)}, u32[]{:S(2)}) collective-permute-start(bf16[384,256]{1,0:T(8,128)(2,1)S(1)} %broadcast_select_fusion), channel_id=1, source_target_pairs={{0,128},{1,129},{2,130},{3,131},{4,132},{5,133},{6,134},{7,135},{8... | collective-permute-start | bytes 589832 | tf_op jit(solution)/shard_map/ppermute | solution.py:122
  170.2 17.7 %all-to-all-start.2 = ((f32[32,1,768]{2,1,0:T(1,128)}), f32[32,1,768]{2,1,0:T(1,128)S(1)}, u32[]{:S(2)}, u32[]{:S(2)}) async-start(f32[32,1,768]{2,1,0:T(1,128)} %broadcast_in_dim.9), calls=%async_computation.3 | async-start | bytes 196608 | tf_op jit(solution)/shard_map/all_to_all | solution.py:156
  (1 other events, 0.8 us)
Sparse Core Ops, SparseCore 0:
  37.3 99.9 reduce-scatter.1

commit v3 on v2

--- a/solution.py
+++ b/solution.py
@@ -11,9 +11,11 @@
 D = 8192
 NZ, NY = 8, 4
 COLS = 256
+STEP = 2
 HALF = 384
 ORDER = ((0, 192), (192, HALF))
-SCALE, FAR = 1, 100
+TIE = 3 * 10**11
+SCALE, FAR = 20, 1
 VMEM = 58 * 2**20
 AXES = ("s", "xh", "c", "y", "z")
 F32, BF16 = jnp.float32, jnp.bfloat16
@@ -31,14 +33,16 @@
 def product_kernel(first, rows, y_major, m_ref, h0_ref, h1_ref, w_ref, r0_ref, r1_ref, *refs):
     out_ref = refs[-1]
 
-    def block(i, half):
-        return (i * 2 + half, 0) if y_major else (0, i * 2 + half)
+    def block(i, half, k):
+        return (i * 2 + half, k) if y_major else (k, i * 2 + half)
 
+    parts = [slice(k * COLS, (k + 1) * COLS) for k in range(STEP)]
     for i, h_ref in enumerate((h0_ref, h1_ref)):
         for half in range(2):
             at = half * rows
             acc = jnp.dot(h_ref[at : at + rows], w_ref[...], preferred_element_type=F32)
-            out_ref[block(i, half)] = acc.astype(BF16)
+            for k, part in enumerate(parts):
+                out_ref[block(i, half, k)] = acc[:, part].astype(BF16)
 
     m = m_ref[0]
     row = m % 16 * 24
@@ -47,28 +51,32 @@
     def _():
         window = pl.ds(pl.multiple_of(row // 16 * 16 - first, 16), 32)
         for i, r_ref in enumerate((r0_ref, r1_ref)):
-            at = block(i, m // 16) + (window, slice(None))
-            out_ref[at] = (out_ref[at].astype(F32) + r_ref[...].astype(F32)).astype(BF16)
+            none = jnp.zeros((8, COLS), F32)
+            for k, part in enumerate(parts):
+                r = r_ref[:, part].astype(F32)
+                late, soon = jnp.concatenate([none, r]), jnp.concatenate([r, none])
+                at = block(i, m // 16, k) + (window, slice(None))
+                out_ref[at] = (out_ref[at].astype(F32) + jnp.where(row % 16 == 8, late, soon)).astype(BF16)
 
 
 def product(m, h, w, res, first, rows, y_major, scale=1, after=()):
     whole = lambda j: (0, 0)
     columns = lambda j: (0, j)
     if y_major:
-        shape, block, place = (NY, NZ, rows, COLS), (NY, 1, rows, COLS), lambda j: (0, j, 0, 0)
+        shape, block, place = (NY, NZ, rows, COLS), (NY, STEP, rows, COLS), lambda j: (0, j, 0, 0)
     else:
-        shape, block, place = (NZ, NY, rows, COLS), (1, NY, rows, COLS), lambda j: (j, 0, 0, 0)
+        shape, block, place = (NZ, NY, rows, COLS), (STEP, NY, rows, COLS), lambda j: (j, 0, 0, 0)
     return pl.pallas_call(
         functools.partial(product_kernel, first, rows, y_major),
         out_shape=jax.ShapeDtypeStruct(shape, BF16),
-        grid=(NZ,),
+        grid=(NZ // STEP,),
         in_specs=[
             pl.BlockSpec(memory_space=pltpu.SMEM),
             pl.BlockSpec(h[0].shape, whole),
             pl.BlockSpec(h[1].shape, whole),
-            pl.BlockSpec((w.shape[0], COLS), columns),
-            pl.BlockSpec((32, COLS), columns),
-            pl.BlockSpec((32, COLS), columns),
+            pl.BlockSpec((w.shape[0], STEP * COLS), columns),
+            pl.BlockSpec((24, STEP * COLS), columns),
+            pl.BlockSpec((24, STEP * COLS), columns),
         ]
         + [pl.BlockSpec(memory_space=pl.ANY)] * len(after),
         out_specs=pl.BlockSpec(block, place),
@@ -81,7 +89,7 @@
     )(m, h[0], h[1], w, res[0], res[1], *after)
 
 
-def tied(x, *after):
+def tied(x, *after, flops=0):
     anywhere = pl.BlockSpec(memory_space=pl.ANY)
     return pl.pallas_call(
         lambda *refs: None,
@@ -89,6 +97,7 @@
         in_specs=[anywhere] * (1 + len(after)),
         out_specs=anywhere,
         input_output_aliases={0: 0},
+        cost_estimate=pl.CostEstimate(flops=flops, bytes_accessed=0, transcendentals=0),
     )(x, *after)
 
 
@@ -129,23 +138,21 @@
     h, w, gain = hidden[0], down_weight[0], norm_gain[0]
     xh, c, y, z = (lax.axis_index(a) for a in AXES[1:])
     group = xh * 2 + c
-    res = residual[0].reshape(24, 4, 2048)
-    part = lambda x, r: lax.dynamic_index_in_dim(x, group ^ r, axis=1, keepdims=False)
-    got = flipped(jnp.stack([part(res, 1), part(res, 3)]), "c")
-    far = flipped(jnp.stack([part(res, 2), got[1]]), "xh")
+    part = lambda r: lax.dynamic_slice_in_dim(residual[0], (group ^ r) * 2048, 2048, axis=1)
+    got = flipped(jnp.stack([part(1), part(3)]), "c")
+    far_res = jnp.stack([part(2), got[1]])
+    near_res = (part(0), got[0])
     m = y * NZ + z
-    pad = lambda x: jnp.where(m % 2 == 0, jnp.pad(x, ((0, 8), (0, 0))), jnp.pad(x, ((8, 0), (0, 0))))
-    near_res = (pad(part(res, 0)), pad(got[0]))
-    far_res = (pad(far[0]), pad(far[1]))
     m = m.reshape(1)
     core = flipped(h, "c")
     product_near = product(m, (h, core), w, near_res, 0, HALF, False, SCALE)
+    far_res = flipped(far_res, "xh")
     near = summed_along_y(summed_along_z(product_near), y).astype(BF16)
     sums, last = [], product_near
     for a, b in ORDER:
         x = h.reshape(2, HALF, -1)[:, a:b].reshape(2 * (b - a), -1)
         x = flipped(tied(x, near_res[1]) if a else x, "xh")
-        x = tied(x, last)
+        x = tied(x, last, flops=0 if a else TIE)
         x = last = product(m, (x, flipped(x, "c")), w, far_res, a, b - a, True, 1 if a else FAR)
         x = summed_along_y(x, y).astype(BF16)
         x = lax.all_to_all(x, "z", split_axis=0, concat_axis=0, tiled=True)

time: 198 us -> 183 us (0.924)
  waiting for transfers between devices: 70.3 us -> 60.4 us
  Pallas kernels: 29.9 us -> 25.1 us
  local copies, waits for them, and re-layouts: 12.6 us -> 16.6 us
  other arithmetic: 17.4 us -> 14.1 us
    ppermute x12, waiting for transfers between devices: 35.1 us -> 25 us  [shifted(): return lax.ppermute(x, axis, [(i, (i + by) % n) for i in range(n)])]
    reduce_scatter x1, waiting for transfers between devices: 6.57 us -> 0.02 us  [summed_along_z(): return lax.psum_scatter(x, 'z', scatter_dimension=0, tiled=False)]
    ppermute x7, waiting for transfers between devices: 3.86 us -> 10.1 us  [flipped(): return lax.ppermute(x, axes, [(i, n - 1 - i) for i in range(n)])]
    pallas_call x3, Pallas kernels: 29.9 us -> 25.1 us  [product(): pl.pallas_call(functools.partial(product_kernel, first, rows, y_major), o...]
    ppermute x1, starting transfers between devices: 1.52 us -> 4.45 us  [handed_over(): two = lax.ppermute(two, AXES, handing(1))]
    select_n x4 -> x0, other arithmetic: 2.7 us -> none  [shards(): jnp.where(m % 2 == 0, jnp.pad(x, ((0, 8), (0, 0))), jnp.pad(x, ((8, 0), (...]
    all_to_all x2, waiting for transfers between devices: 10.4 us -> 12.7 us  [shards(): x = lax.all_to_all(x, 'z', split_axis=0, concat_axis=0, tiled=True)]
    ppermute x1, waiting for transfers between devices: 4.68 us -> 2.41 us  [handed_over(): two = lax.ppermute(two, AXES, handing(1))]
  transfers between devices with their start and end apart: 25 -> 25, of which waited for: 14 -> 14; matrix products, arithmetic and copies ran while one was open for 11% -> 13% of each run, Pallas kernels for 15% -> 14%
where the time goes in v3:
time: 183 us; the launch traced here: 181 us
  waiting for transfers between devices  60.4 us (33%)
  starting transfers between devices  50.9 us (28%)
  Pallas kernels  25.1 us (14%)
  local copies, waits for them, and re-layouts  16.6 us (9%)
  between operations  14.3 us (8%)
  other arithmetic  14.1 us (8%)
    pallas_call x3, Pallas kernels, product(): pl.pallas_call(functools.partial(product_kernel, first, rows, y_major), o...  25.1 us
    ppermute x12, waiting for transfers between devices, shifted(): return lax.ppermute(x, axis, [(i, (i + by) % n) for i in range(n)])  25 us
    ppermute x12, starting transfers between devices, shifted(): return lax.ppermute(x, axis, [(i, (i + by) % n) for i in range(n)])  20 us
    all_to_all x2, waiting for transfers between devices, shards(): x = lax.all_to_all(x, 'z', split_axis=0, concat_axis=0, tiled=True)  12.7 us
    all_to_all x2, starting transfers between devices, shards(): x = lax.all_to_all(x, 'z', split_axis=0, concat_axis=0, tiled=True)  11.9 us
    ppermute x7, waiting for transfers between devices, flipped(): return lax.ppermute(x, axes, [(i, n - 1 - i) for i in range(n)])  10.1 us
    all_to_all x1, waiting for transfers between devices, shards(): lax.all_to_all(jnp.broadcast_to(squares, (NY * NZ, 768)), ('y', 'z'), spl...  9.37 us
    all_to_all x1, starting transfers between devices, shards(): lax.all_to_all(jnp.broadcast_to(squares, (NY * NZ, 768)), ('y', 'z'), spl...  7.48 us
  transfers between devices with their start and end apart: 25, of which 14 were waited for; matrix products, arithmetic and copies ran while one was open for 13% of the time, Pallas kernels for 14%

profile of v3, /device:TPU:2, one launch (start us, length us, event | category | flops | bytes accessed | tf_op | source)
XLA Modules:
  0.0 181.4 jit_solution(6025633497015867299)
XLA Ops:
  7.3 1.7 constant_dynamic-slice_fusion
  9.7 2.3 %fusion.14 = (bf16[2,192,896]{2,1,0:T(8,128)(2,1)S(1)}, bf16[2,192,896]{2,1,0:T(8,128)(2,1)}) fusion(bf16[2,384,896]{2,1,0:T(8,128)(2,1)} %bitcast.81), kind=kLoop, calls=%fused_computation.58 | loop fusion | bytes 2752512 | tf_op jit(solution)/shard_map/slice | solution.py:153
  11.9 2.1 %collective-permute-start.6 = (bf16[384,896]{1,0:T(8,128)(2,1)S(1)}, bf16[384,896]{1,0:T(8,128)(2,1)S(1)}, u32[]{:S(2)}, u32[]{:S(2)}) collective-permute-start(bf16[384,896]{1,0:T(8,128)(2,1)S(1)} %bitcast.83), channel_id=1, source_target_pairs={{0,64},{64,0},{1,65},{65,1},{2,66},{66,2},{3,67},{67,3},{4,68},{68... | collective-permute-start | bytes 2064392 | tf_op jit(solution)/shard_map/ppermute | solution.py:30
  15.8 10.7 %shard_map.59.refs_1_ = bf16[8,4,384,256]{3,2,1,0:T(8,128)(2,1)} custom-call(s32[1]{0:T(128)} %bitcast.m_ref, bf16[768,896]{1,0:T(8,128)(2,1)} %bitcast.82, bf16[768,896]{1,0:T(8,128)(2,1)} %copy-done.6, bf16[896,2048]{1,0:T(8,128)(2,1)} %bitcast.85, bf16[24,2048]{1,0:T(8,128)(2,1)} %get-tuple-element.28.r0_ref, ...), custom_call_target="tpu_custom_call" | custom-call | flops 112742891520 | bytes 12713984 | tf_op jit(solution)/shard_map/pallas_call | solution.py:69
  26.5 4.3 %collective-permute-done.6.refs_0_ = bf16[384,896]{1,0:T(8,128)(2,1)S(1)} collective-permute-done((bf16[384,896]{1,0:T(8,128)(2,1)S(1)}, bf16[384,896]{1,0:T(8,128)(2,1)S(1)}, u32[]{:S(2)}, u32[]{:S(2)}) %collective-permute-start.6) | collective-permute-done | bytes 688160 | tf_op jit(solution)/shard_map/ppermute | solution.py:30
  32.6 2.2 %collective-permute-start.8 = (bf16[2,24,2048]{2,1,0:T(8,128)(2,1)S(1)}, bf16[2,24,2048]{2,1,0:T(8,128)(2,1)S(1)}, u32[]{:S(2)}, u32[]{:S(2)}) collective-permute-start(bf16[2,24,2048]{2,1,0:T(8,128)(2,1)S(1)} %pad_maximum_fusion.8), channel_id=1, source_target_pairs={{0,64},{64,0},{1,65},{65,1},{2,66},{66,2},{3,67},{67,3},{4,68},{68... | collective-permute-start | bytes 589832 | tf_op jit(solution)/shard_map/ppermute | solution.py:30
  36.3 5.8 %collective-permute-done.8 = bf16[2,24,2048]{2,1,0:T(8,128)(2,1)S(1)} collective-permute-done((bf16[2,24,2048]{2,1,0:T(8,128)(2,1)S(1)}, bf16[2,24,2048]{2,1,0:T(8,128)(2,1)S(1)}, u32[]{:S(2)}, u32[]{:S(2)}) %collective-permute-start.8) | collective-permute-done | bytes 196640 | tf_op jit(solution)/shard_map/ppermute | solution.py:30
  43.6 7.2 %shard_map.61.refs_1_ = bf16[4,8,192,256]{3,2,1,0:T(8,128)(2,1)} custom-call(s32[1]{0:T(128)} %bitcast.m_ref, bf16[384,896]{1,0:T(8,128)(2,1)} %shard_map.60.h0_ref, bf16[384,896]{1,0:T(8,128)(2,1)} %copy-done.7, bf16[896,2048]{1,0:T(8,128)(2,1)} %bitcast.86, bf16[24,2048]{1,0:T(8,128)(2,1)} %get-tuple-element.31.r0_ref, ...), custom_call_target="tpu_custom_call" | custom-call | flops 2818572288 | bytes 8192000 | tf_op jit(solution)/shard_map/pallas_call | solution.py:69
  50.8 2.4 %dynamic-slice_bitcast_fusion.10 = (bf16[4,192,256]{2,1,0:T(8,128)(2,1)}, bf16[4,192,256]{2,1,0:T(8,128)(2,1)S(1)}, bf16[4,192,256]{2,1,0:T(8,128)(2,1)}, bf16[4,192,256]{2,1,0:T(8,128)(2,1)}) fusion(bf16[4,8,192,256]{3,2,1,0:T(8,128)(2,1)} %shard_map.61.refs_1_, s32[]{:T(128)S(6)} %select_n.106, s32[]{:T(128)S(6)} %select_n.108, s32[]{:T(128)S(6)} %add.162, ...), kind=kLoop, calls=%fused_computation.25 | loop fusion | bytes 3145744 | tf_op jit(solution)/shard_map/slice | solution.py:108
  53.3 2.9 %collective-permute-start.11 = (bf16[4,192,256]{2,1,0:T(8,128)(2,1)}, bf16[4,192,256]{2,1,0:T(8,128)(2,1)}, u32[]{:S(2)}, u32[]{:S(2)}) collective-permute-start(bf16[4,192,256]{2,1,0:T(8,128)(2,1)} %get-tuple-element.8), channel_id=1, source_target_pairs={{0,24},{8,0},{16,8},{24,16},{1,25},{9,1},{17,9},{25,17},{2,26},{10... | collective-permute-start | bytes 1179656 | tf_op jit(solution)/shard_map/ppermute | solution.py:25
  56.3 6.0 %collective-permute-done.11 = bf16[4,192,256]{2,1,0:T(8,128)(2,1)} collective-permute-done((bf16[4,192,256]{2,1,0:T(8,128)(2,1)}, bf16[4,192,256]{2,1,0:T(8,128)(2,1)}, u32[]{:S(2)}, u32[]{:S(2)}) %collective-permute-start.11) | collective-permute-done | bytes 393248 | tf_op jit(solution)/shard_map/ppermute | solution.py:25
  62.3 3.4 %collective-permute-done.9 = bf16[4,192,256]{2,1,0:T(8,128)(2,1)} collective-permute-done((bf16[4,192,256]{2,1,0:T(8,128)(2,1)}, bf16[4,192,256]{2,1,0:T(8,128)(2,1)}, u32[]{:S(2)}, u32[]{:S(2)}) %collective-permute-start.9) | collective-permute-done | bytes 393248 | tf_op jit(solution)/shard_map/ppermute | solution.py:25
  68.9 3.2 %collective-permute-start.12 = (bf16[8,192,256]{2,1,0:T(8,128)(2,1)}, bf16[8,192,256]{2,1,0:T(8,128)(2,1)}, u32[]{:S(2)}, u32[]{:S(2)}) collective-permute-start(bf16[8,192,256]{2,1,0:T(8,128)(2,1)} %pad_maximum_fusion.1), channel_id=1, source_target_pairs={{0,24},{8,0},{16,8},{24,16},{1,25},{9,1},{17,9},{25,17},{2,26},{10... | collective-permute-start | bytes 2359304 | tf_op jit(solution)/shard_map/ppermute | solution.py:25
  73.0 7.2 %shard_map.64 = bf16[4,8,192,256]{3,2,1,0:T(8,128)(2,1)} custom-call(s32[1]{0:T(128)} %bitcast.m_ref, bf16[384,896]{1,0:T(8,128)(2,1)} %shard_map.63.h0_ref, bf16[384,896]{1,0:T(8,128)(2,1)} %copy-done.9, bf16[896,2048]{1,0:T(8,128)(2,1)} %bitcast.87, bf16[24,2048]{1,0:T(8,128)(2,1)} %get-tuple-element.31.r0_ref, bf16[24,2048]{1,0:T(8,128)(2,1)} %get-tuple-element.30.r1_ref), custom_call_target="tpu_custom_call" | custom-call | flops 2818572288 | bytes 8192000 | tf_op jit(solution)/shard_map/pallas_call | solution.py:69
  80.2 2.4 %dynamic-slice_bitcast_fusion.4 = (bf16[4,192,256]{2,1,0:T(8,128)(2,1)}, bf16[4,192,256]{2,1,0:T(8,128)(2,1)S(1)}, bf16[4,192,256]{2,1,0:T(8,128)(2,1)}, bf16[4,192,256]{2,1,0:T(8,128)(2,1)}) fusion(bf16[4,8,192,256]{3,2,1,0:T(8,128)(2,1)} %shard_map.64, s32[]{:T(128)S(6)} %select_n.106, s32[]{:T(128)S(6)} %select_n.108, s32[]{:T(128)S(6)} %add.162, ...), kind=kLoop, calls=%fused_computation.17 | loop fusion | bytes 3145744 | tf_op jit(solution)/shard_map/slice | solution.py:108
  82.6 3.2 %collective-permute-start.17 = (bf16[4,192,256]{2,1,0:T(8,128)(2,1)}, bf16[4,192,256]{2,1,0:T(8,128)(2,1)}, u32[]{:S(2)}, u32[]{:S(2)}) collective-permute-start(bf16[4,192,256]{2,1,0:T(8,128)(2,1)} %get-tuple-element.14), channel_id=1, source_target_pairs={{0,24},{8,0},{16,8},{24,16},{1,25},{9,1},{17,9},{25,17},{2,26},{10... | collective-permute-start | bytes 1179656 | tf_op jit(solution)/shard_map/ppermute | solution.py:25
  85.8 1.7 collective-permute-done.10
  88.8 2.6 %fusion.3 = bf16[8,192,256]{2,1,0:T(8,128)(2,1)} fusion(bf16[8,192,256]{2,1,0:T(8,128)(2,1)} %collective-permute-done.12, bf16[8,192,256]{2,1,0:T(8,128)(2,1)} %collective-permute-done.10, bf16[4,8,192,256]{3,2,1,0:T(8,128)(2,1)S(1)} %copy-done, s32[]{:T(128)S(6)} %select_n.102), kind=kLoop, calls=%fused_computation.5 | loop fusion | flops 2359296 | bytes 3145732 | tf_op jit(solution)/shard_map/convert_element_type | solution.py:157
  91.4 8.4 %all-to-all-start = ((bf16[8,192,256]{2,1,0:T(8,128)(2,1)}), bf16[8,192,256]{2,1,0:T(8,128)(2,1)S(1)}, u32[]{:S(2)}, u32[]{:S(2)}) async-start(bf16[8,192,256]{2,1,0:T(8,128)(2,1)} %fusion.3), calls=%async_computation.1 | async-start | bytes 1572864 | tf_op jit(solution)/shard_map/all_to_all | solution.py:158
  101.5 3.8 %collective-permute-start.18 = (bf16[8,192,256]{2,1,0:T(8,128)(2,1)S(1)}, bf16[8,192,256]{2,1,0:T(8,128)(2,1)S(1)}, u32[]{:S(2)}, u32[]{:S(2)}) collective-permute-start(bf16[8,192,256]{2,1,0:T(8,128)(2,1)S(1)} %pad_maximum_fusion.3), channel_id=1, source_target_pairs={{0,24},{8,0},{16,8},{24,16},{1,25},{9,1},{17,9},{25,17},{2,26},{10... | collective-permute-start | bytes 2359304 | tf_op jit(solution)/shard_map/ppermute | solution.py:25
  105.3 9.8 %collective-permute-done.16 = bf16[8,192,256]{2,1,0:T(8,128)(2,1)S(1)} collective-permute-done((bf16[8,192,256]{2,1,0:T(8,128)(2,1)S(1)}, bf16[8,192,256]{2,1,0:T(8,128)(2,1)S(1)}, u32[]{:S(2)}, u32[]{:S(2)}) %collective-permute-start.16) | collective-permute-done | bytes 786464 | tf_op jit(solution)/shard_map/ppermute | solution.py:25
  115.1 2.3 %fusion.1 = bf16[8,192,256]{2,1,0:T(8,128)(2,1)} fusion(bf16[8,192,256]{2,1,0:T(8,128)(2,1)S(1)} %collective-permute-done.18, bf16[8,192,256]{2,1,0:T(8,128)(2,1)S(1)} %collective-permute-done.16, bf16[4,8,192,256]{3,2,1,0:T(8,128)(2,1)} %shard_map.64, s32[]{:T(128)S(6)} %select_n.102), kind=kLoop, calls=%fused_computation.2 | loop fusion | flops 2359296 | bytes 3145732 | tf_op jit(solution)/shard_map/convert_element_type | solution.py:157
  117.4 4.3 %all-to-all-done = bf16[8,192,256]{2,1,0:T(8,128)(2,1)S(1)} async-done(((bf16[8,192,256]{2,1,0:T(8,128)(2,1)}), bf16[8,192,256]{2,1,0:T(8,128)(2,1)S(1)}, u32[]{:S(2)}, u32[]{:S(2)}) %all-to-all-start) | async-done | bytes 786464 | tf_op jit(solution)/shard_map/all_to_all | solution.py:158
  121.8 3.5 %all-to-all-start.1 = ((bf16[8,192,256]{2,1,0:T(8,128)(2,1)}), bf16[8,192,256]{2,1,0:T(8,128)(2,1)S(1)}, u32[]{:S(2)}, u32[]{:S(2)}) async-start(bf16[8,192,256]{2,1,0:T(8,128)(2,1)} %fusion.1), calls=%async_computation.2 | async-start | bytes 1572864 | tf_op jit(solution)/shard_map/all_to_all | solution.py:158
  128.0 1.8 collective-permute-start.4
  129.8 2.6 %collective-permute-done.2 = bf16[192,256]{1,0:T(8,128)(2,1)S(1)} collective-permute-done((bf16[192,256]{1,0:T(8,128)(2,1)S(1)}, bf16[192,256]{1,0:T(8,128)(2,1)S(1)}, u32[]{:S(2)}, u32[]{:S(2)}) %collective-permute-start.2) | collective-permute-done | bytes 98336 | tf_op jit(solution)/shard_map/ppermute | solution.py:25
  135.3 1.8 collective-permute-start.5
  137.2 8.4 %all-to-all-done.1 = bf16[8,192,256]{2,1,0:T(8,128)(2,1)S(1)} async-done(((bf16[8,192,256]{2,1,0:T(8,128)(2,1)}), bf16[8,192,256]{2,1,0:T(8,128)(2,1)S(1)}, u32[]{:S(2)}, u32[]{:S(2)}) %all-to-all-start.1) | async-done | bytes 786464 | tf_op jit(solution)/shard_map/all_to_all | solution.py:158
  147.3 4.5 %collective-permute-start.19 = (bf16[384,256]{1,0:T(8,128)(2,1)S(1)}, bf16[384,256]{1,0:T(8,128)(2,1)S(1)}, u32[]{:S(2)}, u32[]{:S(2)}) collective-permute-start(bf16[384,256]{1,0:T(8,128)(2,1)S(1)} %get-tuple-element.2), channel_id=1, source_target_pairs={{0,192},{1,193},{2,194},{3,195},{4,196},{5,197},{6,198},{7,199},{8... | collective-permute-start | bytes 589832 | tf_op jit(solution)/shard_map/ppermute | solution.py:132
  152.6 2.4 %collective-permute-done.19 = bf16[384,256]{1,0:T(8,128)(2,1)S(1)} collective-permute-done((bf16[384,256]{1,0:T(8,128)(2,1)S(1)}, bf16[384,256]{1,0:T(8,128)(2,1)S(1)}, u32[]{:S(2)}, u32[]{:S(2)}) %collective-permute-start.19) | collective-permute-done | bytes 196640 | tf_op jit(solution)/shard_map/ppermute | solution.py:132
  155.9 7.5 %all-to-all-start.2 = ((f32[32,1,768]{2,1,0:T(1,128)}), f32[32,1,768]{2,1,0:T(1,128)S(1)}, u32[]{:S(2)}, u32[]{:S(2)}) async-start(f32[32,1,768]{2,1,0:T(1,128)} %broadcast_in_dim.9), calls=%async_computation.3 | async-start | bytes 196608 | tf_op jit(solution)/shard_map/all_to_all | solution.py:163
  164.1 9.4 %all-to-all-done.2 = f32[32,1,768]{2,1,0:T(1,128)S(1)} async-done(((f32[32,1,768]{2,1,0:T(1,128)}), f32[32,1,768]{2,1,0:T(1,128)S(1)}, u32[]{:S(2)}, u32[]{:S(2)}) %all-to-all-start.2) | async-done | bytes 98336 | tf_op jit(solution)/shard_map/all_to_all | solution.py:163
  (76 shorter events, 25.3 us)
Async XLA Ops:
  7.2 118.2 %reduce-scatter.2.cloned.1.call-start = ((), (), s32[]{:S(2)}) async-start(), calls=%async_computation.4 | async-start | bytes 7077888 | tf_op jit(solution)/shard_map/reduce_scatter | solution.py:116
  7.2 7.5 %collective-permute-start = (bf16[768,896]{1,0:T(8,128)(2,1)}, bf16[768,896]{1,0:T(8,128)(2,1)S(1)}, u32[]{:S(2)}, u32[]{:S(2)}) collective-permute-start(bf16[768,896]{1,0:T(8,128)(2,1)} %bitcast.80), channel_id=1, source_target_pairs={{0,32},{32,0},{1,33},{33,1},{2,34},{34,2},{3,35},{35,3},{4,36},{36... | collective-permute-start | bytes 4128776 | tf_op jit(solution)/shard_map/ppermute | solution.py:30
  9.1 5.0 %collective-permute-start.1 = (bf16[2,24,2048]{2,1,0:T(8,128)(2,1)S(1)}, bf16[2,24,2048]{2,1,0:T(8,128)(2,1)S(1)}, u32[]{:S(2)}, u32[]{:S(2)}) collective-permute-start(bf16[2,24,2048]{2,1,0:T(8,128)(2,1)S(1)} %pad_maximum_fusion.5), channel_id=1, source_target_pairs={{0,32},{32,0},{1,33},{33,1},{2,34},{34,2},{3,35},{35,3},{4,36},{36... | collective-permute-start | bytes 589832 | tf_op jit(solution)/shard_map/ppermute | solution.py:30
  11.9 18.9 %collective-permute-start.6 = (bf16[384,896]{1,0:T(8,128)(2,1)S(1)}, bf16[384,896]{1,0:T(8,128)(2,1)S(1)}, u32[]{:S(2)}, u32[]{:S(2)}) collective-permute-start(bf16[384,896]{1,0:T(8,128)(2,1)S(1)} %bitcast.83), channel_id=1, source_target_pairs={{0,64},{64,0},{1,65},{65,1},{2,66},{66,2},{3,67},{67,3},{4,68},{68... | collective-permute-start | bytes 2064392 | tf_op jit(solution)/shard_map/ppermute | solution.py:30
  14.8 1.1 copy-start.6
  31.7 0.9 copy-start.3
  31.7 0.9 copy-start.4
  31.7 11.1 %collective-permute-start.7 = (bf16[384,896]{1,0:T(8,128)(2,1)}, bf16[384,896]{1,0:T(8,128)(2,1)S(1)}, u32[]{:S(2)}, u32[]{:S(2)}) collective-permute-start(bf16[384,896]{1,0:T(8,128)(2,1)} %shard_map.60.h0_ref), channel_id=1, source_target_pairs={{0,32},{32,0},{1,33},{33,1},{2,34},{34,2},{3,35},{35,3},{4,36},{36... | collective-permute-start | bytes 2064392 | tf_op jit(solution)/shard_map/ppermute | solution.py:30
  32.6 9.4 %collective-permute-start.8 = (bf16[2,24,2048]{2,1,0:T(8,128)(2,1)S(1)}, bf16[2,24,2048]{2,1,0:T(8,128)(2,1)S(1)}, u32[]{:S(2)}, u32[]{:S(2)}) collective-permute-start(bf16[2,24,2048]{2,1,0:T(8,128)(2,1)S(1)} %pad_maximum_fusion.8), channel_id=1, source_target_pairs={{0,64},{64,0},{1,65},{65,1},{2,66},{66,2},{3,67},{67,3},{4,68},{68... | collective-permute-start | bytes 589832 | tf_op jit(solution)/shard_map/ppermute | solution.py:30
  34.9 21.3 %collective-permute-start.13 = (bf16[384,896]{1,0:T(8,128)(2,1)}, bf16[384,896]{1,0:T(8,128)(2,1)}, u32[]{:S(2)}, u32[]{:S(2)}) collective-permute-start(bf16[384,896]{1,0:T(8,128)(2,1)} %shard_map.62), channel_id=1, source_target_pairs={{0,64},{64,0},{1,65},{65,1},{2,66},{66,2},{3,67},{67,3},{4,68},{68... | collective-permute-start | bytes 2064392 | tf_op jit(solution)/shard_map/ppermute | solution.py:30
  53.3 9.0 %collective-permute-start.11 = (bf16[4,192,256]{2,1,0:T(8,128)(2,1)}, bf16[4,192,256]{2,1,0:T(8,128)(2,1)}, u32[]{:S(2)}, u32[]{:S(2)}) collective-permute-start(bf16[4,192,256]{2,1,0:T(8,128)(2,1)} %get-tuple-element.8), channel_id=1, source_target_pairs={{0,24},{8,0},{16,8},{24,16},{1,25},{9,1},{17,9},{25,17},{2,26},{10... | collective-permute-start | bytes 1179656 | tf_op jit(solution)/shard_map/ppermute | solution.py:25
  56.2 9.5 %copy-start = (bf16[4,8,192,256]{3,2,1,0:T(8,128)(2,1)S(1)}, bf16[4,8,192,256]{3,2,1,0:T(8,128)(2,1)}, u32[]{:S(2)}) copy-start(bf16[4,8,192,256]{3,2,1,0:T(8,128)(2,1)} %shard_map.61.refs_1_) | copy-start | bytes 9437188
  56.2 9.5 %collective-permute-start.9 = (bf16[4,192,256]{2,1,0:T(8,128)(2,1)}, bf16[4,192,256]{2,1,0:T(8,128)(2,1)}, u32[]{:S(2)}, u32[]{:S(2)}) collective-permute-start(bf16[4,192,256]{2,1,0:T(8,128)(2,1)} %get-tuple-element.6), channel_id=1, source_target_pairs={{0,8},{8,16},{16,24},{24,0},{1,9},{9,17},{17,25},{25,1},{2,10},{10... | collective-permute-start | bytes 1179656 | tf_op jit(solution)/shard_map/ppermute | solution.py:25
  56.2 10.7 %copy-start.2 = (bf16[4,192,256]{2,1,0:T(8,128)(2,1)S(1)}, bf16[4,192,256]{2,1,0:T(8,128)(2,1)}, u32[]{:S(2)}) copy-start(bf16[4,192,256]{2,1,0:T(8,128)(2,1)} %get-tuple-element.9) | copy-start | bytes 1179652
  56.2 15.9 %collective-permute-start.14 = (bf16[384,896]{1,0:T(8,128)(2,1)}, bf16[384,896]{1,0:T(8,128)(2,1)S(1)}, u32[]{:S(2)}, u32[]{:S(2)}) collective-permute-start(bf16[384,896]{1,0:T(8,128)(2,1)} %shard_map.63.h0_ref), channel_id=1, source_target_pairs={{0,32},{32,0},{1,33},{33,1},{2,34},{34,2},{3,35},{35,3},{4,36},{36... | collective-permute-start | bytes 2064392 | tf_op jit(solution)/shard_map/ppermute | solution.py:30
  67.9 19.6 %collective-permute-start.10 = (bf16[8,192,256]{2,1,0:T(8,128)(2,1)}, bf16[8,192,256]{2,1,0:T(8,128)(2,1)}, u32[]{:S(2)}, u32[]{:S(2)}) collective-permute-start(bf16[8,192,256]{2,1,0:T(8,128)(2,1)} %pad_maximum_fusion), channel_id=1, source_target_pairs={{0,8},{8,16},{16,24},{24,0},{1,9},{9,17},{17,25},{25,1},{2,10},{10... | collective-permute-start | bytes 2359304 | tf_op jit(solution)/shard_map/ppermute | solution.py:25
  68.9 19.9 %collective-permute-start.12 = (bf16[8,192,256]{2,1,0:T(8,128)(2,1)}, bf16[8,192,256]{2,1,0:T(8,128)(2,1)}, u32[]{:S(2)}, u32[]{:S(2)}) collective-permute-start(bf16[8,192,256]{2,1,0:T(8,128)(2,1)} %pad_maximum_fusion.1), channel_id=1, source_target_pairs={{0,24},{8,0},{16,8},{24,16},{1,25},{9,1},{17,9},{25,17},{2,26},{10... | collective-permute-start | bytes 2359304 | tf_op jit(solution)/shard_map/ppermute | solution.py:25
  82.6 17.1 %collective-permute-start.15 = (bf16[4,192,256]{2,1,0:T(8,128)(2,1)}, bf16[4,192,256]{2,1,0:T(8,128)(2,1)}, u32[]{:S(2)}, u32[]{:S(2)}) collective-permute-start(bf16[4,192,256]{2,1,0:T(8,128)(2,1)} %get-tuple-element.12), channel_id=1, source_target_pairs={{0,8},{8,16},{16,24},{24,0},{1,9},{9,17},{17,25},{25,1},{2,10},{10... | collective-permute-start | bytes 1179656 | tf_op jit(solution)/shard_map/ppermute | solution.py:25
  82.6 17.1 %collective-permute-start.17 = (bf16[4,192,256]{2,1,0:T(8,128)(2,1)}, bf16[4,192,256]{2,1,0:T(8,128)(2,1)}, u32[]{:S(2)}, u32[]{:S(2)}) collective-permute-start(bf16[4,192,256]{2,1,0:T(8,128)(2,1)} %get-tuple-element.14), channel_id=1, source_target_pairs={{0,24},{8,0},{16,8},{24,16},{1,25},{9,1},{17,9},{25,17},{2,26},{10... | collective-permute-start | bytes 1179656 | tf_op jit(solution)/shard_map/ppermute | solution.py:25
  91.4 30.4 %all-to-all-start = ((bf16[8,192,256]{2,1,0:T(8,128)(2,1)}), bf16[8,192,256]{2,1,0:T(8,128)(2,1)S(1)}, u32[]{:S(2)}, u32[]{:S(2)}) async-start(bf16[8,192,256]{2,1,0:T(8,128)(2,1)} %fusion.3), calls=%async_computation.1 | async-start | bytes 1572864 | tf_op jit(solution)/shard_map/all_to_all | solution.py:158
  99.7 1.5 copy-start.1
  101.3 13.8 %collective-permute-start.16 = (bf16[8,192,256]{2,1,0:T(8,128)(2,1)S(1)}, bf16[8,192,256]{2,1,0:T(8,128)(2,1)S(1)}, u32[]{:S(2)}, u32[]{:S(2)}) collective-permute-start(bf16[8,192,256]{2,1,0:T(8,128)(2,1)S(1)} %pad_maximum_fusion.2), channel_id=1, source_target_pairs={{0,8},{8,16},{16,24},{24,0},{1,9},{9,17},{17,25},{25,1},{2,10},{10... | collective-permute-start | bytes 2359304 | tf_op jit(solution)/shard_map/ppermute | solution.py:25
  101.5 13.6 %collective-permute-start.18 = (bf16[8,192,256]{2,1,0:T(8,128)(2,1)S(1)}, bf16[8,192,256]{2,1,0:T(8,128)(2,1)S(1)}, u32[]{:S(2)}, u32[]{:S(2)}) collective-permute-start(bf16[8,192,256]{2,1,0:T(8,128)(2,1)S(1)} %pad_maximum_fusion.3), channel_id=1, source_target_pairs={{0,24},{8,0},{16,8},{24,16},{1,25},{9,1},{17,9},{25,17},{2,26},{10... | collective-permute-start | bytes 2359304 | tf_op jit(solution)/shard_map/ppermute | solution.py:25
  121.8 23.8 %all-to-all-start.1 = ((bf16[8,192,256]{2,1,0:T(8,128)(2,1)}), bf16[8,192,256]{2,1,0:T(8,128)(2,1)S(1)}, u32[]{:S(2)}, u32[]{:S(2)}) async-start(bf16[8,192,256]{2,1,0:T(8,128)(2,1)} %fusion.1), calls=%async_computation.2 | async-start | bytes 1572864 | tf_op jit(solution)/shard_map/all_to_all | solution.py:158
  126.4 5.9 %collective-permute-start.2 = (bf16[192,256]{1,0:T(8,128)(2,1)S(1)}, bf16[192,256]{1,0:T(8,128)(2,1)S(1)}, u32[]{:S(2)}, u32[]{:S(2)}) collective-permute-start(bf16[192,256]{1,0:T(8,128)(2,1)S(1)} %get-tuple-element.20), channel_id=1, source_target_pairs={{0,8},{8,16},{16,24},{24,0},{1,9},{9,17},{17,25},{25,1},{2,10},{10... | collective-permute-start | bytes 294920 | tf_op jit(solution)/shard_map/ppermute | solution.py:25
  128.0 4.6 %collective-permute-start.4 = (bf16[192,256]{1,0:T(8,128)(2,1)S(1)}, bf16[192,256]{1,0:T(8,128)(2,1)S(1)}, u32[]{:S(2)}, u32[]{:S(2)}) collective-permute-start(bf16[192,256]{1,0:T(8,128)(2,1)S(1)} %get-tuple-element.22), channel_id=1, source_target_pairs={{0,24},{8,0},{16,8},{24,16},{1,25},{9,1},{17,9},{25,17},{2,26},{10... | collective-permute-start | bytes 294920 | tf_op jit(solution)/shard_map/ppermute | solution.py:25
  133.6 12.0 %collective-permute-start.3 = (bf16[384,256]{1,0:T(8,128)(2,1)S(1)}, bf16[384,256]{1,0:T(8,128)(2,1)S(1)}, u32[]{:S(2)}, u32[]{:S(2)}) collective-permute-start(bf16[384,256]{1,0:T(8,128)(2,1)S(1)} %pad_maximum_fusion.6), channel_id=1, source_target_pairs={{0,8},{8,16},{16,24},{24,0},{1,9},{9,17},{17,25},{25,1},{2,10},{10... | collective-permute-start | bytes 589832 | tf_op jit(solution)/shard_map/ppermute | solution.py:25
  135.3 10.4 %collective-permute-start.5 = (bf16[384,256]{1,0:T(8,128)(2,1)S(1)}, bf16[384,256]{1,0:T(8,128)(2,1)S(1)}, u32[]{:S(2)}, u32[]{:S(2)}) collective-permute-start(bf16[384,256]{1,0:T(8,128)(2,1)S(1)} %pad_maximum_fusion.7), channel_id=1, source_target_pairs={{0,24},{8,0},{16,8},{24,16},{1,25},{9,1},{17,9},{25,17},{2,26},{10... | collective-permute-start | bytes 589832 | tf_op jit(solution)/shard_map/ppermute | solution.py:25
  146.7 26.9 %copy-start.5 = (f32[1,256]{1,0:T(1,128)S(1)}, f32[1,256]{1,0:T(1,128)}, u32[]{:S(2)}) copy-start(f32[1,256]{1,0:T(1,128)} %param.7) | copy-start | bytes 3076
  146.8 5.8 %collective-permute-start.20 = (bf16[384,256]{1,0:T(8,128)(2,1)S(1)}, bf16[384,256]{1,0:T(8,128)(2,1)S(1)}, u32[]{:S(2)}, u32[]{:S(2)}) collective-permute-start(bf16[384,256]{1,0:T(8,128)(2,1)S(1)} %broadcast_select_fusion), channel_id=1, source_target_pairs={{0,128},{1,129},{2,130},{3,131},{4,132},{5,133},{6,134},{7,135},{8... | collective-permute-start | bytes 589832 | tf_op jit(solution)/shard_map/ppermute | solution.py:131
  147.3 7.6 %collective-permute-start.19 = (bf16[384,256]{1,0:T(8,128)(2,1)S(1)}, bf16[384,256]{1,0:T(8,128)(2,1)S(1)}, u32[]{:S(2)}, u32[]{:S(2)}) collective-permute-start(bf16[384,256]{1,0:T(8,128)(2,1)S(1)} %get-tuple-element.2), channel_id=1, source_target_pairs={{0,192},{1,193},{2,194},{3,195},{4,196},{5,197},{6,198},{7,199},{8... | collective-permute-start | bytes 589832 | tf_op jit(solution)/shard_map/ppermute | solution.py:132
  155.9 17.6 %all-to-all-start.2 = ((f32[32,1,768]{2,1,0:T(1,128)}), f32[32,1,768]{2,1,0:T(1,128)S(1)}, u32[]{:S(2)}, u32[]{:S(2)}) async-start(f32[32,1,768]{2,1,0:T(1,128)} %broadcast_in_dim.9), calls=%async_computation.3 | async-start | bytes 196608 | tf_op jit(solution)/shard_map/all_to_all | solution.py:163
  (3 other events, 2.6 us)
Sparse Core Ops, SparseCore 0:
  26.6 87.0 reduce-scatter.1

commit v4 on v3

--- a/solution.py
+++ b/solution.py
@@ -30,21 +30,32 @@
     return lax.ppermute(x, axes, [(i, n - 1 - i) for i in range(n)])
 
 
-def product_kernel(first, rows, y_major, m_ref, h0_ref, h1_ref, w_ref, r0_ref, r1_ref, *refs):
-    out_ref = refs[-1]
-
-    def block(i, half, k):
-        return (i * 2 + half, k) if y_major else (k, i * 2 + half)
-
+def product_kernel(first, rows, relative, m_ref, h0_ref, h1_ref, w_ref, r0_ref, r1_ref, *out_refs):
+    m = m_ref[0]
+    step = pl.program_id(0)
     parts = [slice(k * COLS, (k + 1) * COLS) for k in range(STEP)]
+
+    def at_owner(owner, k, use):
+        if not relative:
+            use(out_refs[0], (k, owner))
+            return
+        low_ref, high_ref, rest_ref = out_refs
+        ahead = lax.rem(owner - m // NZ + NY, NY)
+        pl.when(ahead != 2)(lambda: use(rest_ref, (jnp.where(ahead == 3, 2, ahead), k)))
+        early = step < NZ // STEP // 2
+        pl.when((ahead == 2) & early)(lambda: use(low_ref, (k,)))
+        pl.when((ahead == 2) & jnp.logical_not(early))(lambda: use(high_ref, (k,)))
+
     for i, h_ref in enumerate((h0_ref, h1_ref)):
+        acc = jnp.dot(h_ref[...], w_ref[...], preferred_element_type=F32).astype(BF16)
         for half in range(2):
-            at = half * rows
-            acc = jnp.dot(h_ref[at : at + rows], w_ref[...], preferred_element_type=F32)
             for k, part in enumerate(parts):
-                out_ref[block(i, half, k)] = acc[:, part].astype(BF16)
-
-    m = m_ref[0]
+
+                def store(ref, at, value=acc[half * rows : (half + 1) * rows, part]):
+                    ref[at] = value
+
+                at_owner(i * 2 + half, k, store)
+
     row = m % 16 * 24
 
     @pl.when((row >= first) & (row < first + rows))
@@ -55,20 +66,29 @@
             for k, part in enumerate(parts):
                 r = r_ref[:, part].astype(F32)
                 late, soon = jnp.concatenate([none, r]), jnp.concatenate([r, none])
-                at = block(i, m // 16, k) + (window, slice(None))
-                out_ref[at] = (out_ref[at].astype(F32) + jnp.where(row % 16 == 8, late, soon)).astype(BF16)
-
-
-def product(m, h, w, res, first, rows, y_major, scale=1, after=()):
+
+                def add(ref, at, value=jnp.where(row % 16 == 8, late, soon)):
+                    at = at + (window, slice(None))
+                    ref[at] = (ref[at].astype(F32) + value).astype(BF16)
+
+                at_owner(i * 2 + m // 16, k, add)
+
+
+def product(m, h, w, res, first, rows, relative, scale=1):
     whole = lambda j: (0, 0)
     columns = lambda j: (0, j)
-    if y_major:
-        shape, block, place = (NY, NZ, rows, COLS), (NY, STEP, rows, COLS), lambda j: (0, j, 0, 0)
+    if relative:
+        last = NZ // STEP // 2 - 1
+        out = [
+            ((NZ // 2, rows, COLS), (STEP, rows, COLS), lambda j: (jnp.minimum(j, last), 0, 0)),
+            ((NZ // 2, rows, COLS), (STEP, rows, COLS), lambda j: (jnp.maximum(j - last - 1, 0), 0, 0)),
+            ((3, NZ, rows, COLS), (3, STEP, rows, COLS), lambda j: (0, j, 0, 0)),
+        ]
     else:
-        shape, block, place = (NZ, NY, rows, COLS), (STEP, NY, rows, COLS), lambda j: (j, 0, 0, 0)
+        out = [((NZ, NY, rows, COLS), (STEP, NY, rows, COLS), lambda j: (j, 0, 0, 0))]
     return pl.pallas_call(
-        functools.partial(product_kernel, first, rows, y_major),
-        out_shape=jax.ShapeDtypeStruct(shape, BF16),
+        functools.partial(product_kernel, first, rows, relative),
+        out_shape=[jax.ShapeDtypeStruct(shape, BF16) for shape, _, _ in out],
         grid=(NZ // STEP,),
         in_specs=[
             pl.BlockSpec(memory_space=pltpu.SMEM),
@@ -77,16 +97,15 @@
             pl.BlockSpec((w.shape[0], STEP * COLS), columns),
             pl.BlockSpec((24, STEP * COLS), columns),
             pl.BlockSpec((24, STEP * COLS), columns),
-        ]
-        + [pl.BlockSpec(memory_space=pl.ANY)] * len(after),
-        out_specs=pl.BlockSpec(block, place),
+        ],
+        out_specs=[pl.BlockSpec(block, place) for _, block, place in out],
         compiler_params=pltpu.CompilerParams(vmem_limit_bytes=VMEM),
         cost_estimate=pl.CostEstimate(
             flops=scale * 2 * NY * rows * w.size,
             bytes_accessed=2 * (NY * rows * NZ * COLS + w.size + 2 * h[0].size),
             transcendentals=0,
         ),
-    )(m, h[0], h[1], w, res[0], res[1], *after)
+    )(m, h[0], h[1], w, res[0], res[1])
 
 
 def tied(x, *after, flops=0):
@@ -101,15 +120,13 @@
     )(x, *after)
 
 
-def summed_along_y(x, y):
-    half = x.shape[1] // 2
-    take = lambda j: lax.dynamic_index_in_dim(x, (y + j) % NY, axis=0, keepdims=False)
-    far, ahead, behind = take(2), take(1), take(-1)
-    up, down = shifted(far[:half], "y", NY, 1), shifted(far[half:], "y", NY, -1)
+def summed_along_y(low, high, own, ahead, behind):
+    half = low.shape[0]
+    up, down = shifted(low, "y", NY, 1), shifted(high, "y", NY, -1)
     ahead = jnp.concatenate([ahead[:half] + up, ahead[half:]])
     behind = jnp.concatenate([behind[:half], behind[half:] + down])
     up, down = shifted(ahead, "y", NY, 1), shifted(behind, "y", NY, -1)
-    return take(0).astype(F32) + up.astype(F32) + down.astype(F32)
+    return own.astype(F32) + up.astype(F32) + down.astype(F32)
 
 
 def summed_along_z(x):
@@ -145,25 +162,31 @@
     m = y * NZ + z
     m = m.reshape(1)
     core = flipped(h, "c")
-    product_near = product(m, (h, core), w, near_res, 0, HALF, False, SCALE)
+    (product_near,) = product(m, (h, core), w, near_res, 0, HALF, False, SCALE)
     far_res = flipped(far_res, "xh")
-    near = summed_along_y(summed_along_z(product_near), y).astype(BF16)
-    sums, last = [], product_near
+    near = summed_along_z(product_near)
+    take = lambda j: lax.dynamic_index_in_dim(near, (y + j) % NY, axis=0, keepdims=False)
+    opposite = take(2)
+    near = summed_along_y(opposite[: HALF // 2], opposite[HALF // 2 :], take(0), take(1), take(-1))
+    near = near.astype(BF16)
+    sums, last = [], (product_near, far_res)
     for a, b in ORDER:
         x = h.reshape(2, HALF, -1)[:, a:b].reshape(2 * (b - a), -1)
         x = flipped(tied(x, near_res[1]) if a else x, "xh")
-        x = tied(x, last, flops=0 if a else TIE)
-        x = last = product(m, (x, flipped(x, "c")), w, far_res, a, b - a, True, 1 if a else FAR)
-        x = summed_along_y(x, y).astype(BF16)
+        x = tied(x, *last, flops=0 if a else TIE)
+        low, high, rest = product(m, (x, flipped(x, "c")), w, far_res, a, b - a, True, 1 if a else FAR)
+        last = (rest,)
+        x = summed_along_y(low, high, *rest).astype(BF16)
         x = lax.all_to_all(x, "z", split_axis=0, concat_axis=0, tiled=True)
         sums.append(jnp.sum(x.astype(F32), axis=0).astype(BF16))
     handed = handed_over((near, jnp.concatenate(sums)), group, y)
     wide = handed.astype(F32)
     squares = jnp.sum(wide * wide, axis=1)
-    squares = lax.all_to_all(
-        jnp.broadcast_to(squares, (NY * NZ, 768)), ("y", "z"), split_axis=0, concat_axis=0, tiled=True
-    )
-    scale = lax.rsqrt(jnp.sum(squares, axis=0) / D + 1e-05)
+    for axis, n in (("z", NZ), ("y", NY)):
+        squares = jnp.broadcast_to(squares, (n, 768))
+        squares = lax.all_to_all(squares, axis, split_axis=0, concat_axis=0, tiled=True)
+        squares = jnp.sum(squares, axis=0)
+    scale = lax.rsqrt(squares / D + 1e-05)
     normed = (wide * scale[:, None] * gain[None, :]).astype(BF16)
     return (handed[None], normed[None])
 

time: 183 us -> 188 us (1.027)
  blocking collectives: 0 us -> 13.1 us
  starting transfers between devices: 50.9 us -> 44.4 us
  other arithmetic: 14.1 us -> 11.7 us
  Pallas kernels: 25.1 us -> 27.2 us
    all_to_all x0 -> x1, blocking collectives: none -> 13.1 us  [shards(): lax.all_to_all(squares, axis, split_axis=0, concat_axis=0, tiled=True)]
    all_to_all x1, waiting for transfers between devices: 9.37 us -> 4.53 us  [shards(): lax.all_to_all(squares, axis, split_axis=0, concat_axis=0, tiled=True)]
    all_to_all x1, starting transfers between devices: 7.48 us -> 3.25 us  [shards(): lax.all_to_all(squares, axis, split_axis=0, concat_axis=0, tiled=True)]
    slice x3, local copies, waits for them, and re-layouts: 5.95 us -> 2.31 us  [the longest x2 1.24 us: summed_along_y(): ahead = jnp.concatenate([ahead[:half] + up, ahead[half:]])]
    ppermute x1, starting transfers between devices: 4.45 us -> 1.62 us  [handed_over(): two = lax.ppermute(two, AXES, handing(1))]
    ppermute x12, waiting for transfers between devices: 25 us -> 27.4 us  [shifted(): return lax.ppermute(x, axis, [(i, (i + by) % n) for i in range(n)])]
    unnamed x20 -> x18, local copies, waits for them, and re-layouts: 4.59 us -> 6.84 us
    pallas_call x3, Pallas kernels: 25.1 us -> 27.2 us  [product(): pl.pallas_call(functools.partial(product_kernel, first, rows, relative),...]
  transfers between devices with their start and end apart: 25 -> 25, of which waited for: 14 -> 15; matrix products, arithmetic and copies ran while one was open for 13% -> 9% of each run, Pallas kernels for 14% -> 15%
where the time goes in v4:
time: 188 us; the launch traced here: 187 us
  waiting for transfers between devices  61.3 us (33%)
  starting transfers between devices  44.4 us (24%)
  Pallas kernels  27.2 us (14%)
  local copies, waits for them, and re-layouts  15.1 us (8%)
  between operations  14.4 us (8%)
  blocking collectives  13.1 us (7%)
  other arithmetic  11.7 us (6%)
    ppermute x12, waiting for transfers between devices, shifted(): return lax.ppermute(x, axis, [(i, (i + by) % n) for i in range(n)])  27.4 us
    pallas_call x3, Pallas kernels, product(): pl.pallas_call(functools.partial(product_kernel, first, rows, relative),...  27.2 us
    ppermute x12, starting transfers between devices, shifted(): return lax.ppermute(x, axis, [(i, (i + by) % n) for i in range(n)])  18.8 us
    all_to_all x2, waiting for transfers between devices, shards(): x = lax.all_to_all(x, 'z', split_axis=0, concat_axis=0, tiled=True)  14.2 us
    all_to_all x1, blocking collectives, shards(): lax.all_to_all(squares, axis, split_axis=0, concat_axis=0, tiled=True)  13.1 us
    all_to_all x2, starting transfers between devices, shards(): x = lax.all_to_all(x, 'z', split_axis=0, concat_axis=0, tiled=True)  12.5 us
    ppermute x7, waiting for transfers between devices, flipped(): return lax.ppermute(x, axes, [(i, n - 1 - i) for i in range(n)])  11.3 us
    unnamed x18, local copies, waits for them, and re-layouts  6.84 us
  transfers between devices with their start and end apart: 25, of which 15 were waited for; matrix products, arithmetic and copies ran while one was open for 9% of the time, Pallas kernels for 15%

profile of v4, /device:TPU:2, one launch (start us, length us, event | category | flops | bytes accessed | tf_op | source)
XLA Modules:
  0.0 187.2 jit_solution(16461469658496768156)
XLA Ops:
  7.3 1.7 constant_dynamic-slice_fusion
  9.6 2.3 %fusion.10 = (bf16[2,192,896]{2,1,0:T(8,128)(2,1)S(1)}, bf16[2,192,896]{2,1,0:T(8,128)(2,1)}) fusion(bf16[2,384,896]{2,1,0:T(8,128)(2,1)} %bitcast.65), kind=kLoop, calls=%fused_computation.50 | loop fusion | bytes 2752512 | tf_op jit(solution)/shard_map/slice | solution.py:174
  11.9 2.1 %collective-permute-start.6 = (bf16[384,896]{1,0:T(8,128)(2,1)S(1)}, bf16[384,896]{1,0:T(8,128)(2,1)S(1)}, u32[]{:S(2)}, u32[]{:S(2)}) collective-permute-start(bf16[384,896]{1,0:T(8,128)(2,1)S(1)} %bitcast.67), channel_id=1, source_target_pairs={{0,64},{64,0},{1,65},{65,1},{2,66},{66,2},{3,67},{67,3},{4,68},{68... | collective-permute-start | bytes 2064392 | tf_op jit(solution)/shard_map/ppermute | solution.py:30
  17.3 10.6 %shard_map.59.refs_1_ = bf16[8,4,384,256]{3,2,1,0:T(8,128)(2,1)} custom-call(s32[1]{0:T(128)} %bitcast.m_ref, bf16[768,896]{1,0:T(8,128)(2,1)} %bitcast.66, bf16[768,896]{1,0:T(8,128)(2,1)} %copy-done.5, bf16[896,2048]{1,0:T(8,128)(2,1)} %bitcast.69, bf16[24,2048]{1,0:T(8,128)(2,1)} %get-tuple-element.36.r0_ref, ...), custom_call_target="tpu_custom_call" | custom-call | flops 112742891520 | bytes 12713984 | tf_op jit(solution)/shard_map/pallas_call | solution.py:89
  27.9 7.1 %collective-permute-done.7.refs_2_ = bf16[2,24,2048]{2,1,0:T(8,128)(2,1)S(1)} collective-permute-done((bf16[2,24,2048]{2,1,0:T(8,128)(2,1)S(1)}, bf16[2,24,2048]{2,1,0:T(8,128)(2,1)S(1)}, u32[]{:S(2)}, u32[]{:S(2)}) %collective-permute-start.7) | collective-permute-done | bytes 196640 | tf_op jit(solution)/shard_map/ppermute | solution.py:30
  36.5 2.1 %collective-permute-start.13 = (bf16[384,896]{1,0:T(8,128)(2,1)}, bf16[384,896]{1,0:T(8,128)(2,1)S(1)}, u32[]{:S(2)}, u32[]{:S(2)}) collective-permute-start(bf16[384,896]{1,0:T(8,128)(2,1)} %shard_map.62), channel_id=1, source_target_pairs={{0,64},{64,0},{1,65},{65,1},{2,66},{66,2},{3,67},{67,3},{4,68},{68... | collective-permute-start | bytes 2064392 | tf_op jit(solution)/shard_map/ppermute | solution.py:30
  40.2 8.4 %shard_map.61 = (bf16[4,192,256]{2,1,0:T(8,128)(2,1)}, bf16[4,192,256]{2,1,0:T(8,128)(2,1)}, bf16[3,8,192,256]{3,2,1,0:T(8,128)(2,1)}) custom-call(s32[1]{0:T(128)} %bitcast.m_ref, bf16[384,896]{1,0:T(8,128)(2,1)} %shard_map.60.h0_ref, bf16[384,896]{1,0:T(8,128)(2,1)} %copy-done.8, bf16[896,2048]{1,0:T(8,128)(2,1)} %bitcast.70, ...), custom_call_target="tpu_custom_call" | custom-call | flops 2818572288 | bytes 8192000 | tf_op jit(solution)/shard_map/pallas_call | solution.py:89
  49.9 1.9 %collective-permute-start.11 = (bf16[4,192,256]{2,1,0:T(8,128)(2,1)}, bf16[4,192,256]{2,1,0:T(8,128)(2,1)}, u32[]{:S(2)}, u32[]{:S(2)}) collective-permute-start(bf16[4,192,256]{2,1,0:T(8,128)(2,1)} %get-tuple-element.10), channel_id=1, source_target_pairs={{0,24},{8,0},{16,8},{24,16},{1,25},{9,1},{17,9},{25,17},{2,26},{10... | collective-permute-start | bytes 1179656 | tf_op jit(solution)/shard_map/ppermute | solution.py:25
  51.8 4.2 %collective-permute-done.13.refs_0_ = bf16[384,896]{1,0:T(8,128)(2,1)S(1)} collective-permute-done((bf16[384,896]{1,0:T(8,128)(2,1)}, bf16[384,896]{1,0:T(8,128)(2,1)S(1)}, u32[]{:S(2)}, u32[]{:S(2)}) %collective-permute-start.13) | collective-permute-done | bytes 688160 | tf_op jit(solution)/shard_map/ppermute | solution.py:30
  56.9 1.7 copy-done
  58.7 2.6 %collective-permute-done.9 = bf16[4,192,256]{2,1,0:T(8,128)(2,1)S(1)} collective-permute-done((bf16[4,192,256]{2,1,0:T(8,128)(2,1)}, bf16[4,192,256]{2,1,0:T(8,128)(2,1)S(1)}, u32[]{:S(2)}, u32[]{:S(2)}) %collective-permute-start.9) | collective-permute-done | bytes 393248 | tf_op jit(solution)/shard_map/ppermute | solution.py:25
  62.5 3.1 %collective-permute-start.12 = (bf16[8,192,256]{2,1,0:T(8,128)(2,1)S(1)}, bf16[8,192,256]{2,1,0:T(8,128)(2,1)}, u32[]{:S(2)}, u32[]{:S(2)}) collective-permute-start(bf16[8,192,256]{2,1,0:T(8,128)(2,1)S(1)} %pad_maximum_fusion.1), channel_id=1, source_target_pairs={{0,24},{8,0},{16,8},{24,16},{1,25},{9,1},{17,9},{25,17},{2,26},{10... | collective-permute-start | bytes 2359304 | tf_op jit(solution)/shard_map/ppermute | solution.py:25
  66.6 8.1 %shard_map.64 = (bf16[4,192,256]{2,1,0:T(8,128)(2,1)}, bf16[4,192,256]{2,1,0:T(8,128)(2,1)}, bf16[3,8,192,256]{3,2,1,0:T(8,128)(2,1)}) custom-call(s32[1]{0:T(128)} %bitcast.m_ref, bf16[384,896]{1,0:T(8,128)(2,1)} %shard_map.63.h0_ref, bf16[384,896]{1,0:T(8,128)(2,1)} %copy-done.7, bf16[896,2048]{1,0:T(8,128)(2,1)} %bitcast.71, ...), custom_call_target="tpu_custom_call" | custom-call | flops 2818572288 | bytes 8192000 | tf_op jit(solution)/shard_map/pallas_call | solution.py:89
  75.9 2.7 %collective-permute-start.17 = (bf16[4,192,256]{2,1,0:T(8,128)(2,1)}, bf16[4,192,256]{2,1,0:T(8,128)(2,1)}, u32[]{:S(2)}, u32[]{:S(2)}) collective-permute-start(bf16[4,192,256]{2,1,0:T(8,128)(2,1)} %get-tuple-element.13), channel_id=1, source_target_pairs={{0,24},{8,0},{16,8},{24,16},{1,25},{9,1},{17,9},{25,17},{2,26},{10... | collective-permute-start | bytes 1179656 | tf_op jit(solution)/shard_map/ppermute | solution.py:25
  79.8 3.8 %collective-permute-done.12 = bf16[8,192,256]{2,1,0:T(8,128)(2,1)} collective-permute-done((bf16[8,192,256]{2,1,0:T(8,128)(2,1)S(1)}, bf16[8,192,256]{2,1,0:T(8,128)(2,1)}, u32[]{:S(2)}, u32[]{:S(2)}) %collective-permute-start.12) | collective-permute-done | bytes 786464 | tf_op jit(solution)/shard_map/ppermute | solution.py:25
  83.6 3.8 %collective-permute-done.10 = bf16[8,192,256]{2,1,0:T(8,128)(2,1)S(1)} collective-permute-done((bf16[8,192,256]{2,1,0:T(8,128)(2,1)S(1)}, bf16[8,192,256]{2,1,0:T(8,128)(2,1)S(1)}, u32[]{:S(2)}, u32[]{:S(2)}) %collective-permute-start.10) | collective-permute-done | bytes 786464 | tf_op jit(solution)/shard_map/ppermute | solution.py:25
  87.4 2.3 %fusion.3 = bf16[8,192,256]{2,1,0:T(8,128)(2,1)} fusion(bf16[8,192,256]{2,1,0:T(8,128)(2,1)} %collective-permute-done.12, bf16[8,192,256]{2,1,0:T(8,128)(2,1)S(1)} %collective-permute-done.10, bf16[3,8,192,256]{3,2,1,0:T(8,128)(2,1)S(1)} %copy-done), kind=kLoop, calls=%fused_computation.5 | loop fusion | flops 2359296 | bytes 3145728 | tf_op jit(solution)/shard_map/convert_element_type | solution.py:179
  89.7 9.0 %all-to-all-start = ((bf16[8,192,256]{2,1,0:T(8,128)(2,1)}), bf16[8,192,256]{2,1,0:T(8,128)(2,1)S(1)}, u32[]{:S(2)}, u32[]{:S(2)}) async-start(bf16[8,192,256]{2,1,0:T(8,128)(2,1)} %fusion.3), calls=%async_computation.1 | async-start | bytes 1572864 | tf_op jit(solution)/shard_map/all_to_all | solution.py:180
  100.3 2.1 %collective-permute-start.16 = (bf16[8,192,256]{2,1,0:T(8,128)(2,1)S(1)}, bf16[8,192,256]{2,1,0:T(8,128)(2,1)S(1)}, u32[]{:S(2)}, u32[]{:S(2)}) collective-permute-start(bf16[8,192,256]{2,1,0:T(8,128)(2,1)S(1)} %pad_maximum_fusion.2), channel_id=1, source_target_pairs={{0,8},{8,16},{16,24},{24,0},{1,9},{9,17},{17,25},{25,1},{2,10},{10... | collective-permute-start | bytes 2359304 | tf_op jit(solution)/shard_map/ppermute | solution.py:25
  102.4 12.7 %collective-permute-done.18 = bf16[8,192,256]{2,1,0:T(8,128)(2,1)S(1)} collective-permute-done((bf16[8,192,256]{2,1,0:T(8,128)(2,1)S(1)}, bf16[8,192,256]{2,1,0:T(8,128)(2,1)S(1)}, u32[]{:S(2)}, u32[]{:S(2)}) %collective-permute-start.18) | collective-permute-done | bytes 786464 | tf_op jit(solution)/shard_map/ppermute | solution.py:25
  116.6 2.4 %fusion.1 = bf16[8,192,256]{2,1,0:T(8,128)(2,1)} fusion(bf16[8,192,256]{2,1,0:T(8,128)(2,1)S(1)} %collective-permute-done.18, bf16[8,192,256]{2,1,0:T(8,128)(2,1)S(1)} %collective-permute-done.16, bf16[3,8,192,256]{3,2,1,0:T(8,128)(2,1)} %get-tuple-element.11), kind=kLoop, calls=%fused_computation.2 | loop fusion | flops 2359296 | bytes 3145728 | tf_op jit(solution)/shard_map/convert_element_type | solution.py:179
  118.9 5.2 %all-to-all-done = bf16[8,192,256]{2,1,0:T(8,128)(2,1)S(1)} async-done(((bf16[8,192,256]{2,1,0:T(8,128)(2,1)}), bf16[8,192,256]{2,1,0:T(8,128)(2,1)S(1)}, u32[]{:S(2)}, u32[]{:S(2)}) %all-to-all-start) | async-done | bytes 786464 | tf_op jit(solution)/shard_map/all_to_all | solution.py:180
  124.2 3.5 %all-to-all-start.1 = ((bf16[8,192,256]{2,1,0:T(8,128)(2,1)}), bf16[8,192,256]{2,1,0:T(8,128)(2,1)S(1)}, u32[]{:S(2)}, u32[]{:S(2)}) async-start(bf16[8,192,256]{2,1,0:T(8,128)(2,1)} %fusion.1), calls=%async_computation.2 | async-start | bytes 1572864 | tf_op jit(solution)/shard_map/all_to_all | solution.py:180
  130.4 1.8 collective-permute-start.4
  132.2 2.6 %collective-permute-done.2 = bf16[192,256]{1,0:T(8,128)(2,1)S(1)} collective-permute-done((bf16[192,256]{1,0:T(8,128)(2,1)S(1)}, bf16[192,256]{1,0:T(8,128)(2,1)S(1)}, u32[]{:S(2)}, u32[]{:S(2)}) %collective-permute-start.2) | collective-permute-done | bytes 98336 | tf_op jit(solution)/shard_map/ppermute | solution.py:25
  136.1 3.0 %collective-permute-start.5 = (bf16[384,256]{1,0:T(8,128)(2,1)S(1)}, bf16[384,256]{1,0:T(8,128)(2,1)S(1)}, u32[]{:S(2)}, u32[]{:S(2)}) collective-permute-start(bf16[384,256]{1,0:T(8,128)(2,1)S(1)} %pad_maximum_fusion.7), channel_id=1, source_target_pairs={{0,24},{8,0},{16,8},{24,16},{1,25},{9,1},{17,9},{25,17},{2,26},{10... | collective-permute-start | bytes 589832 | tf_op jit(solution)/shard_map/ppermute | solution.py:25
  139.4 9.0 %all-to-all-done.1 = bf16[8,192,256]{2,1,0:T(8,128)(2,1)S(1)} async-done(((bf16[8,192,256]{2,1,0:T(8,128)(2,1)}), bf16[8,192,256]{2,1,0:T(8,128)(2,1)S(1)}, u32[]{:S(2)}, u32[]{:S(2)}) %all-to-all-start.1) | async-done | bytes 786464 | tf_op jit(solution)/shard_map/all_to_all | solution.py:180
  151.2 1.8 collective-permute-start.20
  153.0 3.3 %collective-permute-done.19 = bf16[384,256]{1,0:T(8,128)(2,1)S(1)} collective-permute-done((bf16[384,256]{1,0:T(8,128)(2,1)S(1)}, bf16[384,256]{1,0:T(8,128)(2,1)S(1)}, u32[]{:S(2)}, u32[]{:S(2)}) %collective-permute-start.19) | collective-permute-done | bytes 196640 | tf_op jit(solution)/shard_map/ppermute | solution.py:149
  157.1 13.1 %all_to_all.22 = f32[8,1,768]{2,1,0:T(1,128)S(1)} all-to-all(f32[8,1,768]{2,1,0:T(1,128)S(1)} %broadcast_in_dim.12), channel_id=1, replica_groups=mesh['s'=2,'xh'=2,'c'=2,'y'=4,'z'=8] {'z'}, dimensions={0} | all-to-all | bytes 49152 | tf_op jit(solution)/shard_map/all_to_all | solution.py:187
  170.9 3.3 %all-to-all-start.3 = ((f32[4,1,768]{2,1,0:T(1,128)}), f32[4,1,768]{2,1,0:T(1,128)S(1)}, u32[]{:S(2)}, u32[]{:S(2)}) async-start(f32[4,1,768]{2,1,0:T(1,128)} %broadcast_in_dim.13), calls=%async_computation.4 | async-start | bytes 24576 | tf_op jit(solution)/shard_map/all_to_all | solution.py:187
  174.9 4.5 %all-to-all-done.3 = f32[4,1,768]{2,1,0:T(1,128)S(1)} async-done(((f32[4,1,768]{2,1,0:T(1,128)}), f32[4,1,768]{2,1,0:T(1,128)S(1)}, u32[]{:S(2)}, u32[]{:S(2)}) %all-to-all-start.3) | async-done | bytes 12320 | tf_op jit(solution)/shard_map/all_to_all | solution.py:187
  (77 shorter events, 27.0 us)
Async XLA Ops:
  7.2 120.6 %reduce-scatter.2.cloned.1.call-start = ((), (), s32[]{:S(2)}) async-start(), calls=%async_computation.5 | async-start | bytes 7077888 | tf_op jit(solution)/shard_map/reduce_scatter | solution.py:133
  7.2 9.0 %collective-permute-start = (bf16[768,896]{1,0:T(8,128)(2,1)}, bf16[768,896]{1,0:T(8,128)(2,1)S(1)}, u32[]{:S(2)}, u32[]{:S(2)}) collective-permute-start(bf16[768,896]{1,0:T(8,128)(2,1)} %bitcast.64), channel_id=1, source_target_pairs={{0,32},{32,0},{1,33},{33,1},{2,34},{34,2},{3,35},{35,3},{4,36},{36... | collective-permute-start | bytes 4128776 | tf_op jit(solution)/shard_map/ppermute | solution.py:30
  9.1 4.9 %collective-permute-start.1 = (bf16[2,24,2048]{2,1,0:T(8,128)(2,1)S(1)}, bf16[2,24,2048]{2,1,0:T(8,128)(2,1)S(1)}, u32[]{:S(2)}, u32[]{:S(2)}) collective-permute-start(bf16[2,24,2048]{2,1,0:T(8,128)(2,1)S(1)} %pad_maximum_fusion.5), channel_id=1, source_target_pairs={{0,32},{32,0},{1,33},{33,1},{2,34},{34,2},{3,35},{35,3},{4,36},{36... | collective-permute-start | bytes 589832 | tf_op jit(solution)/shard_map/ppermute | solution.py:30
  11.9 23.1 %collective-permute-start.6 = (bf16[384,896]{1,0:T(8,128)(2,1)S(1)}, bf16[384,896]{1,0:T(8,128)(2,1)S(1)}, u32[]{:S(2)}, u32[]{:S(2)}) collective-permute-start(bf16[384,896]{1,0:T(8,128)(2,1)S(1)} %bitcast.67), channel_id=1, source_target_pairs={{0,64},{64,0},{1,65},{65,1},{2,66},{66,2},{3,67},{67,3},{4,68},{68... | collective-permute-start | bytes 2064392 | tf_op jit(solution)/shard_map/ppermute | solution.py:30
  14.7 20.3 %collective-permute-start.7 = (bf16[2,24,2048]{2,1,0:T(8,128)(2,1)S(1)}, bf16[2,24,2048]{2,1,0:T(8,128)(2,1)S(1)}, u32[]{:S(2)}, u32[]{:S(2)}) collective-permute-start(bf16[2,24,2048]{2,1,0:T(8,128)(2,1)S(1)} %pad_maximum_fusion.8), channel_id=1, source_target_pairs={{0,64},{64,0},{1,65},{65,1},{2,66},{66,2},{3,67},{67,3},{4,68},{68... | collective-permute-start | bytes 589832 | tf_op jit(solution)/shard_map/ppermute | solution.py:30
  16.2 1.1 copy-start.5
  36.5 2.1 %copy-start.3 = (bf16[2,24,2048]{2,1,0:T(8,128)(2,1)S(1)}, bf16[2,24,2048]{2,1,0:T(8,128)(2,1)}, u32[]{:S(2)}) copy-start(bf16[2,24,2048]{2,1,0:T(8,128)(2,1)} %copy-done.2) | copy-start | bytes 589828
  36.5 2.8 %collective-permute-start.8 = (bf16[384,896]{1,0:T(8,128)(2,1)}, bf16[384,896]{1,0:T(8,128)(2,1)S(1)}, u32[]{:S(2)}, u32[]{:S(2)}) collective-permute-start(bf16[384,896]{1,0:T(8,128)(2,1)} %shard_map.60.h0_ref), channel_id=1, source_target_pairs={{0,32},{32,0},{1,33},{33,1},{2,34},{34,2},{3,35},{35,3},{4,36},{36... | collective-permute-start | bytes 2064392 | tf_op jit(solution)/shard_map/ppermute | solution.py:30
  36.5 19.6 %collective-permute-start.13 = (bf16[384,896]{1,0:T(8,128)(2,1)}, bf16[384,896]{1,0:T(8,128)(2,1)S(1)}, u32[]{:S(2)}, u32[]{:S(2)}) collective-permute-start(bf16[384,896]{1,0:T(8,128)(2,1)} %shard_map.62), channel_id=1, source_target_pairs={{0,64},{64,0},{1,65},{65,1},{2,66},{66,2},{3,67},{67,3},{4,68},{68... | collective-permute-start | bytes 2064392 | tf_op jit(solution)/shard_map/ppermute | solution.py:30
  39.3 0.8 copy-start.8
  48.6 12.7 %collective-permute-start.9 = (bf16[4,192,256]{2,1,0:T(8,128)(2,1)}, bf16[4,192,256]{2,1,0:T(8,128)(2,1)S(1)}, u32[]{:S(2)}, u32[]{:S(2)}) collective-permute-start(bf16[4,192,256]{2,1,0:T(8,128)(2,1)} %get-tuple-element.9), channel_id=1, source_target_pairs={{0,8},{8,16},{16,24},{24,0},{1,9},{9,17},{17,25},{25,1},{2,10},{10... | collective-permute-start | bytes 1179656 | tf_op jit(solution)/shard_map/ppermute | solution.py:25
  49.9 11.4 %collective-permute-start.11 = (bf16[4,192,256]{2,1,0:T(8,128)(2,1)}, bf16[4,192,256]{2,1,0:T(8,128)(2,1)}, u32[]{:S(2)}, u32[]{:S(2)}) collective-permute-start(bf16[4,192,256]{2,1,0:T(8,128)(2,1)} %get-tuple-element.10), channel_id=1, source_target_pairs={{0,24},{8,0},{16,8},{24,16},{1,25},{9,1},{17,9},{25,17},{2,26},{10... | collective-permute-start | bytes 1179656 | tf_op jit(solution)/shard_map/ppermute | solution.py:25
  56.1 0.8 copy-start.1
  56.9 1.7 copy-start
  56.9 8.8 %collective-permute-start.14 = (bf16[384,896]{1,0:T(8,128)(2,1)}, bf16[384,896]{1,0:T(8,128)(2,1)S(1)}, u32[]{:S(2)}, u32[]{:S(2)}) collective-permute-start(bf16[384,896]{1,0:T(8,128)(2,1)} %shard_map.63.h0_ref), channel_id=1, source_target_pairs={{0,32},{32,0},{1,33},{33,1},{2,34},{34,2},{3,35},{35,3},{4,36},{36... | collective-permute-start | bytes 2064392 | tf_op jit(solution)/shard_map/ppermute | solution.py:30
  62.5 21.1 %collective-permute-start.12 = (bf16[8,192,256]{2,1,0:T(8,128)(2,1)S(1)}, bf16[8,192,256]{2,1,0:T(8,128)(2,1)}, u32[]{:S(2)}, u32[]{:S(2)}) collective-permute-start(bf16[8,192,256]{2,1,0:T(8,128)(2,1)S(1)} %pad_maximum_fusion.1), channel_id=1, source_target_pairs={{0,24},{8,0},{16,8},{24,16},{1,25},{9,1},{17,9},{25,17},{2,26},{10... | collective-permute-start | bytes 2359304 | tf_op jit(solution)/shard_map/ppermute | solution.py:25
  65.7 21.8 %collective-permute-start.10 = (bf16[8,192,256]{2,1,0:T(8,128)(2,1)S(1)}, bf16[8,192,256]{2,1,0:T(8,128)(2,1)S(1)}, u32[]{:S(2)}, u32[]{:S(2)}) collective-permute-start(bf16[8,192,256]{2,1,0:T(8,128)(2,1)S(1)} %pad_maximum_fusion), channel_id=1, source_target_pairs={{0,8},{8,16},{16,24},{24,0},{1,9},{9,17},{17,25},{25,1},{2,10},{10... | collective-permute-start | bytes 2359304 | tf_op jit(solution)/shard_map/ppermute | solution.py:25
  65.8 0.9 copy-start.7
  74.8 23.9 %collective-permute-start.15 = (bf16[4,192,256]{2,1,0:T(8,128)(2,1)}, bf16[4,192,256]{2,1,0:T(8,128)(2,1)S(1)}, u32[]{:S(2)}, u32[]{:S(2)}) collective-permute-start(bf16[4,192,256]{2,1,0:T(8,128)(2,1)} %get-tuple-element.12), channel_id=1, source_target_pairs={{0,8},{8,16},{16,24},{24,0},{1,9},{9,17},{17,25},{25,1},{2,10},{10... | collective-permute-start | bytes 1179656 | tf_op jit(solution)/shard_map/ppermute | solution.py:25
  75.9 22.8 %collective-permute-start.17 = (bf16[4,192,256]{2,1,0:T(8,128)(2,1)}, bf16[4,192,256]{2,1,0:T(8,128)(2,1)}, u32[]{:S(2)}, u32[]{:S(2)}) collective-permute-start(bf16[4,192,256]{2,1,0:T(8,128)(2,1)} %get-tuple-element.13), channel_id=1, source_target_pairs={{0,24},{8,0},{16,8},{24,16},{1,25},{9,1},{17,9},{25,17},{2,26},{10... | collective-permute-start | bytes 1179656 | tf_op jit(solution)/shard_map/ppermute | solution.py:25
  89.7 34.4 %all-to-all-start = ((bf16[8,192,256]{2,1,0:T(8,128)(2,1)}), bf16[8,192,256]{2,1,0:T(8,128)(2,1)S(1)}, u32[]{:S(2)}, u32[]{:S(2)}) async-start(bf16[8,192,256]{2,1,0:T(8,128)(2,1)} %fusion.3), calls=%async_computation.1 | async-start | bytes 1572864 | tf_op jit(solution)/shard_map/all_to_all | solution.py:180
  100.1 14.9 %collective-permute-start.18 = (bf16[8,192,256]{2,1,0:T(8,128)(2,1)S(1)}, bf16[8,192,256]{2,1,0:T(8,128)(2,1)S(1)}, u32[]{:S(2)}, u32[]{:S(2)}) collective-permute-start(bf16[8,192,256]{2,1,0:T(8,128)(2,1)S(1)} %pad_maximum_fusion.3), channel_id=1, source_target_pairs={{0,24},{8,0},{16,8},{24,16},{1,25},{9,1},{17,9},{25,17},{2,26},{10... | collective-permute-start | bytes 2359304 | tf_op jit(solution)/shard_map/ppermute | solution.py:25
  100.3 16.3 %collective-permute-start.16 = (bf16[8,192,256]{2,1,0:T(8,128)(2,1)S(1)}, bf16[8,192,256]{2,1,0:T(8,128)(2,1)S(1)}, u32[]{:S(2)}, u32[]{:S(2)}) collective-permute-start(bf16[8,192,256]{2,1,0:T(8,128)(2,1)S(1)} %pad_maximum_fusion.2), channel_id=1, source_target_pairs={{0,8},{8,16},{16,24},{24,0},{1,9},{9,17},{17,25},{25,1},{2,10},{10... | collective-permute-start | bytes 2359304 | tf_op jit(solution)/shard_map/ppermute | solution.py:25
  124.2 24.2 %all-to-all-start.1 = ((bf16[8,192,256]{2,1,0:T(8,128)(2,1)}), bf16[8,192,256]{2,1,0:T(8,128)(2,1)S(1)}, u32[]{:S(2)}, u32[]{:S(2)}) async-start(bf16[8,192,256]{2,1,0:T(8,128)(2,1)} %fusion.1), calls=%async_computation.2 | async-start | bytes 1572864 | tf_op jit(solution)/shard_map/all_to_all | solution.py:180
  128.9 5.9 %collective-permute-start.2 = (bf16[192,256]{1,0:T(8,128)(2,1)S(1)}, bf16[192,256]{1,0:T(8,128)(2,1)S(1)}, u32[]{:S(2)}, u32[]{:S(2)}) collective-permute-start(bf16[192,256]{1,0:T(8,128)(2,1)S(1)} %get-tuple-element.28), channel_id=1, source_target_pairs={{0,8},{8,16},{16,24},{24,0},{1,9},{9,17},{17,25},{25,1},{2,10},{10... | collective-permute-start | bytes 294920 | tf_op jit(solution)/shard_map/ppermute | solution.py:25
  130.4 4.6 %collective-permute-start.4 = (bf16[192,256]{1,0:T(8,128)(2,1)S(1)}, bf16[192,256]{1,0:T(8,128)(2,1)S(1)}, u32[]{:S(2)}, u32[]{:S(2)}) collective-permute-start(bf16[192,256]{1,0:T(8,128)(2,1)S(1)} %get-tuple-element.30), channel_id=1, source_target_pairs={{0,24},{8,0},{16,8},{24,16},{1,25},{9,1},{17,9},{25,17},{2,26},{10... | collective-permute-start | bytes 294920 | tf_op jit(solution)/shard_map/ppermute | solution.py:25
  136.1 12.4 %collective-permute-start.5 = (bf16[384,256]{1,0:T(8,128)(2,1)S(1)}, bf16[384,256]{1,0:T(8,128)(2,1)S(1)}, u32[]{:S(2)}, u32[]{:S(2)}) collective-permute-start(bf16[384,256]{1,0:T(8,128)(2,1)S(1)} %pad_maximum_fusion.7), channel_id=1, source_target_pairs={{0,24},{8,0},{16,8},{24,16},{1,25},{9,1},{17,9},{25,17},{2,26},{10... | collective-permute-start | bytes 589832 | tf_op jit(solution)/shard_map/ppermute | solution.py:25
  139.1 9.3 %collective-permute-start.3 = (bf16[384,256]{1,0:T(8,128)(2,1)S(1)}, bf16[384,256]{1,0:T(8,128)(2,1)S(1)}, u32[]{:S(2)}, u32[]{:S(2)}) collective-permute-start(bf16[384,256]{1,0:T(8,128)(2,1)S(1)} %pad_maximum_fusion.6), channel_id=1, source_target_pairs={{0,8},{8,16},{16,24},{24,0},{1,9},{9,17},{17,25},{25,1},{2,10},{10... | collective-permute-start | bytes 589832 | tf_op jit(solution)/shard_map/ppermute | solution.py:25
  149.5 30.0 %copy-start.4 = (f32[1,256]{1,0:T(1,128)S(1)}, f32[1,256]{1,0:T(1,128)}, u32[]{:S(2)}) copy-start(f32[1,256]{1,0:T(1,128)} %param.7) | copy-start | bytes 3076
  149.6 6.7 %collective-permute-start.19 = (bf16[384,256]{1,0:T(8,128)(2,1)S(1)}, bf16[384,256]{1,0:T(8,128)(2,1)S(1)}, u32[]{:S(2)}, u32[]{:S(2)}) collective-permute-start(bf16[384,256]{1,0:T(8,128)(2,1)S(1)} %get-tuple-element.14), channel_id=1, source_target_pairs={{0,192},{1,193},{2,194},{3,195},{4,196},{5,197},{6,198},{7,199},{8... | collective-permute-start | bytes 589832 | tf_op jit(solution)/shard_map/ppermute | solution.py:149
  151.2 5.7 %collective-permute-start.20 = (bf16[384,256]{1,0:T(8,128)(2,1)S(1)}, bf16[384,256]{1,0:T(8,128)(2,1)S(1)}, u32[]{:S(2)}, u32[]{:S(2)}) collective-permute-start(bf16[384,256]{1,0:T(8,128)(2,1)S(1)} %broadcast_select_fusion), channel_id=1, source_target_pairs={{0,128},{1,129},{2,130},{3,131},{4,132},{5,133},{6,134},{7,135},{8... | collective-permute-start | bytes 589832 | tf_op jit(solution)/shard_map/ppermute | solution.py:148
  170.9 8.6 %all-to-all-start.3 = ((f32[4,1,768]{2,1,0:T(1,128)}), f32[4,1,768]{2,1,0:T(1,128)S(1)}, u32[]{:S(2)}, u32[]{:S(2)}) async-start(f32[4,1,768]{2,1,0:T(1,128)} %broadcast_in_dim.13), calls=%async_computation.4 | async-start | bytes 24576 | tf_op jit(solution)/shard_map/all_to_all | solution.py:187
  (2 other events, 1.5 us)
Sparse Core Ops, SparseCore 0:
  28.0 89.4 reduce-scatter.1

commit v5 on v4

--- a/solution.py
+++ b/solution.py
@@ -14,9 +14,10 @@
 STEP = 2
 HALF = 384
 ORDER = ((0, 192), (192, HALF))
+HOLD = 4 * 10**10
 TIE = 3 * 10**11
 SCALE, FAR = 20, 1
-VMEM = 58 * 2**20
+VMEM = 50 * 2**20
 AXES = ("s", "xh", "c", "y", "z")
 F32, BF16 = jnp.float32, jnp.bfloat16
 
@@ -120,13 +121,19 @@
     )(x, *after)
 
 
-def summed_along_y(low, high, own, ahead, behind):
+def first_step(low, high, ahead, behind):
     half = low.shape[0]
     up, down = shifted(low, "y", NY, 1), shifted(high, "y", NY, -1)
     ahead = jnp.concatenate([ahead[:half] + up, ahead[half:]])
-    behind = jnp.concatenate([behind[:half], behind[half:] + down])
-    up, down = shifted(ahead, "y", NY, 1), shifted(behind, "y", NY, -1)
-    return own.astype(F32) + up.astype(F32) + down.astype(F32)
+    return ahead, jnp.concatenate([behind[:half], behind[half:] + down])
+
+
+def second_step(ahead, behind):
+    return shifted(ahead, "y", NY, 1), shifted(behind, "y", NY, -1)
+
+
+def added(own, up, down):
+    return (own.astype(F32) + up.astype(F32) + down.astype(F32)).astype(BF16)
 
 
 def summed_along_z(x):
@@ -167,25 +174,30 @@
     near = summed_along_z(product_near)
     take = lambda j: lax.dynamic_index_in_dim(near, (y + j) % NY, axis=0, keepdims=False)
     opposite = take(2)
-    near = summed_along_y(opposite[: HALF // 2], opposite[HALF // 2 :], take(0), take(1), take(-1))
-    near = near.astype(BF16)
-    sums, last = [], (product_near, far_res)
+    sent = first_step(opposite[: HALF // 2], opposite[HALF // 2 :], take(1), take(-1))
+    near = added(take(0), *second_step(*sent))
+    steps, last = [], (product_near, far_res)
     for a, b in ORDER:
         x = h.reshape(2, HALF, -1)[:, a:b].reshape(2 * (b - a), -1)
         x = flipped(tied(x, near_res[1]) if a else x, "xh")
         x = tied(x, *last, flops=0 if a else TIE)
         low, high, rest = product(m, (x, flipped(x, "c")), w, far_res, a, b - a, True, 1 if a else FAR)
         last = (rest,)
-        x = summed_along_y(low, high, *rest).astype(BF16)
-        x = lax.all_to_all(x, "z", split_axis=0, concat_axis=0, tiled=True)
-        sums.append(jnp.sum(x.astype(F32), axis=0).astype(BF16))
+        own, ahead, behind = rest
+        steps.append((own, *first_step(low, high, ahead, behind)))
+    (own, *one), (other, *two) = steps
+    up, down = second_step(*one)
+    one = added(own, up, down)
+    sums = [one, added(tied(other, one, flops=HOLD), *second_step(*two))]
+    sums = [lax.all_to_all(x, "z", split_axis=0, concat_axis=0, tiled=True) for x in sums]
+    sums = [jnp.sum(x.astype(F32), axis=0).astype(BF16) for x in sums]
     handed = handed_over((near, jnp.concatenate(sums)), group, y)
     wide = handed.astype(F32)
     squares = jnp.sum(wide * wide, axis=1)
-    for axis, n in (("z", NZ), ("y", NY)):
-        squares = jnp.broadcast_to(squares, (n, 768))
-        squares = lax.all_to_all(squares, axis, split_axis=0, concat_axis=0, tiled=True)
-        squares = jnp.sum(squares, axis=0)
+    squares = lax.all_to_all(
+        jnp.broadcast_to(squares, (NY * NZ, 768)), ("y", "z"), split_axis=0, concat_axis=0, tiled=True
+    )
+    squares = jnp.sum(squares, axis=0)
     scale = lax.rsqrt(squares / D + 1e-05)
     normed = (wide * scale[:, None] * gain[None, :]).astype(BF16)
     return (handed[None], normed[None])

time: 188 us -> 190 us (1.011); the launches traced: 187 us -> 187 us
  blocking collectives: 13.1 us -> 0 us
  waiting for transfers between devices: 61.3 us -> 72 us
  starting transfers between devices: 44.4 us -> 47.6 us
  other arithmetic: 11.7 us -> 14.2 us
  Pallas kernels: 27.2 us -> 25 us
    all_to_all x1 -> x0, blocking collectives: 13.1 us -> none  [shards(): lax.all_to_all(squares, axis, split_axis=0, concat_axis=0, tiled=True)]
    all_to_all x3, waiting for transfers between devices: 18.7 us -> 30.4 us  [the longest x2 20.7 us: shards(): lax.all_to_all(x, 'z', split_axis=0, concat_axis=0, tiled=True)]
    unnamed x18 -> x14, local copies, waits for them, and re-layouts: 6.84 us -> 1.72 us
    ppermute x12, waiting for transfers between devices: 27.4 us -> 24.4 us  [shifted(): return lax.ppermute(x, axis, [(i, (i + by) % n) for i in range(n)])]
    all_to_all x3, starting transfers between devices: 15.8 us -> 18.6 us  [the longest x2 11.9 us: shards(): lax.all_to_all(x, 'z', split_axis=0, concat_axis=0, tiled=True)]
    pallas_call x3, Pallas kernels: 27.2 us -> 25 us  [product(): pl.pallas_call(functools.partial(product_kernel, first, rows, relative),...]
    another operation x0 -> x1, local copies, waits for them, and re-layouts: none -> 2.08 us  [shards(): own, ahead, behind = rest]
  transfers between devices with their start and end apart: 25 -> 25, of which waited for: 15 -> 12; matrix products, arithmetic and copies ran while one was open for 9% -> 13% of each run, Pallas kernels for 15% -> 13%
where the time goes in v5:
time: 190 us; the launch traced here: 187 us
  waiting for transfers between devices  72 us (38%)
  starting transfers between devices  47.6 us (25%)
  Pallas kernels  25 us (13%)
  between operations  14.4 us (8%)
  other arithmetic  14.2 us (7%)
  local copies, waits for them, and re-layouts  14.1 us (7%)
    pallas_call x3, Pallas kernels, product(): pl.pallas_call(functools.partial(product_kernel, first, rows, relative),...  25 us
    ppermute x12, waiting for transfers between devices, shifted(): return lax.ppermute(x, axis, [(i, (i + by) % n) for i in range(n)])  24.4 us
    all_to_all x2, waiting for transfers between devices, shards(): lax.all_to_all(x, 'z', split_axis=0, concat_axis=0, tiled=True)  20.7 us
    ppermute x12, starting transfers between devices, shifted(): return lax.ppermute(x, axis, [(i, (i + by) % n) for i in range(n)])  18.7 us
    ppermute x7, waiting for transfers between devices, flipped(): return lax.ppermute(x, axes, [(i, n - 1 - i) for i in range(n)])  12.9 us
    all_to_all x2, starting transfers between devices, shards(): lax.all_to_all(x, 'z', split_axis=0, concat_axis=0, tiled=True)  11.9 us
    all_to_all x1, waiting for transfers between devices, shards(): lax.all_to_all(jnp.broadcast_to(squares, (NY * NZ, 768)), ('y', 'z'), spl...  9.75 us
    all_to_all x1, starting transfers between devices, shards(): lax.all_to_all(jnp.broadcast_to(squares, (NY * NZ, 768)), ('y', 'z'), spl...  6.71 us
  transfers between devices with their start and end apart: 25, of which 12 were waited for; matrix products, arithmetic and copies ran while one was open for 13% of the time, Pallas kernels for 13%

profile of v5, /device:TPU:2, one launch (start us, length us, event | category | flops | bytes accessed | tf_op | source)
XLA Modules:
  0.0 187.2 jit_solution(11370155421575652400)
XLA Ops:
  7.3 1.7 constant_dynamic-slice_fusion
  10.2 2.6 %fusion.8 = (bf16[2,192,896]{2,1,0:T(8,128)(2,1)}, bf16[2,192,896]{2,1,0:T(8,128)(2,1)}) fusion(bf16[2,384,896]{2,1,0:T(8,128)(2,1)} %bitcast.61), kind=kLoop, calls=%fused_computation.49 | loop fusion | bytes 2752512 | tf_op jit(solution)/shard_map/slice | solution.py:181
  12.8 2.1 %collective-permute-start.6 = (bf16[384,896]{1,0:T(8,128)(2,1)}, bf16[384,896]{1,0:T(8,128)(2,1)S(1)}, u32[]{:S(2)}, u32[]{:S(2)}) collective-permute-start(bf16[384,896]{1,0:T(8,128)(2,1)} %bitcast.13), channel_id=1, source_target_pairs={{0,64},{64,0},{1,65},{65,1},{2,66},{66,2},{3,67},{67,3},{4,68},{68... | collective-permute-start | bytes 2064392 | tf_op jit(solution)/shard_map/ppermute | solution.py:31
  15.9 1.6 pad_maximum_fusion.8
  18.9 9.7 %shard_map.59.refs_1_ = bf16[8,4,384,256]{3,2,1,0:T(8,128)(2,1)} custom-call(s32[1]{0:T(128)} %bitcast.m_ref, bf16[768,896]{1,0:T(8,128)(2,1)S(1)} %bitcast.62, bf16[768,896]{1,0:T(8,128)(2,1)S(1)} %collective-permute-done.h1_ref, bf16[896,2048]{1,0:T(8,128)(2,1)} %bitcast.67, bf16[24,2048]{1,0:T(8,128)(2,1)S(1)} %get-tuple-element.36.r0_ref, ...), custom_call_target="tpu_custom_call" | custom-call | flops 112742891520 | bytes 12713984 | tf_op jit(solution)/shard_map/pallas_call | solution.py:90
  28.7 7.5 %collective-permute-done.7.refs_2_ = bf16[2,24,2048]{2,1,0:T(8,128)(2,1)} collective-permute-done((bf16[2,24,2048]{2,1,0:T(8,128)(2,1)}, bf16[2,24,2048]{2,1,0:T(8,128)(2,1)}, u32[]{:S(2)}, u32[]{:S(2)}) %collective-permute-start.7) | collective-permute-done | bytes 196640 | tf_op jit(solution)/shard_map/ppermute | solution.py:31
  37.1 2.1 %collective-permute-start.13 = (bf16[384,896]{1,0:T(8,128)(2,1)}, bf16[384,896]{1,0:T(8,128)(2,1)S(1)}, u32[]{:S(2)}, u32[]{:S(2)}) collective-permute-start(bf16[384,896]{1,0:T(8,128)(2,1)} %shard_map.62), channel_id=1, source_target_pairs={{0,64},{64,0},{1,65},{65,1},{2,66},{66,2},{3,67},{67,3},{4,68},{68... | collective-permute-start | bytes 2064392 | tf_op jit(solution)/shard_map/ppermute | solution.py:31
  40.2 7.8 %shard_map.61 = (bf16[4,192,256]{2,1,0:T(8,128)(2,1)S(1)}, bf16[4,192,256]{2,1,0:T(8,128)(2,1)S(1)}, bf16[3,8,192,256]{3,2,1,0:T(8,128)(2,1)}) custom-call(s32[1]{0:T(128)} %bitcast.m_ref, bf16[384,896]{1,0:T(8,128)(2,1)S(1)} %copy-done.5, bf16[384,896]{1,0:T(8,128)(2,1)S(1)} %collective-permute-done.8.h1_ref, bf16[896,2048]{1,0:T(8,128)(2,1)} %bitcast.68, ...), custom_call_target="tpu_custom_call" | custom-call | flops 2818572288 | bytes 8192000 | tf_op jit(solution)/shard_map/pallas_call | solution.py:90
  49.4 1.9 %collective-permute-start.11 = (bf16[4,192,256]{2,1,0:T(8,128)(2,1)S(1)}, bf16[4,192,256]{2,1,0:T(8,128)(2,1)S(1)}, u32[]{:S(2)}, u32[]{:S(2)}) collective-permute-start(bf16[4,192,256]{2,1,0:T(8,128)(2,1)S(1)} %get-tuple-element.10), channel_id=1, source_target_pairs={{0,24},{8,0},{16,8},{24,16},{1,25},{9,1},{17,9},{25,17},{2,26},{10... | collective-permute-start | bytes 1179656 | tf_op jit(solution)/shard_map/ppermute | solution.py:26
  51.3 5.4 %collective-permute-done.13.refs_0_ = bf16[384,896]{1,0:T(8,128)(2,1)S(1)} collective-permute-done((bf16[384,896]{1,0:T(8,128)(2,1)}, bf16[384,896]{1,0:T(8,128)(2,1)S(1)}, u32[]{:S(2)}, u32[]{:S(2)}) %collective-permute-start.13) | collective-permute-done | bytes 688160 | tf_op jit(solution)/shard_map/ppermute | solution.py:31
  58.7 1.8 collective-permute-done.9
  61.8 3.0 %collective-permute-start.12 = (bf16[8,192,256]{2,1,0:T(8,128)(2,1)S(1)}, bf16[8,192,256]{2,1,0:T(8,128)(2,1)S(1)}, u32[]{:S(2)}, u32[]{:S(2)}) collective-permute-start(bf16[8,192,256]{2,1,0:T(8,128)(2,1)S(1)} %pad_maximum_fusion.1), channel_id=1, source_target_pairs={{0,24},{8,0},{16,8},{24,16},{1,25},{9,1},{17,9},{25,17},{2,26},{10... | collective-permute-start | bytes 2359304 | tf_op jit(solution)/shard_map/ppermute | solution.py:26
  65.0 7.4 %shard_map.64 = (bf16[4,192,256]{2,1,0:T(8,128)(2,1)S(1)}, bf16[4,192,256]{2,1,0:T(8,128)(2,1)S(1)}, bf16[3,8,192,256]{3,2,1,0:T(8,128)(2,1)}) custom-call(s32[1]{0:T(128)} %bitcast.m_ref, bf16[384,896]{1,0:T(8,128)(2,1)S(1)} %copy-done.2, bf16[384,896]{1,0:T(8,128)(2,1)S(1)} %collective-permute-done.14.h1_ref, bf16[896,2048]{1,0:T(8,128)(2,1)} %bitcast.69, ...), custom_call_target="tpu_custom_call" | custom-call | flops 2818572288 | bytes 8192000 | tf_op jit(solution)/shard_map/pallas_call | solution.py:90
  73.5 2.5 %collective-permute-start.17 = (bf16[4,192,256]{2,1,0:T(8,128)(2,1)S(1)}, bf16[4,192,256]{2,1,0:T(8,128)(2,1)S(1)}, u32[]{:S(2)}, u32[]{:S(2)}) collective-permute-start(bf16[4,192,256]{2,1,0:T(8,128)(2,1)S(1)} %get-tuple-element.13), channel_id=1, source_target_pairs={{0,24},{8,0},{16,8},{24,16},{1,25},{9,1},{17,9},{25,17},{2,26},{10... | collective-permute-start | bytes 1179656 | tf_op jit(solution)/shard_map/ppermute | solution.py:26
  75.9 2.1 %slice_bitcast_fusion.refs_0_ = bf16[8,192,256]{2,1,0:T(8,128)(2,1)} fusion(bf16[3,8,192,256]{3,2,1,0:T(8,128)(2,1)} %get-tuple-element.11), kind=kLoop, calls=%fused_computation.10 | loop fusion | bytes 1572864 | tf_op jit(solution)/shard_map/unstack | solution.py:186
  79.2 13.8 %collective-permute-done.15 = bf16[4,192,256]{2,1,0:T(8,128)(2,1)S(1)} collective-permute-done((bf16[4,192,256]{2,1,0:T(8,128)(2,1)S(1)}, bf16[4,192,256]{2,1,0:T(8,128)(2,1)S(1)}, u32[]{:S(2)}, u32[]{:S(2)}) %collective-permute-start.15) | collective-permute-done | bytes 393248 | tf_op jit(solution)/shard_map/ppermute | solution.py:26
  94.5 2.0 %collective-permute-start.16 = (bf16[8,192,256]{2,1,0:T(8,128)(2,1)S(1)}, bf16[8,192,256]{2,1,0:T(8,128)(2,1)}, u32[]{:S(2)}, u32[]{:S(2)}) collective-permute-start(bf16[8,192,256]{2,1,0:T(8,128)(2,1)S(1)} %pad_maximum_fusion.2), channel_id=1, source_target_pairs={{0,8},{8,16},{16,24},{24,0},{1,9},{9,17},{17,25},{25,1},{2,10},{10... | collective-permute-start | bytes 2359304 | tf_op jit(solution)/shard_map/ppermute | solution.py:26
  96.5 2.3 %fusion.1.refs_1_ = bf16[8,192,256]{2,1,0:T(8,128)(2,1)} fusion(bf16[8,192,256]{2,1,0:T(8,128)(2,1)S(1)} %collective-permute-done.12, bf16[8,192,256]{2,1,0:T(8,128)(2,1)S(1)} %collective-permute-done.10, bf16[3,8,192,256]{3,2,1,0:T(8,128)(2,1)} %get-tuple-element.8.refs_1_), kind=kLoop, calls=%fused_computation.2 | loop fusion | flops 2359296 | bytes 3145728 | tf_op jit(solution)/shard_map/convert_element_type | solution.py:136
  98.8 8.4 %all-to-all-start = ((bf16[8,192,256]{2,1,0:T(8,128)(2,1)}), bf16[8,192,256]{2,1,0:T(8,128)(2,1)S(1)}, u32[]{:S(2)}, u32[]{:S(2)}) async-start(bf16[8,192,256]{2,1,0:T(8,128)(2,1)} %fusion.1.refs_1_), calls=%async_computation.1 | async-start | bytes 1572864 | tf_op jit(solution)/shard_map/all_to_all | solution.py:192
  107.2 4.7 %collective-permute-done.18 = bf16[8,192,256]{2,1,0:T(8,128)(2,1)S(1)} collective-permute-done((bf16[8,192,256]{2,1,0:T(8,128)(2,1)S(1)}, bf16[8,192,256]{2,1,0:T(8,128)(2,1)S(1)}, u32[]{:S(2)}, u32[]{:S(2)}) %collective-permute-start.18) | collective-permute-done | bytes 786464 | tf_op jit(solution)/shard_map/ppermute | solution.py:26
  111.9 1.6 collective-permute-done.16
  113.4 2.5 %add_convert_fusion = bf16[8,192,256]{2,1,0:T(8,128)(2,1)} fusion(bf16[8,192,256]{2,1,0:T(8,128)(2,1)S(1)} %collective-permute-done.18, bf16[8,192,256]{2,1,0:T(8,128)(2,1)} %collective-permute-done.16, bf16[8,192,256]{2,1,0:T(8,128)(2,1)} %shard_map.65), kind=kLoop, calls=%fused_computation.3 | loop fusion | flops 2359296 | bytes 3145728 | tf_op jit(solution)/shard_map/convert_element_type | solution.py:136
  116.0 12.0 %all-to-all-done = bf16[8,192,256]{2,1,0:T(8,128)(2,1)S(1)} async-done(((bf16[8,192,256]{2,1,0:T(8,128)(2,1)}), bf16[8,192,256]{2,1,0:T(8,128)(2,1)S(1)}, u32[]{:S(2)}, u32[]{:S(2)}) %all-to-all-start) | async-done | bytes 786464 | tf_op jit(solution)/shard_map/all_to_all | solution.py:192
  128.0 3.5 %all-to-all-start.1 = ((bf16[8,192,256]{2,1,0:T(8,128)(2,1)}), bf16[8,192,256]{2,1,0:T(8,128)(2,1)S(1)}, u32[]{:S(2)}, u32[]{:S(2)}) async-start(bf16[8,192,256]{2,1,0:T(8,128)(2,1)} %add_convert_fusion), calls=%async_computation.2 | async-start | bytes 1572864 | tf_op jit(solution)/shard_map/all_to_all | solution.py:192
  133.1 2.9 %collective-permute-start.4 = (bf16[192,256]{1,0:T(8,128)(2,1)S(1)}, bf16[192,256]{1,0:T(8,128)(2,1)S(1)}, u32[]{:S(2)}, u32[]{:S(2)}) collective-permute-start(bf16[192,256]{1,0:T(8,128)(2,1)S(1)} %get-tuple-element.30), channel_id=1, source_target_pairs={{0,24},{8,0},{16,8},{24,16},{1,25},{9,1},{17,9},{25,17},{2,26},{10... | collective-permute-start | bytes 294920 | tf_op jit(solution)/shard_map/ppermute | solution.py:26
  136.0 2.6 %collective-permute-done.2 = bf16[192,256]{1,0:T(8,128)(2,1)S(1)} collective-permute-done((bf16[192,256]{1,0:T(8,128)(2,1)S(1)}, bf16[192,256]{1,0:T(8,128)(2,1)S(1)}, u32[]{:S(2)}, u32[]{:S(2)}) %collective-permute-start.2) | collective-permute-done | bytes 98336 | tf_op jit(solution)/shard_map/ppermute | solution.py:26
  139.6 3.3 %collective-permute-start.5 = (bf16[384,256]{1,0:T(8,128)(2,1)S(1)}, bf16[384,256]{1,0:T(8,128)(2,1)S(1)}, u32[]{:S(2)}, u32[]{:S(2)}) collective-permute-start(bf16[384,256]{1,0:T(8,128)(2,1)S(1)} %pad_maximum_fusion.7), channel_id=1, source_target_pairs={{0,24},{8,0},{16,8},{24,16},{1,25},{9,1},{17,9},{25,17},{2,26},{10... | collective-permute-start | bytes 589832 | tf_op jit(solution)/shard_map/ppermute | solution.py:26
  143.2 8.7 %all-to-all-done.1 = bf16[8,192,256]{2,1,0:T(8,128)(2,1)S(1)} async-done(((bf16[8,192,256]{2,1,0:T(8,128)(2,1)}), bf16[8,192,256]{2,1,0:T(8,128)(2,1)S(1)}, u32[]{:S(2)}, u32[]{:S(2)}) %all-to-all-start.1) | async-done | bytes 786464 | tf_op jit(solution)/shard_map/all_to_all | solution.py:192
  153.1 2.4 %collective-permute-start.19 = (bf16[384,256]{1,0:T(8,128)(2,1)S(1)}, bf16[384,256]{1,0:T(8,128)(2,1)S(1)}, u32[]{:S(2)}, u32[]{:S(2)}) collective-permute-start(bf16[384,256]{1,0:T(8,128)(2,1)S(1)} %get-tuple-element.14), channel_id=1, source_target_pairs={{0,192},{1,193},{2,194},{3,195},{4,196},{5,197},{6,198},{7,199},{8... | collective-permute-start | bytes 589832 | tf_op jit(solution)/shard_map/ppermute | solution.py:156
  157.1 2.7 %collective-permute-done.19 = bf16[384,256]{1,0:T(8,128)(2,1)S(1)} collective-permute-done((bf16[384,256]{1,0:T(8,128)(2,1)S(1)}, bf16[384,256]{1,0:T(8,128)(2,1)S(1)}, u32[]{:S(2)}, u32[]{:S(2)}) %collective-permute-start.19) | collective-permute-done | bytes 196640 | tf_op jit(solution)/shard_map/ppermute | solution.py:156
  162.1 6.7 %all-to-all-start.2 = ((f32[32,1,768]{2,1,0:T(1,128)}), f32[32,1,768]{2,1,0:T(1,128)S(1)}, u32[]{:S(2)}, u32[]{:S(2)}) async-start(f32[32,1,768]{2,1,0:T(1,128)} %broadcast_in_dim.9), calls=%async_computation.3 | async-start | bytes 196608 | tf_op jit(solution)/shard_map/all_to_all | solution.py:197
  169.6 9.8 %all-to-all-done.2 = f32[32,1,768]{2,1,0:T(1,128)S(1)} async-done(((f32[32,1,768]{2,1,0:T(1,128)}), f32[32,1,768]{2,1,0:T(1,128)S(1)}, u32[]{:S(2)}, u32[]{:S(2)}) %all-to-all-start.2) | async-done | bytes 98336 | tf_op jit(solution)/shard_map/all_to_all | solution.py:197
  (72 shorter events, 23.6 us)
Async XLA Ops:
  7.2 124.5 %reduce-scatter.2.cloned.1.call-start = ((), (), s32[]{:S(2)}) async-start(), calls=%async_computation.4 | async-start | bytes 7077888 | tf_op jit(solution)/shard_map/reduce_scatter | solution.py:140
  7.2 11.7 %collective-permute-start = (bf16[768,896]{1,0:T(8,128)(2,1)}, bf16[768,896]{1,0:T(8,128)(2,1)S(1)}, u32[]{:S(2)}, u32[]{:S(2)}) collective-permute-start(bf16[768,896]{1,0:T(8,128)(2,1)} %bitcast.60), channel_id=1, source_target_pairs={{0,32},{32,0},{1,33},{33,1},{2,34},{34,2},{3,35},{35,3},{4,36},{36... | collective-permute-start | bytes 4128776 | tf_op jit(solution)/shard_map/ppermute | solution.py:31
  9.7 5.2 %collective-permute-start.1 = (bf16[2,24,2048]{2,1,0:T(8,128)(2,1)}, bf16[2,24,2048]{2,1,0:T(8,128)(2,1)}, u32[]{:S(2)}, u32[]{:S(2)}) collective-permute-start(bf16[2,24,2048]{2,1,0:T(8,128)(2,1)} %pad_maximum_fusion.5), channel_id=1, source_target_pairs={{0,32},{32,0},{1,33},{33,1},{2,34},{34,2},{3,35},{35,3},{4,36},{36... | collective-permute-start | bytes 589832 | tf_op jit(solution)/shard_map/ppermute | solution.py:31
  10.2 8.7 %copy-start = (bf16[1,768,896]{2,1,0:T(8,128)(2,1)S(1)}, bf16[1,768,896]{2,1,0:T(8,128)(2,1)}, u32[]{:S(2)}) copy-start(bf16[1,768,896]{2,1,0:T(8,128)(2,1)} %param.4) | copy-start | bytes 4128772
  12.8 23.4 %collective-permute-start.6 = (bf16[384,896]{1,0:T(8,128)(2,1)}, bf16[384,896]{1,0:T(8,128)(2,1)S(1)}, u32[]{:S(2)}, u32[]{:S(2)}) collective-permute-start(bf16[384,896]{1,0:T(8,128)(2,1)} %bitcast.13), channel_id=1, source_target_pairs={{0,64},{64,0},{1,65},{65,1},{2,66},{66,2},{3,67},{67,3},{4,68},{68... | collective-permute-start | bytes 2064392 | tf_op jit(solution)/shard_map/ppermute | solution.py:31
  15.9 3.0 %copy-start.3 = (bf16[24,2048]{1,0:T(8,128)(2,1)}, bf16[24,2048]{1,0:T(8,128)(2,1)S(1)}, u32[]{:S(2)}) copy-start(bf16[24,2048]{1,0:T(8,128)(2,1)S(1)} %get-tuple-element.41.r1_ref.refs_1_) | copy-start | bytes 294916
  17.5 18.7 %collective-permute-start.7 = (bf16[2,24,2048]{2,1,0:T(8,128)(2,1)}, bf16[2,24,2048]{2,1,0:T(8,128)(2,1)}, u32[]{:S(2)}, u32[]{:S(2)}) collective-permute-start(bf16[2,24,2048]{2,1,0:T(8,128)(2,1)} %pad_maximum_fusion.8), channel_id=1, source_target_pairs={{0,64},{64,0},{1,65},{65,1},{2,66},{66,2},{3,67},{67,3},{4,68},{68... | collective-permute-start | bytes 589832 | tf_op jit(solution)/shard_map/ppermute | solution.py:31
  36.2 0.8 copy-start.4
  37.1 3.1 %copy-start.5 = (bf16[384,896]{1,0:T(8,128)(2,1)S(1)}, bf16[384,896]{1,0:T(8,128)(2,1)}, u32[]{:S(2)}) copy-start(bf16[384,896]{1,0:T(8,128)(2,1)} %shard_map.60.h0_ref) | copy-start | bytes 2064388
  37.1 3.1 %collective-permute-start.8 = (bf16[384,896]{1,0:T(8,128)(2,1)}, bf16[384,896]{1,0:T(8,128)(2,1)S(1)}, u32[]{:S(2)}, u32[]{:S(2)}) collective-permute-start(bf16[384,896]{1,0:T(8,128)(2,1)} %shard_map.60.h0_ref), channel_id=1, source_target_pairs={{0,32},{32,0},{1,33},{33,1},{2,34},{34,2},{3,35},{35,3},{4,36},{36... | collective-permute-start | bytes 2064392 | tf_op jit(solution)/shard_map/ppermute | solution.py:31
  37.1 19.6 %collective-permute-start.13 = (bf16[384,896]{1,0:T(8,128)(2,1)}, bf16[384,896]{1,0:T(8,128)(2,1)S(1)}, u32[]{:S(2)}, u32[]{:S(2)}) collective-permute-start(bf16[384,896]{1,0:T(8,128)(2,1)} %shard_map.62), channel_id=1, source_target_pairs={{0,64},{64,0},{1,65},{65,1},{2,66},{66,2},{3,67},{67,3},{4,68},{68... | collective-permute-start | bytes 2064392 | tf_op jit(solution)/shard_map/ppermute | solution.py:31
  48.0 12.4 %collective-permute-start.9 = (bf16[4,192,256]{2,1,0:T(8,128)(2,1)S(1)}, bf16[4,192,256]{2,1,0:T(8,128)(2,1)S(1)}, u32[]{:S(2)}, u32[]{:S(2)}) collective-permute-start(bf16[4,192,256]{2,1,0:T(8,128)(2,1)S(1)} %get-tuple-element.9), channel_id=1, source_target_pairs={{0,8},{8,16},{16,24},{24,0},{1,9},{9,17},{17,25},{25,1},{2,10},{10... | collective-permute-start | bytes 1179656 | tf_op jit(solution)/shard_map/ppermute | solution.py:26
  49.4 11.1 %collective-permute-start.11 = (bf16[4,192,256]{2,1,0:T(8,128)(2,1)S(1)}, bf16[4,192,256]{2,1,0:T(8,128)(2,1)S(1)}, u32[]{:S(2)}, u32[]{:S(2)}) collective-permute-start(bf16[4,192,256]{2,1,0:T(8,128)(2,1)S(1)} %get-tuple-element.10), channel_id=1, source_target_pairs={{0,24},{8,0},{16,8},{24,16},{1,25},{9,1},{17,9},{25,17},{2,26},{10... | collective-permute-start | bytes 1179656 | tf_op jit(solution)/shard_map/ppermute | solution.py:26
  56.6 0.9 copy-start.1
  57.5 7.5 %collective-permute-start.14 = (bf16[384,896]{1,0:T(8,128)(2,1)}, bf16[384,896]{1,0:T(8,128)(2,1)S(1)}, u32[]{:S(2)}, u32[]{:S(2)}) collective-permute-start(bf16[384,896]{1,0:T(8,128)(2,1)} %shard_map.63.h0_ref), channel_id=1, source_target_pairs={{0,32},{32,0},{1,33},{33,1},{2,34},{34,2},{3,35},{35,3},{4,36},{36... | collective-permute-start | bytes 2064392 | tf_op jit(solution)/shard_map/ppermute | solution.py:31
  61.7 3.3 %copy-start.2 = (bf16[384,896]{1,0:T(8,128)(2,1)S(1)}, bf16[384,896]{1,0:T(8,128)(2,1)}, u32[]{:S(2)}) copy-start(bf16[384,896]{1,0:T(8,128)(2,1)} %shard_map.63.h0_ref) | copy-start | bytes 2064388
  61.8 34.7 %collective-permute-start.12 = (bf16[8,192,256]{2,1,0:T(8,128)(2,1)S(1)}, bf16[8,192,256]{2,1,0:T(8,128)(2,1)S(1)}, u32[]{:S(2)}, u32[]{:S(2)}) collective-permute-start(bf16[8,192,256]{2,1,0:T(8,128)(2,1)S(1)} %pad_maximum_fusion.1), channel_id=1, source_target_pairs={{0,24},{8,0},{16,8},{24,16},{1,25},{9,1},{17,9},{25,17},{2,26},{10... | collective-permute-start | bytes 2359304 | tf_op jit(solution)/shard_map/ppermute | solution.py:26
  64.9 31.6 %collective-permute-start.10 = (bf16[8,192,256]{2,1,0:T(8,128)(2,1)S(1)}, bf16[8,192,256]{2,1,0:T(8,128)(2,1)S(1)}, u32[]{:S(2)}, u32[]{:S(2)}) collective-permute-start(bf16[8,192,256]{2,1,0:T(8,128)(2,1)S(1)} %pad_maximum_fusion), channel_id=1, source_target_pairs={{0,8},{8,16},{16,24},{24,0},{1,9},{9,17},{17,25},{25,1},{2,10},{10... | collective-permute-start | bytes 2359304 | tf_op jit(solution)/shard_map/ppermute | solution.py:26
  72.4 20.5 %collective-permute-start.15 = (bf16[4,192,256]{2,1,0:T(8,128)(2,1)S(1)}, bf16[4,192,256]{2,1,0:T(8,128)(2,1)S(1)}, u32[]{:S(2)}, u32[]{:S(2)}) collective-permute-start(bf16[4,192,256]{2,1,0:T(8,128)(2,1)S(1)} %get-tuple-element.12), channel_id=1, source_target_pairs={{0,8},{8,16},{16,24},{24,0},{1,9},{9,17},{17,25},{25,1},{2,10},{10... | collective-permute-start | bytes 1179656 | tf_op jit(solution)/shard_map/ppermute | solution.py:26
  73.5 19.5 %collective-permute-start.17 = (bf16[4,192,256]{2,1,0:T(8,128)(2,1)S(1)}, bf16[4,192,256]{2,1,0:T(8,128)(2,1)S(1)}, u32[]{:S(2)}, u32[]{:S(2)}) collective-permute-start(bf16[4,192,256]{2,1,0:T(8,128)(2,1)S(1)} %get-tuple-element.13), channel_id=1, source_target_pairs={{0,24},{8,0},{16,8},{24,16},{1,25},{9,1},{17,9},{25,17},{2,26},{10... | collective-permute-start | bytes 1179656 | tf_op jit(solution)/shard_map/ppermute | solution.py:26
  94.2 17.6 %collective-permute-start.18 = (bf16[8,192,256]{2,1,0:T(8,128)(2,1)S(1)}, bf16[8,192,256]{2,1,0:T(8,128)(2,1)S(1)}, u32[]{:S(2)}, u32[]{:S(2)}) collective-permute-start(bf16[8,192,256]{2,1,0:T(8,128)(2,1)S(1)} %pad_maximum_fusion.3), channel_id=1, source_target_pairs={{0,24},{8,0},{16,8},{24,16},{1,25},{9,1},{17,9},{25,17},{2,26},{10... | collective-permute-start | bytes 2359304 | tf_op jit(solution)/shard_map/ppermute | solution.py:26
  94.5 18.9 %collective-permute-start.16 = (bf16[8,192,256]{2,1,0:T(8,128)(2,1)S(1)}, bf16[8,192,256]{2,1,0:T(8,128)(2,1)}, u32[]{:S(2)}, u32[]{:S(2)}) collective-permute-start(bf16[8,192,256]{2,1,0:T(8,128)(2,1)S(1)} %pad_maximum_fusion.2), channel_id=1, source_target_pairs={{0,8},{8,16},{16,24},{24,0},{1,9},{9,17},{17,25},{25,1},{2,10},{10... | collective-permute-start | bytes 2359304 | tf_op jit(solution)/shard_map/ppermute | solution.py:26
  98.8 29.2 %all-to-all-start = ((bf16[8,192,256]{2,1,0:T(8,128)(2,1)}), bf16[8,192,256]{2,1,0:T(8,128)(2,1)S(1)}, u32[]{:S(2)}, u32[]{:S(2)}) async-start(bf16[8,192,256]{2,1,0:T(8,128)(2,1)} %fusion.1.refs_1_), calls=%async_computation.1 | async-start | bytes 1572864 | tf_op jit(solution)/shard_map/all_to_all | solution.py:192
  128.0 23.9 %all-to-all-start.1 = ((bf16[8,192,256]{2,1,0:T(8,128)(2,1)}), bf16[8,192,256]{2,1,0:T(8,128)(2,1)S(1)}, u32[]{:S(2)}, u32[]{:S(2)}) async-start(bf16[8,192,256]{2,1,0:T(8,128)(2,1)} %add_convert_fusion), calls=%async_computation.2 | async-start | bytes 1572864 | tf_op jit(solution)/shard_map/all_to_all | solution.py:192
  132.7 5.9 %collective-permute-start.2 = (bf16[192,256]{1,0:T(8,128)(2,1)S(1)}, bf16[192,256]{1,0:T(8,128)(2,1)S(1)}, u32[]{:S(2)}, u32[]{:S(2)}) collective-permute-start(bf16[192,256]{1,0:T(8,128)(2,1)S(1)} %get-tuple-element.28), channel_id=1, source_target_pairs={{0,8},{8,16},{16,24},{24,0},{1,9},{9,17},{17,25},{25,1},{2,10},{10... | collective-permute-start | bytes 294920 | tf_op jit(solution)/shard_map/ppermute | solution.py:26
  133.1 5.5 %collective-permute-start.4 = (bf16[192,256]{1,0:T(8,128)(2,1)S(1)}, bf16[192,256]{1,0:T(8,128)(2,1)S(1)}, u32[]{:S(2)}, u32[]{:S(2)}) collective-permute-start(bf16[192,256]{1,0:T(8,128)(2,1)S(1)} %get-tuple-element.30), channel_id=1, source_target_pairs={{0,24},{8,0},{16,8},{24,16},{1,25},{9,1},{17,9},{25,17},{2,26},{10... | collective-permute-start | bytes 294920 | tf_op jit(solution)/shard_map/ppermute | solution.py:26
  139.6 12.4 %collective-permute-start.5 = (bf16[384,256]{1,0:T(8,128)(2,1)S(1)}, bf16[384,256]{1,0:T(8,128)(2,1)S(1)}, u32[]{:S(2)}, u32[]{:S(2)}) collective-permute-start(bf16[384,256]{1,0:T(8,128)(2,1)S(1)} %pad_maximum_fusion.7), channel_id=1, source_target_pairs={{0,24},{8,0},{16,8},{24,16},{1,25},{9,1},{17,9},{25,17},{2,26},{10... | collective-permute-start | bytes 589832 | tf_op jit(solution)/shard_map/ppermute | solution.py:26
  143.0 9.0 %collective-permute-start.3 = (bf16[384,256]{1,0:T(8,128)(2,1)S(1)}, bf16[384,256]{1,0:T(8,128)(2,1)S(1)}, u32[]{:S(2)}, u32[]{:S(2)}) collective-permute-start(bf16[384,256]{1,0:T(8,128)(2,1)S(1)} %pad_maximum_fusion.6), channel_id=1, source_target_pairs={{0,8},{8,16},{16,24},{24,0},{1,9},{9,17},{17,25},{25,1},{2,10},{10... | collective-permute-start | bytes 589832 | tf_op jit(solution)/shard_map/ppermute | solution.py:26
  153.1 26.4 %copy-start.6 = (f32[1,256]{1,0:T(1,128)S(1)}, f32[1,256]{1,0:T(1,128)}, u32[]{:S(2)}) copy-start(f32[1,256]{1,0:T(1,128)} %param.7) | copy-start | bytes 3076
  153.1 6.7 %collective-permute-start.19 = (bf16[384,256]{1,0:T(8,128)(2,1)S(1)}, bf16[384,256]{1,0:T(8,128)(2,1)S(1)}, u32[]{:S(2)}, u32[]{:S(2)}) collective-permute-start(bf16[384,256]{1,0:T(8,128)(2,1)S(1)} %get-tuple-element.14), channel_id=1, source_target_pairs={{0,192},{1,193},{2,194},{3,195},{4,196},{5,197},{6,198},{7,199},{8... | collective-permute-start | bytes 589832 | tf_op jit(solution)/shard_map/ppermute | solution.py:156
  155.6 5.7 %collective-permute-start.20 = (bf16[384,256]{1,0:T(8,128)(2,1)S(1)}, bf16[384,256]{1,0:T(8,128)(2,1)S(1)}, u32[]{:S(2)}, u32[]{:S(2)}) collective-permute-start(bf16[384,256]{1,0:T(8,128)(2,1)S(1)} %broadcast_select_fusion), channel_id=1, source_target_pairs={{0,128},{1,129},{2,130},{3,131},{4,132},{5,133},{6,134},{7,135},{8... | collective-permute-start | bytes 589832 | tf_op jit(solution)/shard_map/ppermute | solution.py:155
  162.1 17.2 %all-to-all-start.2 = ((f32[32,1,768]{2,1,0:T(1,128)}), f32[32,1,768]{2,1,0:T(1,128)S(1)}, u32[]{:S(2)}, u32[]{:S(2)}) async-start(f32[32,1,768]{2,1,0:T(1,128)} %broadcast_in_dim.9), calls=%async_computation.3 | async-start | bytes 196608 | tf_op jit(solution)/shard_map/all_to_all | solution.py:197
Sparse Core Ops, SparseCore 0:
  28.8 78.0 reduce-scatter.1

commit v6 on v5

--- a/solution.py
+++ b/solution.py
@@ -14,7 +14,7 @@
 STEP = 2
 HALF = 384
 ORDER = ((0, 192), (192, HALF))
-HOLD = 4 * 10**10
+HOLD = 1 * 10**10
 TIE = 3 * 10**11
 SCALE, FAR = 20, 1
 VMEM = 50 * 2**20
@@ -132,6 +132,20 @@
     return shifted(ahead, "y", NY, 1), shifted(behind, "y", NY, -1)
 
 
+def ring_summed_along_z(x, z):
+    piece = lambda j: lax.dynamic_index_in_dim(x, (z + j) % NZ, axis=0, keepdims=False)
+    far, half = piece(NZ // 2), COLS // 2
+    up, down = shifted(far[:, :half], "z", NZ, 1), shifted(far[:, half:], "z", NZ, -1)
+    ahead, behind = piece(3), piece(-3)
+    ahead = jnp.concatenate([ahead[:, :half] + up, ahead[:, half:]], axis=1)
+    behind = jnp.concatenate([behind[:, :half], behind[:, half:] + down], axis=1)
+    for j in (2, 1, 0):
+        up, down = shifted(ahead, "z", NZ, 1), shifted(behind, "z", NZ, -1)
+        if j:
+            ahead, behind = piece(j) + up, piece(-j) + down
+    return added(piece(0), up, down)
+
+
 def added(own, up, down):
     return (own.astype(F32) + up.astype(F32) + down.astype(F32)).astype(BF16)
 
@@ -188,9 +202,10 @@
     (own, *one), (other, *two) = steps
     up, down = second_step(*one)
     one = added(own, up, down)
-    sums = [one, added(tied(other, one, flops=HOLD), *second_step(*two))]
-    sums = [lax.all_to_all(x, "z", split_axis=0, concat_axis=0, tiled=True) for x in sums]
-    sums = [jnp.sum(x.astype(F32), axis=0).astype(BF16) for x in sums]
+    other = added(tied(other, one, flops=HOLD), *second_step(*two))
+    other = lax.all_to_all(other, "z", split_axis=0, concat_axis=0, tiled=True)
+    other = jnp.sum(other.astype(F32), axis=0).astype(BF16)
+    sums = [ring_summed_along_z(one, z), other]
     handed = handed_over((near, jnp.concatenate(sums)), group, y)
     wide = handed.astype(F32)
     squares = jnp.sum(wide * wide, axis=1)

time: 190 us -> 197 us (1.037)
  starting transfers between devices: 47.6 us -> 61.8 us
  waiting for transfers between devices: 72 us -> 64.3 us
    all_to_all x2 -> x1, waiting for transfers between devices: 20.7 us -> 0.01 us  [shards(): other = lax.all_to_all(other, 'z', split_axis=0, concat_axis=0, tiled=True)]
    ppermute x12 -> x20, waiting for transfers between devices: 24.4 us -> 37.2 us  [shifted(): return lax.ppermute(x, axis, [(i, (i + by) % n) for i in range(n)])]
    ppermute x12 -> x20, starting transfers between devices: 18.7 us -> 30.9 us  [shifted(): return lax.ppermute(x, axis, [(i, (i + by) % n) for i in range(n)])]
    all_to_all x1, starting transfers between devices: 6.71 us -> 12.2 us  [shards(): lax.all_to_all(jnp.broadcast_to(squares, (NY * NZ, 768)), ('y', 'z'), spl...]
    all_to_all x2 -> x1, starting transfers between devices: 11.9 us -> 8.31 us  [shards(): other = lax.all_to_all(other, 'z', split_axis=0, concat_axis=0, tiled=True)]
    convert_element_type x2 -> x3, other arithmetic: 4.86 us -> 3.85 us  [added(): return (own.astype(F32) + up.astype(F32) + down.astype(F32)).astype(BF16)]
  transfers between devices with their start and end apart: 25 -> 32, of which waited for: 12 -> 13; matrix products, arithmetic and copies ran while one was open for 13% -> 12% of each run, Pallas kernels for 13% -> 13%
where the time goes in v6:
time: 197 us; the launch traced here: 194 us
  waiting for transfers between devices  64.3 us (33%)
  starting transfers between devices  61.8 us (31%)
  Pallas kernels  24.8 us (13%)
  between operations  14.4 us (7%)
  local copies, waits for them, and re-layouts  14.2 us (7%)
  other arithmetic  14.1 us (7%)
    ppermute x20, waiting for transfers between devices, shifted(): return lax.ppermute(x, axis, [(i, (i + by) % n) for i in range(n)])  37.2 us
    ppermute x20, starting transfers between devices, shifted(): return lax.ppermute(x, axis, [(i, (i + by) % n) for i in range(n)])  30.9 us
    pallas_call x3, Pallas kernels, product(): pl.pallas_call(functools.partial(product_kernel, first, rows, relative),...  24.8 us
    ppermute x7, waiting for transfers between devices, flipped(): return lax.ppermute(x, axes, [(i, n - 1 - i) for i in range(n)])  13.1 us
    all_to_all x1, starting transfers between devices, shards(): lax.all_to_all(jnp.broadcast_to(squares, (NY * NZ, 768)), ('y', 'z'), spl...  12.2 us
    all_to_all x1, waiting for transfers between devices, shards(): lax.all_to_all(jnp.broadcast_to(squares, (NY * NZ, 768)), ('y', 'z'), spl...  9.77 us
    all_to_all x1, starting transfers between devices, shards(): other = lax.all_to_all(other, 'z', split_axis=0, concat_axis=0, tiled=True)  8.31 us
    ppermute x7, starting transfers between devices, flipped(): return lax.ppermute(x, axes, [(i, n - 1 - i) for i in range(n)])  6.21 us
  transfers between devices with their start and end apart: 32, of which 13 were waited for; matrix products, arithmetic and copies ran while one was open for 12% of the time, Pallas kernels for 13%

profile of v6, /device:TPU:2, one launch (start us, length us, event | category | flops | bytes accessed | tf_op | source)
XLA Modules:
  0.0 193.6 jit_solution(11341937579451433972)
XLA Ops:
  10.2 2.6 %fusion.10 = (bf16[2,192,896]{2,1,0:T(8,128)(2,1)}, bf16[2,192,896]{2,1,0:T(8,128)(2,1)}) fusion(bf16[2,384,896]{2,1,0:T(8,128)(2,1)} %bitcast.78), kind=kLoop, calls=%fused_computation.63 | loop fusion | bytes 2752512 | tf_op jit(solution)/shard_map/slice | solution.py:195
  12.8 2.1 %collective-permute-start.6 = (bf16[384,896]{1,0:T(8,128)(2,1)}, bf16[384,896]{1,0:T(8,128)(2,1)S(1)}, u32[]{:S(2)}, u32[]{:S(2)}) collective-permute-start(bf16[384,896]{1,0:T(8,128)(2,1)} %bitcast.13), channel_id=1, source_target_pairs={{0,64},{64,0},{1,65},{65,1},{2,66},{66,2},{3,67},{67,3},{4,68},{68... | collective-permute-start | bytes 2064392 | tf_op jit(solution)/shard_map/ppermute | solution.py:31
  19.0 9.7 %shard_map.59.refs_1_ = bf16[8,4,384,256]{3,2,1,0:T(8,128)(2,1)} custom-call(s32[1]{0:T(128)} %bitcast.m_ref, bf16[768,896]{1,0:T(8,128)(2,1)S(1)} %bitcast.79, bf16[768,896]{1,0:T(8,128)(2,1)S(1)} %collective-permute-done.h1_ref, bf16[896,2048]{1,0:T(8,128)(2,1)} %bitcast.84, bf16[24,2048]{1,0:T(8,128)(2,1)S(1)} %get-tuple-element.41.r0_ref, ...), custom_call_target="tpu_custom_call" | custom-call | flops 112742891520 | bytes 12713984 | tf_op jit(solution)/shard_map/pallas_call | solution.py:90
  28.6 7.6 %collective-permute-done.7.refs_2_ = bf16[2,24,2048]{2,1,0:T(8,128)(2,1)} collective-permute-done((bf16[2,24,2048]{2,1,0:T(8,128)(2,1)}, bf16[2,24,2048]{2,1,0:T(8,128)(2,1)}, u32[]{:S(2)}, u32[]{:S(2)}) %collective-permute-start.7) | collective-permute-done | bytes 196640 | tf_op jit(solution)/shard_map/ppermute | solution.py:31
  37.1 2.1 %collective-permute-start.21 = (bf16[384,896]{1,0:T(8,128)(2,1)}, bf16[384,896]{1,0:T(8,128)(2,1)S(1)}, u32[]{:S(2)}, u32[]{:S(2)}) collective-permute-start(bf16[384,896]{1,0:T(8,128)(2,1)} %shard_map.62), channel_id=1, source_target_pairs={{0,64},{64,0},{1,65},{65,1},{2,66},{66,2},{3,67},{67,3},{4,68},{68... | collective-permute-start | bytes 2064392 | tf_op jit(solution)/shard_map/ppermute | solution.py:31
  40.2 7.8 %shard_map.61 = (bf16[4,192,256]{2,1,0:T(8,128)(2,1)S(1)}, bf16[4,192,256]{2,1,0:T(8,128)(2,1)S(1)}, bf16[3,8,192,256]{3,2,1,0:T(8,128)(2,1)}) custom-call(s32[1]{0:T(128)} %bitcast.m_ref, bf16[384,896]{1,0:T(8,128)(2,1)S(1)} %copy-done.5, bf16[384,896]{1,0:T(8,128)(2,1)S(1)} %collective-permute-done.8.h1_ref, bf16[896,2048]{1,0:T(8,128)(2,1)} %bitcast.85, ...), custom_call_target="tpu_custom_call" | custom-call | flops 2818572288 | bytes 8192000 | tf_op jit(solution)/shard_map/pallas_call | solution.py:90
  49.3 1.9 collective-permute-start.11
  51.2 5.5 %collective-permute-done.21.refs_0_ = bf16[384,896]{1,0:T(8,128)(2,1)S(1)} collective-permute-done((bf16[384,896]{1,0:T(8,128)(2,1)}, bf16[384,896]{1,0:T(8,128)(2,1)S(1)}, u32[]{:S(2)}, u32[]{:S(2)}) %collective-permute-start.21) | collective-permute-done | bytes 688160 | tf_op jit(solution)/shard_map/ppermute | solution.py:31
  58.7 1.7 collective-permute-done.9
  61.7 3.0 %collective-permute-start.12 = (bf16[8,192,256]{2,1,0:T(8,128)(2,1)S(1)}, bf16[8,192,256]{2,1,0:T(8,128)(2,1)S(1)}, u32[]{:S(2)}, u32[]{:S(2)}) collective-permute-start(bf16[8,192,256]{2,1,0:T(8,128)(2,1)S(1)} %pad_maximum_fusion.1), channel_id=1, source_target_pairs={{0,24},{8,0},{16,8},{24,16},{1,25},{9,1},{17,9},{25,17},{2,26},{10... | collective-permute-start | bytes 2359304 | tf_op jit(solution)/shard_map/ppermute | solution.py:26
  64.9 7.4 %shard_map.64 = (bf16[4,192,256]{2,1,0:T(8,128)(2,1)S(1)}, bf16[4,192,256]{2,1,0:T(8,128)(2,1)S(1)}, bf16[3,8,192,256]{3,2,1,0:T(8,128)(2,1)}) custom-call(s32[1]{0:T(128)} %bitcast.m_ref, bf16[384,896]{1,0:T(8,128)(2,1)S(1)} %copy-done.2, bf16[384,896]{1,0:T(8,128)(2,1)S(1)} %collective-permute-done.22.h1_ref, bf16[896,2048]{1,0:T(8,128)(2,1)} %bitcast.86, ...), custom_call_target="tpu_custom_call" | custom-call | flops 2818572288 | bytes 8192000 | tf_op jit(solution)/shard_map/pallas_call | solution.py:90
  73.4 2.5 %collective-permute-start.25 = (bf16[4,192,256]{2,1,0:T(8,128)(2,1)S(1)}, bf16[4,192,256]{2,1,0:T(8,128)(2,1)S(1)}, u32[]{:S(2)}, u32[]{:S(2)}) collective-permute-start(bf16[4,192,256]{2,1,0:T(8,128)(2,1)S(1)} %get-tuple-element.13), channel_id=1, source_target_pairs={{0,24},{8,0},{16,8},{24,16},{1,25},{9,1},{17,9},{25,17},{2,26},{10... | collective-permute-start | bytes 1179656 | tf_op jit(solution)/shard_map/ppermute | solution.py:26
  75.9 2.1 %slice_bitcast_fusion.refs_0_ = bf16[8,192,256]{2,1,0:T(8,128)(2,1)} fusion(bf16[3,8,192,256]{3,2,1,0:T(8,128)(2,1)} %get-tuple-element.11), kind=kLoop, calls=%fused_computation.10 | loop fusion | bytes 1572864 | tf_op jit(solution)/shard_map/unstack | solution.py:200
  79.2 13.8 %collective-permute-done.23 = bf16[4,192,256]{2,1,0:T(8,128)(2,1)S(1)} collective-permute-done((bf16[4,192,256]{2,1,0:T(8,128)(2,1)S(1)}, bf16[4,192,256]{2,1,0:T(8,128)(2,1)S(1)}, u32[]{:S(2)}, u32[]{:S(2)}) %collective-permute-start.23) | collective-permute-done | bytes 393248 | tf_op jit(solution)/shard_map/ppermute | solution.py:26
  94.5 2.0 %collective-permute-start.24 = (bf16[8,192,256]{2,1,0:T(8,128)(2,1)S(1)}, bf16[8,192,256]{2,1,0:T(8,128)(2,1)}, u32[]{:S(2)}, u32[]{:S(2)}) collective-permute-start(bf16[8,192,256]{2,1,0:T(8,128)(2,1)S(1)} %pad_maximum_fusion.2), channel_id=1, source_target_pairs={{0,8},{8,16},{16,24},{24,0},{1,9},{9,17},{17,25},{25,1},{2,10},{10... | collective-permute-start | bytes 2359304 | tf_op jit(solution)/shard_map/ppermute | solution.py:26
  98.0 1.8 collective-permute-start.13
  99.9 4.4 %collective-permute-start.17 = (bf16[192,128]{1,0:T(8,128)(2,1)S(1)}, bf16[192,128]{1,0:T(8,128)(2,1)S(1)}, u32[]{:S(2)}, u32[]{:S(2)}) collective-permute-start(bf16[192,128]{1,0:T(8,128)(2,1)S(1)} %get-tuple-element.50), channel_id=1, source_target_pairs={{0,7},{1,0},{2,1},{3,2},{4,3},{5,4},{6,5},{7,6},{8,15},{9,8},{10,9... | collective-permute-start | bytes 147464 | tf_op jit(solution)/shard_map/ppermute | solution.py:26
  104.2 2.5 %collective-permute-done.13 = bf16[192,128]{1,0:T(8,128)(2,1)S(1)} collective-permute-done((bf16[192,128]{1,0:T(8,128)(2,1)S(1)}, bf16[192,128]{1,0:T(8,128)(2,1)S(1)}, u32[]{:S(2)}, u32[]{:S(2)}) %collective-permute-start.13) | collective-permute-done | bytes 49184 | tf_op jit(solution)/shard_map/ppermute | solution.py:26
  106.8 3.3 %collective-permute-start.18 = (bf16[192,256]{1,0:T(8,128)(2,1)S(1)}, bf16[192,256]{1,0:T(8,128)(2,1)S(1)}, u32[]{:S(2)}, u32[]{:S(2)}) collective-permute-start(bf16[192,256]{1,0:T(8,128)(2,1)S(1)} %pad_maximum_fusion.11), channel_id=1, source_target_pairs={{0,7},{1,0},{2,1},{3,2},{4,3},{5,4},{6,5},{7,6},{8,15},{9,8},{10,9... | collective-permute-start | bytes 294920 | tf_op jit(solution)/shard_map/ppermute | solution.py:26
  110.1 2.5 %collective-permute-done.14 = bf16[192,256]{1,0:T(8,128)(2,1)S(1)} collective-permute-done((bf16[192,256]{1,0:T(8,128)(2,1)S(1)}, bf16[192,256]{1,0:T(8,128)(2,1)S(1)}, u32[]{:S(2)}, u32[]{:S(2)}) %collective-permute-start.14) | collective-permute-done | bytes 98336 | tf_op jit(solution)/shard_map/ppermute | solution.py:26
  113.6 2.3 %add_convert_fusion = bf16[8,192,256]{2,1,0:T(8,128)(2,1)} fusion(bf16[8,192,256]{2,1,0:T(8,128)(2,1)S(1)} %collective-permute-done.26, bf16[8,192,256]{2,1,0:T(8,128)(2,1)} %collective-permute-done.24, bf16[8,192,256]{2,1,0:T(8,128)(2,1)S(1)} %copy-done.6), kind=kLoop, calls=%fused_computation.3 | loop fusion | flops 2359296 | bytes 3145728 | tf_op jit(solution)/shard_map/convert_element_type | solution.py:150
  116.0 8.3 %all-to-all-start = ((bf16[8,192,256]{2,1,0:T(8,128)(2,1)}), bf16[8,192,256]{2,1,0:T(8,128)(2,1)S(1)}, u32[]{:S(2)}, u32[]{:S(2)}) async-start(bf16[8,192,256]{2,1,0:T(8,128)(2,1)} %add_convert_fusion), calls=%async_computation.1 | async-start | bytes 1572864 | tf_op jit(solution)/shard_map/all_to_all | solution.py:206
  124.3 2.1 %collective-permute-start.16 = (bf16[192,256]{1,0:T(8,128)(2,1)S(1)}, bf16[192,256]{1,0:T(8,128)(2,1)S(1)}, u32[]{:S(2)}, u32[]{:S(2)}) collective-permute-start(bf16[192,256]{1,0:T(8,128)(2,1)S(1)} %get-tuple-element.32), channel_id=1, source_target_pairs={{0,1},{1,2},{2,3},{3,4},{4,5},{5,6},{6,7},{7,0},{8,9},{9,10},{10,1... | collective-permute-start | bytes 294920 | tf_op jit(solution)/shard_map/ppermute | solution.py:26
  129.3 2.8 %collective-permute-start.4 = (bf16[192,256]{1,0:T(8,128)(2,1)S(1)}, bf16[192,256]{1,0:T(8,128)(2,1)S(1)}, u32[]{:S(2)}, u32[]{:S(2)}) collective-permute-start(bf16[192,256]{1,0:T(8,128)(2,1)S(1)} %get-tuple-element.30), channel_id=1, source_target_pairs={{0,24},{8,0},{16,8},{24,16},{1,25},{9,1},{17,9},{25,17},{2,26},{10... | collective-permute-start | bytes 294920 | tf_op jit(solution)/shard_map/ppermute | solution.py:26
  132.1 11.8 %collective-permute-done.19 = bf16[192,256]{1,0:T(8,128)(2,1)S(1)} collective-permute-done((bf16[192,256]{1,0:T(8,128)(2,1)S(1)}, bf16[192,256]{1,0:T(8,128)(2,1)S(1)}, u32[]{:S(2)}, u32[]{:S(2)}) %collective-permute-start.19) | collective-permute-done | bytes 98336 | tf_op jit(solution)/shard_map/ppermute | solution.py:26
  145.5 2.0 %collective-permute-start.3 = (bf16[384,256]{1,0:T(8,128)(2,1)S(1)}, bf16[384,256]{1,0:T(8,128)(2,1)S(1)}, u32[]{:S(2)}, u32[]{:S(2)}) collective-permute-start(bf16[384,256]{1,0:T(8,128)(2,1)S(1)} %pad_maximum_fusion.6), channel_id=1, source_target_pairs={{0,8},{8,16},{16,24},{24,0},{1,9},{9,17},{17,25},{25,1},{2,10},{10... | collective-permute-start | bytes 589832 | tf_op jit(solution)/shard_map/ppermute | solution.py:26
  148.8 2.0 %collective-permute-done.5 = bf16[384,256]{1,0:T(8,128)(2,1)S(1)} collective-permute-done((bf16[384,256]{1,0:T(8,128)(2,1)S(1)}, bf16[384,256]{1,0:T(8,128)(2,1)S(1)}, u32[]{:S(2)}, u32[]{:S(2)}) %collective-permute-start.5) | collective-permute-done | bytes 196640 | tf_op jit(solution)/shard_map/ppermute | solution.py:26
  150.8 1.8 collective-permute-done.3
  153.8 2.7 %collective-permute-start.27 = (bf16[384,256]{1,0:T(8,128)(2,1)S(1)}, bf16[384,256]{1,0:T(8,128)(2,1)S(1)}, u32[]{:S(2)}, u32[]{:S(2)}) collective-permute-start(bf16[384,256]{1,0:T(8,128)(2,1)S(1)} %get-tuple-element.14), channel_id=1, source_target_pairs={{0,192},{1,193},{2,194},{3,195},{4,196},{5,197},{6,198},{7,199},{8... | collective-permute-start | bytes 589832 | tf_op jit(solution)/shard_map/ppermute | solution.py:170
  158.0 2.5 %collective-permute-done.27 = bf16[384,256]{1,0:T(8,128)(2,1)S(1)} collective-permute-done((bf16[384,256]{1,0:T(8,128)(2,1)S(1)}, bf16[384,256]{1,0:T(8,128)(2,1)S(1)}, u32[]{:S(2)}, u32[]{:S(2)}) %collective-permute-start.27) | collective-permute-done | bytes 196640 | tf_op jit(solution)/shard_map/ppermute | solution.py:170
  163.0 12.2 %all-to-all-start.1 = ((f32[32,1,768]{2,1,0:T(1,128)}), f32[32,1,768]{2,1,0:T(1,128)S(1)}, u32[]{:S(2)}, u32[]{:S(2)}) async-start(f32[32,1,768]{2,1,0:T(1,128)} %broadcast_in_dim.9), calls=%async_computation.2 | async-start | bytes 196608 | tf_op jit(solution)/shard_map/all_to_all | solution.py:212
  176.0 9.8 %all-to-all-done.1 = f32[32,1,768]{2,1,0:T(1,128)S(1)} async-done(((f32[32,1,768]{2,1,0:T(1,128)}), f32[32,1,768]{2,1,0:T(1,128)S(1)}, u32[]{:S(2)}, u32[]{:S(2)}) %all-to-all-start.1) | async-done | bytes 98336 | tf_op jit(solution)/shard_map/all_to_all | solution.py:212
  (101 shorter events, 32.8 us)
Async XLA Ops:
  7.2 120.6 %reduce-scatter.2.cloned.1.call-start = ((), (), s32[]{:S(2)}) async-start(), calls=%async_computation.3 | async-start | bytes 7077888 | tf_op jit(solution)/shard_map/reduce_scatter | solution.py:154
  7.2 11.7 %collective-permute-start = (bf16[768,896]{1,0:T(8,128)(2,1)}, bf16[768,896]{1,0:T(8,128)(2,1)S(1)}, u32[]{:S(2)}, u32[]{:S(2)}) collective-permute-start(bf16[768,896]{1,0:T(8,128)(2,1)} %bitcast.77), channel_id=1, source_target_pairs={{0,32},{32,0},{1,33},{33,1},{2,34},{34,2},{3,35},{35,3},{4,36},{36... | collective-permute-start | bytes 4128776 | tf_op jit(solution)/shard_map/ppermute | solution.py:31
  9.7 5.2 %collective-permute-start.1 = (bf16[2,24,2048]{2,1,0:T(8,128)(2,1)}, bf16[2,24,2048]{2,1,0:T(8,128)(2,1)}, u32[]{:S(2)}, u32[]{:S(2)}) collective-permute-start(bf16[2,24,2048]{2,1,0:T(8,128)(2,1)} %pad_maximum_fusion.5), channel_id=1, source_target_pairs={{0,32},{32,0},{1,33},{33,1},{2,34},{34,2},{3,35},{35,3},{4,36},{36... | collective-permute-start | bytes 589832 | tf_op jit(solution)/shard_map/ppermute | solution.py:31
  12.8 23.4 %collective-permute-start.6 = (bf16[384,896]{1,0:T(8,128)(2,1)}, bf16[384,896]{1,0:T(8,128)(2,1)S(1)}, u32[]{:S(2)}, u32[]{:S(2)}) collective-permute-start(bf16[384,896]{1,0:T(8,128)(2,1)} %bitcast.13), channel_id=1, source_target_pairs={{0,64},{64,0},{1,65},{65,1},{2,66},{66,2},{3,67},{67,3},{4,68},{68... | collective-permute-start | bytes 2064392 | tf_op jit(solution)/shard_map/ppermute | solution.py:31
  17.5 18.7 %collective-permute-start.7 = (bf16[2,24,2048]{2,1,0:T(8,128)(2,1)}, bf16[2,24,2048]{2,1,0:T(8,128)(2,1)}, u32[]{:S(2)}, u32[]{:S(2)}) collective-permute-start(bf16[2,24,2048]{2,1,0:T(8,128)(2,1)} %pad_maximum_fusion.8), channel_id=1, source_target_pairs={{0,64},{64,0},{1,65},{65,1},{2,66},{66,2},{3,67},{67,3},{4,68},{68... | collective-permute-start | bytes 589832 | tf_op jit(solution)/shard_map/ppermute | solution.py:31
  37.1 3.1 %collective-permute-start.8 = (bf16[384,896]{1,0:T(8,128)(2,1)}, bf16[384,896]{1,0:T(8,128)(2,1)S(1)}, u32[]{:S(2)}, u32[]{:S(2)}) collective-permute-start(bf16[384,896]{1,0:T(8,128)(2,1)} %shard_map.60.h0_ref), channel_id=1, source_target_pairs={{0,32},{32,0},{1,33},{33,1},{2,34},{34,2},{3,35},{35,3},{4,36},{36... | collective-permute-start | bytes 2064392 | tf_op jit(solution)/shard_map/ppermute | solution.py:31
  37.1 19.6 %collective-permute-start.21 = (bf16[384,896]{1,0:T(8,128)(2,1)}, bf16[384,896]{1,0:T(8,128)(2,1)S(1)}, u32[]{:S(2)}, u32[]{:S(2)}) collective-permute-start(bf16[384,896]{1,0:T(8,128)(2,1)} %shard_map.62), channel_id=1, source_target_pairs={{0,64},{64,0},{1,65},{65,1},{2,66},{66,2},{3,67},{67,3},{4,68},{68... | collective-permute-start | bytes 2064392 | tf_op jit(solution)/shard_map/ppermute | solution.py:31
  48.0 12.4 %collective-permute-start.9 = (bf16[4,192,256]{2,1,0:T(8,128)(2,1)S(1)}, bf16[4,192,256]{2,1,0:T(8,128)(2,1)S(1)}, u32[]{:S(2)}, u32[]{:S(2)}) collective-permute-start(bf16[4,192,256]{2,1,0:T(8,128)(2,1)S(1)} %get-tuple-element.9), channel_id=1, source_target_pairs={{0,8},{8,16},{16,24},{24,0},{1,9},{9,17},{17,25},{25,1},{2,10},{10... | collective-permute-start | bytes 1179656 | tf_op jit(solution)/shard_map/ppermute | solution.py:26
  49.3 11.1 %collective-permute-start.11 = (bf16[4,192,256]{2,1,0:T(8,128)(2,1)S(1)}, bf16[4,192,256]{2,1,0:T(8,128)(2,1)S(1)}, u32[]{:S(2)}, u32[]{:S(2)}) collective-permute-start(bf16[4,192,256]{2,1,0:T(8,128)(2,1)S(1)} %get-tuple-element.10), channel_id=1, source_target_pairs={{0,24},{8,0},{16,8},{24,16},{1,25},{9,1},{17,9},{25,17},{2,26},{10... | collective-permute-start | bytes 1179656 | tf_op jit(solution)/shard_map/ppermute | solution.py:26
  57.5 7.4 %collective-permute-start.22 = (bf16[384,896]{1,0:T(8,128)(2,1)}, bf16[384,896]{1,0:T(8,128)(2,1)S(1)}, u32[]{:S(2)}, u32[]{:S(2)}) collective-permute-start(bf16[384,896]{1,0:T(8,128)(2,1)} %shard_map.63.h0_ref), channel_id=1, source_target_pairs={{0,32},{32,0},{1,33},{33,1},{2,34},{34,2},{3,35},{35,3},{4,36},{36... | collective-permute-start | bytes 2064392 | tf_op jit(solution)/shard_map/ppermute | solution.py:31
  61.7 34.7 %collective-permute-start.12 = (bf16[8,192,256]{2,1,0:T(8,128)(2,1)S(1)}, bf16[8,192,256]{2,1,0:T(8,128)(2,1)S(1)}, u32[]{:S(2)}, u32[]{:S(2)}) collective-permute-start(bf16[8,192,256]{2,1,0:T(8,128)(2,1)S(1)} %pad_maximum_fusion.1), channel_id=1, source_target_pairs={{0,24},{8,0},{16,8},{24,16},{1,25},{9,1},{17,9},{25,17},{2,26},{10... | collective-permute-start | bytes 2359304 | tf_op jit(solution)/shard_map/ppermute | solution.py:26
  64.8 31.6 %collective-permute-start.10 = (bf16[8,192,256]{2,1,0:T(8,128)(2,1)S(1)}, bf16[8,192,256]{2,1,0:T(8,128)(2,1)S(1)}, u32[]{:S(2)}, u32[]{:S(2)}) collective-permute-start(bf16[8,192,256]{2,1,0:T(8,128)(2,1)S(1)} %pad_maximum_fusion), channel_id=1, source_target_pairs={{0,8},{8,16},{16,24},{24,0},{1,9},{9,17},{17,25},{25,1},{2,10},{10... | collective-permute-start | bytes 2359304 | tf_op jit(solution)/shard_map/ppermute | solution.py:26
  72.4 20.5 %collective-permute-start.23 = (bf16[4,192,256]{2,1,0:T(8,128)(2,1)S(1)}, bf16[4,192,256]{2,1,0:T(8,128)(2,1)S(1)}, u32[]{:S(2)}, u32[]{:S(2)}) collective-permute-start(bf16[4,192,256]{2,1,0:T(8,128)(2,1)S(1)} %get-tuple-element.12), channel_id=1, source_target_pairs={{0,8},{8,16},{16,24},{24,0},{1,9},{9,17},{17,25},{25,1},{2,10},{10... | collective-permute-start | bytes 1179656 | tf_op jit(solution)/shard_map/ppermute | solution.py:26
  73.4 19.5 %collective-permute-start.25 = (bf16[4,192,256]{2,1,0:T(8,128)(2,1)S(1)}, bf16[4,192,256]{2,1,0:T(8,128)(2,1)S(1)}, u32[]{:S(2)}, u32[]{:S(2)}) collective-permute-start(bf16[4,192,256]{2,1,0:T(8,128)(2,1)S(1)} %get-tuple-element.13), channel_id=1, source_target_pairs={{0,24},{8,0},{16,8},{24,16},{1,25},{9,1},{17,9},{25,17},{2,26},{10... | collective-permute-start | bytes 1179656 | tf_op jit(solution)/shard_map/ppermute | solution.py:26
  94.2 19.4 %collective-permute-start.26 = (bf16[8,192,256]{2,1,0:T(8,128)(2,1)S(1)}, bf16[8,192,256]{2,1,0:T(8,128)(2,1)S(1)}, u32[]{:S(2)}, u32[]{:S(2)}) collective-permute-start(bf16[8,192,256]{2,1,0:T(8,128)(2,1)S(1)} %pad_maximum_fusion.3), channel_id=1, source_target_pairs={{0,24},{8,0},{16,8},{24,16},{1,25},{9,1},{17,9},{25,17},{2,26},{10... | collective-permute-start | bytes 2359304 | tf_op jit(solution)/shard_map/ppermute | solution.py:26
  94.5 19.1 %collective-permute-start.24 = (bf16[8,192,256]{2,1,0:T(8,128)(2,1)S(1)}, bf16[8,192,256]{2,1,0:T(8,128)(2,1)}, u32[]{:S(2)}, u32[]{:S(2)}) collective-permute-start(bf16[8,192,256]{2,1,0:T(8,128)(2,1)S(1)} %pad_maximum_fusion.2), channel_id=1, source_target_pairs={{0,8},{8,16},{16,24},{24,0},{1,9},{9,17},{17,25},{25,1},{2,10},{10... | collective-permute-start | bytes 2359304 | tf_op jit(solution)/shard_map/ppermute | solution.py:26
  98.0 8.7 %collective-permute-start.13 = (bf16[192,128]{1,0:T(8,128)(2,1)S(1)}, bf16[192,128]{1,0:T(8,128)(2,1)S(1)}, u32[]{:S(2)}, u32[]{:S(2)}) collective-permute-start(bf16[192,128]{1,0:T(8,128)(2,1)S(1)} %get-tuple-element.49), channel_id=1, source_target_pairs={{0,1},{1,2},{2,3},{3,4},{4,5},{5,6},{6,7},{7,0},{8,9},{9,10},{10,1... | collective-permute-start | bytes 147464 | tf_op jit(solution)/shard_map/ppermute | solution.py:26
  99.9 6.9 %collective-permute-start.17 = (bf16[192,128]{1,0:T(8,128)(2,1)S(1)}, bf16[192,128]{1,0:T(8,128)(2,1)S(1)}, u32[]{:S(2)}, u32[]{:S(2)}) collective-permute-start(bf16[192,128]{1,0:T(8,128)(2,1)S(1)} %get-tuple-element.50), channel_id=1, source_target_pairs={{0,7},{1,0},{2,1},{3,2},{4,3},{5,4},{6,5},{7,6},{8,15},{9,8},{10,9... | collective-permute-start | bytes 147464 | tf_op jit(solution)/shard_map/ppermute | solution.py:26
  106.7 5.9 %collective-permute-start.14 = (bf16[192,256]{1,0:T(8,128)(2,1)S(1)}, bf16[192,256]{1,0:T(8,128)(2,1)S(1)}, u32[]{:S(2)}, u32[]{:S(2)}) collective-permute-start(bf16[192,256]{1,0:T(8,128)(2,1)S(1)} %pad_maximum_fusion.10), channel_id=1, source_target_pairs={{0,1},{1,2},{2,3},{3,4},{4,5},{5,6},{6,7},{7,0},{8,9},{9,10},{10,1... | collective-permute-start | bytes 294920 | tf_op jit(solution)/shard_map/ppermute | solution.py:26
  106.8 17.4 %collective-permute-start.18 = (bf16[192,256]{1,0:T(8,128)(2,1)S(1)}, bf16[192,256]{1,0:T(8,128)(2,1)S(1)}, u32[]{:S(2)}, u32[]{:S(2)}) collective-permute-start(bf16[192,256]{1,0:T(8,128)(2,1)S(1)} %pad_maximum_fusion.11), channel_id=1, source_target_pairs={{0,7},{1,0},{2,1},{3,2},{4,3},{5,4},{6,5},{7,6},{8,15},{9,8},{10,9... | collective-permute-start | bytes 294920 | tf_op jit(solution)/shard_map/ppermute | solution.py:26
  113.5 10.8 %collective-permute-start.15 = (bf16[192,256]{1,0:T(8,128)(2,1)S(1)}, bf16[192,256]{1,0:T(8,128)(2,1)S(1)}, u32[]{:S(2)}, u32[]{:S(2)}) collective-permute-start(bf16[192,256]{1,0:T(8,128)(2,1)S(1)} %bitcast_add_fusion.6), channel_id=1, source_target_pairs={{0,1},{1,2},{2,3},{3,4},{4,5},{5,6},{6,7},{7,0},{8,9},{9,10},{10,1... | collective-permute-start | bytes 294920 | tf_op jit(solution)/shard_map/ppermute | solution.py:26
  116.0 32.7 %all-to-all-start = ((bf16[8,192,256]{2,1,0:T(8,128)(2,1)}), bf16[8,192,256]{2,1,0:T(8,128)(2,1)S(1)}, u32[]{:S(2)}, u32[]{:S(2)}) async-start(bf16[8,192,256]{2,1,0:T(8,128)(2,1)} %add_convert_fusion), calls=%async_computation.1 | async-start | bytes 1572864 | tf_op jit(solution)/shard_map/all_to_all | solution.py:206
  124.3 23.2 %collective-permute-start.16 = (bf16[192,256]{1,0:T(8,128)(2,1)S(1)}, bf16[192,256]{1,0:T(8,128)(2,1)S(1)}, u32[]{:S(2)}, u32[]{:S(2)}) collective-permute-start(bf16[192,256]{1,0:T(8,128)(2,1)S(1)} %get-tuple-element.32), channel_id=1, source_target_pairs={{0,1},{1,2},{2,3},{3,4},{4,5},{5,6},{6,7},{7,0},{8,9},{9,10},{10,1... | collective-permute-start | bytes 294920 | tf_op jit(solution)/shard_map/ppermute | solution.py:26
  126.4 17.5 %collective-permute-start.19 = (bf16[192,256]{1,0:T(8,128)(2,1)S(1)}, bf16[192,256]{1,0:T(8,128)(2,1)S(1)}, u32[]{:S(2)}, u32[]{:S(2)}) collective-permute-start(bf16[192,256]{1,0:T(8,128)(2,1)S(1)} %get-tuple-element.33), channel_id=1, source_target_pairs={{0,7},{1,0},{2,1},{3,2},{4,3},{5,4},{6,5},{7,6},{8,15},{9,8},{10,9... | collective-permute-start | bytes 294920 | tf_op jit(solution)/shard_map/ppermute | solution.py:26
  128.8 15.2 %collective-permute-start.2 = (bf16[192,256]{1,0:T(8,128)(2,1)S(1)}, bf16[192,256]{1,0:T(8,128)(2,1)S(1)}, u32[]{:S(2)}, u32[]{:S(2)}) collective-permute-start(bf16[192,256]{1,0:T(8,128)(2,1)S(1)} %get-tuple-element.28), channel_id=1, source_target_pairs={{0,8},{8,16},{16,24},{24,0},{1,9},{9,17},{17,25},{25,1},{2,10},{10... | collective-permute-start | bytes 294920 | tf_op jit(solution)/shard_map/ppermute | solution.py:26
  129.3 14.8 %collective-permute-start.4 = (bf16[192,256]{1,0:T(8,128)(2,1)S(1)}, bf16[192,256]{1,0:T(8,128)(2,1)S(1)}, u32[]{:S(2)}, u32[]{:S(2)}) collective-permute-start(bf16[192,256]{1,0:T(8,128)(2,1)S(1)} %get-tuple-element.30), channel_id=1, source_target_pairs={{0,24},{8,0},{16,8},{24,16},{1,25},{9,1},{17,9},{25,17},{2,26},{10... | collective-permute-start | bytes 294920 | tf_op jit(solution)/shard_map/ppermute | solution.py:26
  144.0 4.7 %collective-permute-start.20 = (bf16[192,256]{1,0:T(8,128)(2,1)S(1)}, bf16[192,256]{1,0:T(8,128)(2,1)S(1)}, u32[]{:S(2)}, u32[]{:S(2)}) collective-permute-start(bf16[192,256]{1,0:T(8,128)(2,1)S(1)} %bitcast_add_fusion.5), channel_id=1, source_target_pairs={{0,7},{1,0},{2,1},{3,2},{4,3},{5,4},{6,5},{7,6},{8,15},{9,8},{10,9... | collective-permute-start | bytes 294920 | tf_op jit(solution)/shard_map/ppermute | solution.py:26
  145.1 5.7 %collective-permute-start.5 = (bf16[384,256]{1,0:T(8,128)(2,1)S(1)}, bf16[384,256]{1,0:T(8,128)(2,1)S(1)}, u32[]{:S(2)}, u32[]{:S(2)}) collective-permute-start(bf16[384,256]{1,0:T(8,128)(2,1)S(1)} %pad_maximum_fusion.7), channel_id=1, source_target_pairs={{0,24},{8,0},{16,8},{24,16},{1,25},{9,1},{17,9},{25,17},{2,26},{10... | collective-permute-start | bytes 589832 | tf_op jit(solution)/shard_map/ppermute | solution.py:26
  145.5 7.2 %collective-permute-start.3 = (bf16[384,256]{1,0:T(8,128)(2,1)S(1)}, bf16[384,256]{1,0:T(8,128)(2,1)S(1)}, u32[]{:S(2)}, u32[]{:S(2)}) collective-permute-start(bf16[384,256]{1,0:T(8,128)(2,1)S(1)} %pad_maximum_fusion.6), channel_id=1, source_target_pairs={{0,8},{8,16},{16,24},{24,0},{1,9},{9,17},{17,25},{25,1},{2,10},{10... | collective-permute-start | bytes 589832 | tf_op jit(solution)/shard_map/ppermute | solution.py:26
  153.8 6.7 %collective-permute-start.27 = (bf16[384,256]{1,0:T(8,128)(2,1)S(1)}, bf16[384,256]{1,0:T(8,128)(2,1)S(1)}, u32[]{:S(2)}, u32[]{:S(2)}) collective-permute-start(bf16[384,256]{1,0:T(8,128)(2,1)S(1)} %get-tuple-element.14), channel_id=1, source_target_pairs={{0,192},{1,193},{2,194},{3,195},{4,196},{5,197},{6,198},{7,199},{8... | collective-permute-start | bytes 589832 | tf_op jit(solution)/shard_map/ppermute | solution.py:170
  156.4 5.7 %collective-permute-start.28 = (bf16[384,256]{1,0:T(8,128)(2,1)S(1)}, bf16[384,256]{1,0:T(8,128)(2,1)S(1)}, u32[]{:S(2)}, u32[]{:S(2)}) collective-permute-start(bf16[384,256]{1,0:T(8,128)(2,1)S(1)} %broadcast_select_fusion), channel_id=1, source_target_pairs={{0,128},{1,129},{2,130},{3,131},{4,132},{5,133},{6,134},{7,135},{8... | collective-permute-start | bytes 589832 | tf_op jit(solution)/shard_map/ppermute | solution.py:169
  163.0 22.8 %all-to-all-start.1 = ((f32[32,1,768]{2,1,0:T(1,128)}), f32[32,1,768]{2,1,0:T(1,128)S(1)}, u32[]{:S(2)}, u32[]{:S(2)}) async-start(f32[32,1,768]{2,1,0:T(1,128)} %broadcast_in_dim.9), calls=%async_computation.2 | async-start | bytes 196608 | tf_op jit(solution)/shard_map/all_to_all | solution.py:212
  (10 other events, 76.1 us)
Sparse Core Ops, SparseCore 0:
  28.8 78.8 reduce-scatter.1

commit v7 on v3

--- a/solution.py
+++ b/solution.py
@@ -16,7 +16,7 @@
 ORDER = ((0, 192), (192, HALF))
 TIE = 3 * 10**11
 SCALE, FAR = 20, 1
-VMEM = 58 * 2**20
+VMEM = 50 * 2**20
 AXES = ("s", "xh", "c", "y", "z")
 F32, BF16 = jnp.float32, jnp.bfloat16
 

time: 183 us -> 184 us (level)
  waiting for transfers between devices: 60.4 us -> 64 us
  starting transfers between devices: 50.9 us -> 53.8 us
  Pallas kernels: 25.1 us -> 23.2 us
    all_to_all x1, starting transfers between devices: 7.48 us -> 11.4 us  [shards(): lax.all_to_all(jnp.broadcast_to(squares, (NY * NZ, 768)), ('y', 'z'), spl...]
    ppermute x7, waiting for transfers between devices: 10.1 us -> 12.8 us  [flipped(): return lax.ppermute(x, axes, [(i, n - 1 - i) for i in range(n)])]
    pallas_call x3, Pallas kernels: 25.1 us -> 23.2 us  [product(): pl.pallas_call(functools.partial(product_kernel, first, rows, y_major), o...]
    unnamed x20 -> x18, local copies, waits for them, and re-layouts: 4.59 us -> 3.27 us
  transfers between devices with their start and end apart: 25 -> 25, of which waited for: 14 -> 13; matrix products, arithmetic and copies ran while one was open for 13% -> 12% of each run, Pallas kernels for 14% -> 13%
where the time goes in v7:
time: 184 us; the launch traced here: 183 us
  waiting for transfers between devices  64 us (35%)
  starting transfers between devices  53.8 us (29%)
  Pallas kernels  23.2 us (13%)
  local copies, waits for them, and re-layouts  14.8 us (8%)
  between operations  14.3 us (8%)
  other arithmetic  12.7 us (7%)
    ppermute x12, waiting for transfers between devices, shifted(): return lax.ppermute(x, axis, [(i, (i + by) % n) for i in range(n)])  25.4 us
    pallas_call x3, Pallas kernels, product(): pl.pallas_call(functools.partial(product_kernel, first, rows, y_major), o...  23.2 us
    ppermute x12, starting transfers between devices, shifted(): return lax.ppermute(x, axis, [(i, (i + by) % n) for i in range(n)])  19.8 us
    all_to_all x2, waiting for transfers between devices, shards(): x = lax.all_to_all(x, 'z', split_axis=0, concat_axis=0, tiled=True)  13.1 us
    ppermute x7, waiting for transfers between devices, flipped(): return lax.ppermute(x, axes, [(i, n - 1 - i) for i in range(n)])  12.8 us
    all_to_all x2, starting transfers between devices, shards(): x = lax.all_to_all(x, 'z', split_axis=0, concat_axis=0, tiled=True)  12.1 us
    all_to_all x1, starting transfers between devices, shards(): lax.all_to_all(jnp.broadcast_to(squares, (NY * NZ, 768)), ('y', 'z'), spl...  11.4 us
    all_to_all x1, waiting for transfers between devices, shards(): lax.all_to_all(jnp.broadcast_to(squares, (NY * NZ, 768)), ('y', 'z'), spl...  9.37 us
  transfers between devices with their start and end apart: 25, of which 13 were waited for; matrix products, arithmetic and copies ran while one was open for 12% of the time, Pallas kernels for 13%

profile of v7, /device:TPU:2, one launch (start us, length us, event | category | flops | bytes accessed | tf_op | source)
XLA Modules:
  0.0 182.8 jit_solution(782651795509356170)
XLA Ops:
  7.3 1.7 constant_dynamic-slice_fusion
  10.2 2.6 %fusion.14 = (bf16[2,192,896]{2,1,0:T(8,128)(2,1)}, bf16[2,192,896]{2,1,0:T(8,128)(2,1)}) fusion(bf16[2,384,896]{2,1,0:T(8,128)(2,1)} %bitcast.78), kind=kLoop, calls=%fused_computation.58 | loop fusion | bytes 2752512 | tf_op jit(solution)/shard_map/slice | solution.py:153
  12.8 2.1 %collective-permute-start.6 = (bf16[384,896]{1,0:T(8,128)(2,1)}, bf16[384,896]{1,0:T(8,128)(2,1)S(1)}, u32[]{:S(2)}, u32[]{:S(2)}) collective-permute-start(bf16[384,896]{1,0:T(8,128)(2,1)} %bitcast.13), channel_id=1, source_target_pairs={{0,64},{64,0},{1,65},{65,1},{2,66},{66,2},{3,67},{67,3},{4,68},{68... | collective-permute-start | bytes 2064392 | tf_op jit(solution)/shard_map/ppermute | solution.py:30
  16.5 9.7 %shard_map.59.refs_1_ = bf16[8,4,384,256]{3,2,1,0:T(8,128)(2,1)} custom-call(s32[1]{0:T(128)} %bitcast.m_ref, bf16[768,896]{1,0:T(8,128)(2,1)S(1)} %bitcast.79, bf16[768,896]{1,0:T(8,128)(2,1)S(1)} %collective-permute-done.h1_ref, bf16[896,2048]{1,0:T(8,128)(2,1)} %bitcast.84, bf16[24,2048]{1,0:T(8,128)(2,1)S(1)} %get-tuple-element.28.r0_ref, ...), custom_call_target="tpu_custom_call" | custom-call | flops 112742891520 | bytes 12713984 | tf_op jit(solution)/shard_map/pallas_call | solution.py:69
  26.9 5.0 %collective-permute-done.6.refs_0_ = bf16[384,896]{1,0:T(8,128)(2,1)S(1)} collective-permute-done((bf16[384,896]{1,0:T(8,128)(2,1)}, bf16[384,896]{1,0:T(8,128)(2,1)S(1)}, u32[]{:S(2)}, u32[]{:S(2)}) %collective-permute-start.6) | collective-permute-done | bytes 688160 | tf_op jit(solution)/shard_map/ppermute | solution.py:30
  33.7 2.2 %collective-permute-start.8 = (bf16[2,24,2048]{2,1,0:T(8,128)(2,1)S(1)}, bf16[2,24,2048]{2,1,0:T(8,128)(2,1)S(1)}, u32[]{:S(2)}, u32[]{:S(2)}) collective-permute-start(bf16[2,24,2048]{2,1,0:T(8,128)(2,1)S(1)} %pad_maximum_fusion.8), channel_id=1, source_target_pairs={{0,64},{64,0},{1,65},{65,1},{2,66},{66,2},{3,67},{67,3},{4,68},{68... | collective-permute-start | bytes 589832 | tf_op jit(solution)/shard_map/ppermute | solution.py:30
  37.3 5.8 %collective-permute-done.8 = bf16[2,24,2048]{2,1,0:T(8,128)(2,1)S(1)} collective-permute-done((bf16[2,24,2048]{2,1,0:T(8,128)(2,1)S(1)}, bf16[2,24,2048]{2,1,0:T(8,128)(2,1)S(1)}, u32[]{:S(2)}, u32[]{:S(2)}) %collective-permute-start.8) | collective-permute-done | bytes 196640 | tf_op jit(solution)/shard_map/ppermute | solution.py:30
  43.2 6.8 %shard_map.61.refs_1_ = bf16[4,8,192,256]{3,2,1,0:T(8,128)(2,1)} custom-call(s32[1]{0:T(128)} %bitcast.m_ref, bf16[384,896]{1,0:T(8,128)(2,1)S(1)} %copy-done.5, bf16[384,896]{1,0:T(8,128)(2,1)S(1)} %collective-permute-done.7.h1_ref, bf16[896,2048]{1,0:T(8,128)(2,1)} %bitcast.85, bf16[24,2048]{1,0:T(8,128)(2,1)S(1)} %get-tuple-element.31.r0_ref, ...), custom_call_target="tpu_custom_call" | custom-call | flops 2818572288 | bytes 8192000 | tf_op jit(solution)/shard_map/pallas_call | solution.py:69
  51.4 3.0 %collective-permute-start.11 = (bf16[4,192,256]{2,1,0:T(8,128)(2,1)S(1)}, bf16[4,192,256]{2,1,0:T(8,128)(2,1)S(1)}, u32[]{:S(2)}, u32[]{:S(2)}) collective-permute-start(bf16[4,192,256]{2,1,0:T(8,128)(2,1)S(1)} %get-tuple-element.8), channel_id=1, source_target_pairs={{0,24},{8,0},{16,8},{24,16},{1,25},{9,1},{17,9},{25,17},{2,26},{10... | collective-permute-start | bytes 1179656 | tf_op jit(solution)/shard_map/ppermute | solution.py:25
  54.4 2.0 %collective-permute-done.13.refs_0_ = bf16[384,896]{1,0:T(8,128)(2,1)S(1)} collective-permute-done((bf16[384,896]{1,0:T(8,128)(2,1)}, bf16[384,896]{1,0:T(8,128)(2,1)S(1)}, u32[]{:S(2)}, u32[]{:S(2)}) %collective-permute-start.13) | collective-permute-done | bytes 688160 | tf_op jit(solution)/shard_map/ppermute | solution.py:30
  57.3 3.0 %collective-permute-done.11 = bf16[4,192,256]{2,1,0:T(8,128)(2,1)S(1)} collective-permute-done((bf16[4,192,256]{2,1,0:T(8,128)(2,1)S(1)}, bf16[4,192,256]{2,1,0:T(8,128)(2,1)S(1)}, u32[]{:S(2)}, u32[]{:S(2)}) %collective-permute-start.11) | collective-permute-done | bytes 393248 | tf_op jit(solution)/shard_map/ppermute | solution.py:25
  60.3 3.4 %collective-permute-done.9 = bf16[4,192,256]{2,1,0:T(8,128)(2,1)S(1)} collective-permute-done((bf16[4,192,256]{2,1,0:T(8,128)(2,1)S(1)}, bf16[4,192,256]{2,1,0:T(8,128)(2,1)S(1)}, u32[]{:S(2)}, u32[]{:S(2)}) %collective-permute-start.9) | collective-permute-done | bytes 393248 | tf_op jit(solution)/shard_map/ppermute | solution.py:25
  65.2 3.3 %collective-permute-start.12 = (bf16[8,192,256]{2,1,0:T(8,128)(2,1)S(1)}, bf16[8,192,256]{2,1,0:T(8,128)(2,1)S(1)}, u32[]{:S(2)}, u32[]{:S(2)}) collective-permute-start(bf16[8,192,256]{2,1,0:T(8,128)(2,1)S(1)} %pad_maximum_fusion.1), channel_id=1, source_target_pairs={{0,24},{8,0},{16,8},{24,16},{1,25},{9,1},{17,9},{25,17},{2,26},{10... | collective-permute-start | bytes 2359304 | tf_op jit(solution)/shard_map/ppermute | solution.py:25
  68.5 6.7 %shard_map.64 = bf16[4,8,192,256]{3,2,1,0:T(8,128)(2,1)} custom-call(s32[1]{0:T(128)} %bitcast.m_ref, bf16[384,896]{1,0:T(8,128)(2,1)S(1)} %copy-done.2, bf16[384,896]{1,0:T(8,128)(2,1)S(1)} %collective-permute-done.14.h1_ref, bf16[896,2048]{1,0:T(8,128)(2,1)} %bitcast.86, bf16[24,2048]{1,0:T(8,128)(2,1)S(1)} %get-tuple-element.31.r0_ref, ...), custom_call_target="tpu_custom_call" | custom-call | flops 2818572288 | bytes 8192000 | tf_op jit(solution)/shard_map/pallas_call | solution.py:69
  75.1 2.4 %dynamic-slice_bitcast_fusion.4 = (bf16[4,192,256]{2,1,0:T(8,128)(2,1)}, bf16[4,192,256]{2,1,0:T(8,128)(2,1)S(1)}, bf16[4,192,256]{2,1,0:T(8,128)(2,1)}, bf16[4,192,256]{2,1,0:T(8,128)(2,1)S(1)}) fusion(bf16[4,8,192,256]{3,2,1,0:T(8,128)(2,1)} %shard_map.64, s32[]{:T(128)S(6)} %select_n.106, s32[]{:T(128)S(6)} %select_n.108, s32[]{:T(128)S(6)} %add.162, ...), kind=kLoop, calls=%fused_computation.17 | loop fusion | bytes 3145744 | tf_op jit(solution)/shard_map/slice | solution.py:108
  77.5 3.2 %collective-permute-start.17 = (bf16[4,192,256]{2,1,0:T(8,128)(2,1)}, bf16[4,192,256]{2,1,0:T(8,128)(2,1)}, u32[]{:S(2)}, u32[]{:S(2)}) collective-permute-start(bf16[4,192,256]{2,1,0:T(8,128)(2,1)} %get-tuple-element.14), channel_id=1, source_target_pairs={{0,24},{8,0},{16,8},{24,16},{1,25},{9,1},{17,9},{25,17},{2,26},{10... | collective-permute-start | bytes 1179656 | tf_op jit(solution)/shard_map/ppermute | solution.py:25
  80.7 5.5 %collective-permute-done.10 = bf16[8,192,256]{2,1,0:T(8,128)(2,1)} collective-permute-done((bf16[8,192,256]{2,1,0:T(8,128)(2,1)S(1)}, bf16[8,192,256]{2,1,0:T(8,128)(2,1)}, u32[]{:S(2)}, u32[]{:S(2)}) %collective-permute-start.10) | collective-permute-done | bytes 786464 | tf_op jit(solution)/shard_map/ppermute | solution.py:25
  86.2 2.6 %fusion.3 = bf16[8,192,256]{2,1,0:T(8,128)(2,1)} fusion(bf16[8,192,256]{2,1,0:T(8,128)(2,1)S(1)} %collective-permute-done.12, bf16[8,192,256]{2,1,0:T(8,128)(2,1)} %collective-permute-done.10, bf16[4,8,192,256]{3,2,1,0:T(8,128)(2,1)} %shard_map.61.refs_1_, s32[]{:T(128)S(6)} %select_n.102), kind=kLoop, calls=%fused_computation.5 | loop fusion | flops 2359296 | bytes 3145732 | tf_op jit(solution)/shard_map/convert_element_type | solution.py:157
  88.8 8.5 %all-to-all-start = ((bf16[8,192,256]{2,1,0:T(8,128)(2,1)}), bf16[8,192,256]{2,1,0:T(8,128)(2,1)S(1)}, u32[]{:S(2)}, u32[]{:S(2)}) async-start(bf16[8,192,256]{2,1,0:T(8,128)(2,1)} %fusion.3), calls=%async_computation.1 | async-start | bytes 1572864 | tf_op jit(solution)/shard_map/all_to_all | solution.py:158
  98.9 3.3 %collective-permute-start.18 = (bf16[8,192,256]{2,1,0:T(8,128)(2,1)S(1)}, bf16[8,192,256]{2,1,0:T(8,128)(2,1)S(1)}, u32[]{:S(2)}, u32[]{:S(2)}) collective-permute-start(bf16[8,192,256]{2,1,0:T(8,128)(2,1)S(1)} %pad_maximum_fusion.3), channel_id=1, source_target_pairs={{0,24},{8,0},{16,8},{24,16},{1,25},{9,1},{17,9},{25,17},{2,26},{10... | collective-permute-start | bytes 2359304 | tf_op jit(solution)/shard_map/ppermute | solution.py:25
  102.2 9.8 %collective-permute-done.16 = bf16[8,192,256]{2,1,0:T(8,128)(2,1)S(1)} collective-permute-done((bf16[8,192,256]{2,1,0:T(8,128)(2,1)S(1)}, bf16[8,192,256]{2,1,0:T(8,128)(2,1)S(1)}, u32[]{:S(2)}, u32[]{:S(2)}) %collective-permute-start.16) | collective-permute-done | bytes 786464 | tf_op jit(solution)/shard_map/ppermute | solution.py:25
  112.0 2.3 %fusion.1 = bf16[8,192,256]{2,1,0:T(8,128)(2,1)} fusion(bf16[8,192,256]{2,1,0:T(8,128)(2,1)S(1)} %collective-permute-done.18, bf16[8,192,256]{2,1,0:T(8,128)(2,1)S(1)} %collective-permute-done.16, bf16[4,8,192,256]{3,2,1,0:T(8,128)(2,1)} %shard_map.64, s32[]{:T(128)S(6)} %select_n.102), kind=kLoop, calls=%fused_computation.2 | loop fusion | flops 2359296 | bytes 3145732 | tf_op jit(solution)/shard_map/convert_element_type | solution.py:157
  114.4 7.8 %all-to-all-done = bf16[8,192,256]{2,1,0:T(8,128)(2,1)S(1)} async-done(((bf16[8,192,256]{2,1,0:T(8,128)(2,1)}), bf16[8,192,256]{2,1,0:T(8,128)(2,1)S(1)}, u32[]{:S(2)}, u32[]{:S(2)}) %all-to-all-start) | async-done | bytes 786464 | tf_op jit(solution)/shard_map/all_to_all | solution.py:158
  122.2 3.5 %all-to-all-start.1 = ((bf16[8,192,256]{2,1,0:T(8,128)(2,1)}), bf16[8,192,256]{2,1,0:T(8,128)(2,1)S(1)}, u32[]{:S(2)}, u32[]{:S(2)}) async-start(bf16[8,192,256]{2,1,0:T(8,128)(2,1)} %fusion.1), calls=%async_computation.2 | async-start | bytes 1572864 | tf_op jit(solution)/shard_map/all_to_all | solution.py:158
  128.4 1.8 collective-permute-start.4
  130.2 3.6 %collective-permute-done.2 = bf16[192,256]{1,0:T(8,128)(2,1)S(1)} collective-permute-done((bf16[192,256]{1,0:T(8,128)(2,1)S(1)}, bf16[192,256]{1,0:T(8,128)(2,1)S(1)}, u32[]{:S(2)}, u32[]{:S(2)}) %collective-permute-start.2) | collective-permute-done | bytes 98336 | tf_op jit(solution)/shard_map/ppermute | solution.py:25
  136.4 1.9 %collective-permute-start.5 = (bf16[384,256]{1,0:T(8,128)(2,1)S(1)}, bf16[384,256]{1,0:T(8,128)(2,1)S(1)}, u32[]{:S(2)}, u32[]{:S(2)}) collective-permute-start(bf16[384,256]{1,0:T(8,128)(2,1)S(1)} %pad_maximum_fusion.7), channel_id=1, source_target_pairs={{0,24},{8,0},{16,8},{24,16},{1,25},{9,1},{17,9},{25,17},{2,26},{10... | collective-permute-start | bytes 589832 | tf_op jit(solution)/shard_map/ppermute | solution.py:25
  138.4 5.2 %all-to-all-done.1 = bf16[8,192,256]{2,1,0:T(8,128)(2,1)S(1)} async-done(((bf16[8,192,256]{2,1,0:T(8,128)(2,1)}), bf16[8,192,256]{2,1,0:T(8,128)(2,1)S(1)}, u32[]{:S(2)}, u32[]{:S(2)}) %all-to-all-start.1) | async-done | bytes 786464 | tf_op jit(solution)/shard_map/all_to_all | solution.py:158
  145.6 3.4 %collective-permute-start.19 = (bf16[384,256]{1,0:T(8,128)(2,1)S(1)}, bf16[384,256]{1,0:T(8,128)(2,1)S(1)}, u32[]{:S(2)}, u32[]{:S(2)}) collective-permute-start(bf16[384,256]{1,0:T(8,128)(2,1)S(1)} %get-tuple-element.2), channel_id=1, source_target_pairs={{0,192},{1,193},{2,194},{3,195},{4,196},{5,197},{6,198},{7,199},{8... | collective-permute-start | bytes 589832 | tf_op jit(solution)/shard_map/ppermute | solution.py:132
  150.6 1.8 %collective-permute-done.19 = bf16[384,256]{1,0:T(8,128)(2,1)S(1)} collective-permute-done((bf16[384,256]{1,0:T(8,128)(2,1)S(1)}, bf16[384,256]{1,0:T(8,128)(2,1)S(1)}, u32[]{:S(2)}, u32[]{:S(2)}) %collective-permute-start.19) | collective-permute-done | bytes 196640 | tf_op jit(solution)/shard_map/ppermute | solution.py:132
  153.4 11.4 %all-to-all-start.2 = ((f32[32,1,768]{2,1,0:T(1,128)}), f32[32,1,768]{2,1,0:T(1,128)S(1)}, u32[]{:S(2)}, u32[]{:S(2)}) async-start(f32[32,1,768]{2,1,0:T(1,128)} %broadcast_in_dim.9), calls=%async_computation.3 | async-start | bytes 196608 | tf_op jit(solution)/shard_map/all_to_all | solution.py:163
  165.6 9.4 %all-to-all-done.2 = f32[32,1,768]{2,1,0:T(1,128)S(1)} async-done(((f32[32,1,768]{2,1,0:T(1,128)}), f32[32,1,768]{2,1,0:T(1,128)S(1)}, u32[]{:S(2)}, u32[]{:S(2)}) %all-to-all-start.2) | async-done | bytes 98336 | tf_op jit(solution)/shard_map/all_to_all | solution.py:163
  (74 shorter events, 23.6 us)
Async XLA Ops:
  7.2 118.6 %reduce-scatter.2.cloned.1.call-start = ((), (), s32[]{:S(2)}) async-start(), calls=%async_computation.4 | async-start | bytes 7077888 | tf_op jit(solution)/shard_map/reduce_scatter | solution.py:116
  7.2 9.3 %collective-permute-start = (bf16[768,896]{1,0:T(8,128)(2,1)}, bf16[768,896]{1,0:T(8,128)(2,1)S(1)}, u32[]{:S(2)}, u32[]{:S(2)}) collective-permute-start(bf16[768,896]{1,0:T(8,128)(2,1)} %bitcast.77), channel_id=1, source_target_pairs={{0,32},{32,0},{1,33},{33,1},{2,34},{34,2},{3,35},{35,3},{4,36},{36... | collective-permute-start | bytes 4128776 | tf_op jit(solution)/shard_map/ppermute | solution.py:30
  9.7 5.2 %collective-permute-start.1 = (bf16[2,24,2048]{2,1,0:T(8,128)(2,1)}, bf16[2,24,2048]{2,1,0:T(8,128)(2,1)}, u32[]{:S(2)}, u32[]{:S(2)}) collective-permute-start(bf16[2,24,2048]{2,1,0:T(8,128)(2,1)} %pad_maximum_fusion.5), channel_id=1, source_target_pairs={{0,32},{32,0},{1,33},{33,1},{2,34},{34,2},{3,35},{35,3},{4,36},{36... | collective-permute-start | bytes 589832 | tf_op jit(solution)/shard_map/ppermute | solution.py:30
  10.2 6.3 %copy-start = (bf16[1,768,896]{2,1,0:T(8,128)(2,1)S(1)}, bf16[1,768,896]{2,1,0:T(8,128)(2,1)}, u32[]{:S(2)}) copy-start(bf16[1,768,896]{2,1,0:T(8,128)(2,1)} %param.4) | copy-start | bytes 4128772
  12.8 19.1 %collective-permute-start.6 = (bf16[384,896]{1,0:T(8,128)(2,1)}, bf16[384,896]{1,0:T(8,128)(2,1)S(1)}, u32[]{:S(2)}, u32[]{:S(2)}) collective-permute-start(bf16[384,896]{1,0:T(8,128)(2,1)} %bitcast.13), channel_id=1, source_target_pairs={{0,64},{64,0},{1,65},{65,1},{2,66},{66,2},{3,67},{67,3},{4,68},{68... | collective-permute-start | bytes 2064392 | tf_op jit(solution)/shard_map/ppermute | solution.py:30
  31.9 0.9 copy-start.4
  32.8 0.9 copy-start.6
  32.8 0.9 copy-start.7
  32.8 10.4 %copy-start.5 = (bf16[384,896]{1,0:T(8,128)(2,1)S(1)}, bf16[384,896]{1,0:T(8,128)(2,1)}, u32[]{:S(2)}) copy-start(bf16[384,896]{1,0:T(8,128)(2,1)} %shard_map.60.h0_ref) | copy-start | bytes 2064388
  32.8 10.4 %collective-permute-start.7 = (bf16[384,896]{1,0:T(8,128)(2,1)}, bf16[384,896]{1,0:T(8,128)(2,1)S(1)}, u32[]{:S(2)}, u32[]{:S(2)}) collective-permute-start(bf16[384,896]{1,0:T(8,128)(2,1)} %shard_map.60.h0_ref), channel_id=1, source_target_pairs={{0,32},{32,0},{1,33},{33,1},{2,34},{34,2},{3,35},{35,3},{4,36},{36... | collective-permute-start | bytes 2064392 | tf_op jit(solution)/shard_map/ppermute | solution.py:30
  33.7 9.4 %collective-permute-start.8 = (bf16[2,24,2048]{2,1,0:T(8,128)(2,1)S(1)}, bf16[2,24,2048]{2,1,0:T(8,128)(2,1)S(1)}, u32[]{:S(2)}, u32[]{:S(2)}) collective-permute-start(bf16[2,24,2048]{2,1,0:T(8,128)(2,1)S(1)} %pad_maximum_fusion.8), channel_id=1, source_target_pairs={{0,64},{64,0},{1,65},{65,1},{2,66},{66,2},{3,67},{67,3},{4,68},{68... | collective-permute-start | bytes 589832 | tf_op jit(solution)/shard_map/ppermute | solution.py:30
  35.9 20.5 %collective-permute-start.13 = (bf16[384,896]{1,0:T(8,128)(2,1)}, bf16[384,896]{1,0:T(8,128)(2,1)S(1)}, u32[]{:S(2)}, u32[]{:S(2)}) collective-permute-start(bf16[384,896]{1,0:T(8,128)(2,1)} %shard_map.62), channel_id=1, source_target_pairs={{0,64},{64,0},{1,65},{65,1},{2,66},{66,2},{3,67},{67,3},{4,68},{68... | collective-permute-start | bytes 2064392 | tf_op jit(solution)/shard_map/ppermute | solution.py:30
  51.4 8.9 %collective-permute-start.11 = (bf16[4,192,256]{2,1,0:T(8,128)(2,1)S(1)}, bf16[4,192,256]{2,1,0:T(8,128)(2,1)S(1)}, u32[]{:S(2)}, u32[]{:S(2)}) collective-permute-start(bf16[4,192,256]{2,1,0:T(8,128)(2,1)S(1)} %get-tuple-element.8), channel_id=1, source_target_pairs={{0,24},{8,0},{16,8},{24,16},{1,25},{9,1},{17,9},{25,17},{2,26},{10... | collective-permute-start | bytes 1179656 | tf_op jit(solution)/shard_map/ppermute | solution.py:25
  54.4 9.3 %collective-permute-start.9 = (bf16[4,192,256]{2,1,0:T(8,128)(2,1)S(1)}, bf16[4,192,256]{2,1,0:T(8,128)(2,1)S(1)}, u32[]{:S(2)}, u32[]{:S(2)}) collective-permute-start(bf16[4,192,256]{2,1,0:T(8,128)(2,1)S(1)} %get-tuple-element.6), channel_id=1, source_target_pairs={{0,8},{8,16},{16,24},{24,0},{1,9},{9,17},{17,25},{25,1},{2,10},{10... | collective-permute-start | bytes 1179656 | tf_op jit(solution)/shard_map/ppermute | solution.py:25
  57.3 11.2 %collective-permute-start.14 = (bf16[384,896]{1,0:T(8,128)(2,1)}, bf16[384,896]{1,0:T(8,128)(2,1)S(1)}, u32[]{:S(2)}, u32[]{:S(2)}) collective-permute-start(bf16[384,896]{1,0:T(8,128)(2,1)} %shard_map.63.h0_ref), channel_id=1, source_target_pairs={{0,32},{32,0},{1,33},{33,1},{2,34},{34,2},{3,35},{35,3},{4,36},{36... | collective-permute-start | bytes 2064392 | tf_op jit(solution)/shard_map/ppermute | solution.py:30
  64.9 3.6 %copy-start.2 = (bf16[384,896]{1,0:T(8,128)(2,1)S(1)}, bf16[384,896]{1,0:T(8,128)(2,1)}, u32[]{:S(2)}) copy-start(bf16[384,896]{1,0:T(8,128)(2,1)} %shard_map.63.h0_ref) | copy-start | bytes 2064388
  65.0 21.2 %collective-permute-start.10 = (bf16[8,192,256]{2,1,0:T(8,128)(2,1)S(1)}, bf16[8,192,256]{2,1,0:T(8,128)(2,1)}, u32[]{:S(2)}, u32[]{:S(2)}) collective-permute-start(bf16[8,192,256]{2,1,0:T(8,128)(2,1)S(1)} %pad_maximum_fusion), channel_id=1, source_target_pairs={{0,8},{8,16},{16,24},{24,0},{1,9},{9,17},{17,25},{25,1},{2,10},{10... | collective-permute-start | bytes 2359304 | tf_op jit(solution)/shard_map/ppermute | solution.py:25
  65.2 21.1 %collective-permute-start.12 = (bf16[8,192,256]{2,1,0:T(8,128)(2,1)S(1)}, bf16[8,192,256]{2,1,0:T(8,128)(2,1)S(1)}, u32[]{:S(2)}, u32[]{:S(2)}) collective-permute-start(bf16[8,192,256]{2,1,0:T(8,128)(2,1)S(1)} %pad_maximum_fusion.1), channel_id=1, source_target_pairs={{0,24},{8,0},{16,8},{24,16},{1,25},{9,1},{17,9},{25,17},{2,26},{10... | collective-permute-start | bytes 2359304 | tf_op jit(solution)/shard_map/ppermute | solution.py:25
  77.5 19.9 %collective-permute-start.15 = (bf16[4,192,256]{2,1,0:T(8,128)(2,1)}, bf16[4,192,256]{2,1,0:T(8,128)(2,1)S(1)}, u32[]{:S(2)}, u32[]{:S(2)}) collective-permute-start(bf16[4,192,256]{2,1,0:T(8,128)(2,1)} %get-tuple-element.12), channel_id=1, source_target_pairs={{0,8},{8,16},{16,24},{24,0},{1,9},{9,17},{17,25},{25,1},{2,10},{10... | collective-permute-start | bytes 1179656 | tf_op jit(solution)/shard_map/ppermute | solution.py:25
  77.5 19.9 %collective-permute-start.17 = (bf16[4,192,256]{2,1,0:T(8,128)(2,1)}, bf16[4,192,256]{2,1,0:T(8,128)(2,1)}, u32[]{:S(2)}, u32[]{:S(2)}) collective-permute-start(bf16[4,192,256]{2,1,0:T(8,128)(2,1)} %get-tuple-element.14), channel_id=1, source_target_pairs={{0,24},{8,0},{16,8},{24,16},{1,25},{9,1},{17,9},{25,17},{2,26},{10... | collective-permute-start | bytes 1179656 | tf_op jit(solution)/shard_map/ppermute | solution.py:25
  88.8 33.4 %all-to-all-start = ((bf16[8,192,256]{2,1,0:T(8,128)(2,1)}), bf16[8,192,256]{2,1,0:T(8,128)(2,1)S(1)}, u32[]{:S(2)}, u32[]{:S(2)}) async-start(bf16[8,192,256]{2,1,0:T(8,128)(2,1)} %fusion.3), calls=%async_computation.1 | async-start | bytes 1572864 | tf_op jit(solution)/shard_map/all_to_all | solution.py:158
  98.8 13.3 %collective-permute-start.16 = (bf16[8,192,256]{2,1,0:T(8,128)(2,1)S(1)}, bf16[8,192,256]{2,1,0:T(8,128)(2,1)S(1)}, u32[]{:S(2)}, u32[]{:S(2)}) collective-permute-start(bf16[8,192,256]{2,1,0:T(8,128)(2,1)S(1)} %pad_maximum_fusion.2), channel_id=1, source_target_pairs={{0,8},{8,16},{16,24},{24,0},{1,9},{9,17},{17,25},{25,1},{2,10},{10... | collective-permute-start | bytes 2359304 | tf_op jit(solution)/shard_map/ppermute | solution.py:25
  98.9 13.1 %collective-permute-start.18 = (bf16[8,192,256]{2,1,0:T(8,128)(2,1)S(1)}, bf16[8,192,256]{2,1,0:T(8,128)(2,1)S(1)}, u32[]{:S(2)}, u32[]{:S(2)}) collective-permute-start(bf16[8,192,256]{2,1,0:T(8,128)(2,1)S(1)} %pad_maximum_fusion.3), channel_id=1, source_target_pairs={{0,24},{8,0},{16,8},{24,16},{1,25},{9,1},{17,9},{25,17},{2,26},{10... | collective-permute-start | bytes 2359304 | tf_op jit(solution)/shard_map/ppermute | solution.py:25
  122.2 21.4 %all-to-all-start.1 = ((bf16[8,192,256]{2,1,0:T(8,128)(2,1)}), bf16[8,192,256]{2,1,0:T(8,128)(2,1)S(1)}, u32[]{:S(2)}, u32[]{:S(2)}) async-start(bf16[8,192,256]{2,1,0:T(8,128)(2,1)} %fusion.1), calls=%async_computation.2 | async-start | bytes 1572864 | tf_op jit(solution)/shard_map/all_to_all | solution.py:158
  126.8 6.9 %collective-permute-start.2 = (bf16[192,256]{1,0:T(8,128)(2,1)S(1)}, bf16[192,256]{1,0:T(8,128)(2,1)S(1)}, u32[]{:S(2)}, u32[]{:S(2)}) collective-permute-start(bf16[192,256]{1,0:T(8,128)(2,1)S(1)} %get-tuple-element.20), channel_id=1, source_target_pairs={{0,8},{8,16},{16,24},{24,0},{1,9},{9,17},{17,25},{25,1},{2,10},{10... | collective-permute-start | bytes 294920 | tf_op jit(solution)/shard_map/ppermute | solution.py:25
  128.4 5.4 %collective-permute-start.4 = (bf16[192,256]{1,0:T(8,128)(2,1)S(1)}, bf16[192,256]{1,0:T(8,128)(2,1)S(1)}, u32[]{:S(2)}, u32[]{:S(2)}) collective-permute-start(bf16[192,256]{1,0:T(8,128)(2,1)S(1)} %get-tuple-element.22), channel_id=1, source_target_pairs={{0,24},{8,0},{16,8},{24,16},{1,25},{9,1},{17,9},{25,17},{2,26},{10... | collective-permute-start | bytes 294920 | tf_op jit(solution)/shard_map/ppermute | solution.py:25
  134.8 8.9 %collective-permute-start.3 = (bf16[384,256]{1,0:T(8,128)(2,1)S(1)}, bf16[384,256]{1,0:T(8,128)(2,1)S(1)}, u32[]{:S(2)}, u32[]{:S(2)}) collective-permute-start(bf16[384,256]{1,0:T(8,128)(2,1)S(1)} %pad_maximum_fusion.6), channel_id=1, source_target_pairs={{0,8},{8,16},{16,24},{24,0},{1,9},{9,17},{17,25},{25,1},{2,10},{10... | collective-permute-start | bytes 589832 | tf_op jit(solution)/shard_map/ppermute | solution.py:25
  136.4 7.3 %collective-permute-start.5 = (bf16[384,256]{1,0:T(8,128)(2,1)S(1)}, bf16[384,256]{1,0:T(8,128)(2,1)S(1)}, u32[]{:S(2)}, u32[]{:S(2)}) collective-permute-start(bf16[384,256]{1,0:T(8,128)(2,1)S(1)} %pad_maximum_fusion.7), channel_id=1, source_target_pairs={{0,24},{8,0},{16,8},{24,16},{1,25},{9,1},{17,9},{25,17},{2,26},{10... | collective-permute-start | bytes 589832 | tf_op jit(solution)/shard_map/ppermute | solution.py:25
  144.8 30.2 %copy-start.8 = (f32[1,256]{1,0:T(1,128)S(1)}, f32[1,256]{1,0:T(1,128)}, u32[]{:S(2)}) copy-start(f32[1,256]{1,0:T(1,128)} %param.7) | copy-start | bytes 3076
  144.8 5.8 %collective-permute-start.20 = (bf16[384,256]{1,0:T(8,128)(2,1)S(1)}, bf16[384,256]{1,0:T(8,128)(2,1)S(1)}, u32[]{:S(2)}, u32[]{:S(2)}) collective-permute-start(bf16[384,256]{1,0:T(8,128)(2,1)S(1)} %broadcast_select_fusion), channel_id=1, source_target_pairs={{0,128},{1,129},{2,130},{3,131},{4,132},{5,133},{6,134},{7,135},{8... | collective-permute-start | bytes 589832 | tf_op jit(solution)/shard_map/ppermute | solution.py:131
  145.6 6.8 %collective-permute-start.19 = (bf16[384,256]{1,0:T(8,128)(2,1)S(1)}, bf16[384,256]{1,0:T(8,128)(2,1)S(1)}, u32[]{:S(2)}, u32[]{:S(2)}) collective-permute-start(bf16[384,256]{1,0:T(8,128)(2,1)S(1)} %get-tuple-element.2), channel_id=1, source_target_pairs={{0,192},{1,193},{2,194},{3,195},{4,196},{5,197},{6,198},{7,199},{8... | collective-permute-start | bytes 589832 | tf_op jit(solution)/shard_map/ppermute | solution.py:132
  153.4 21.6 %all-to-all-start.2 = ((f32[32,1,768]{2,1,0:T(1,128)}), f32[32,1,768]{2,1,0:T(1,128)S(1)}, u32[]{:S(2)}, u32[]{:S(2)}) async-start(f32[32,1,768]{2,1,0:T(1,128)} %broadcast_in_dim.9), calls=%async_computation.3 | async-start | bytes 196608 | tf_op jit(solution)/shard_map/all_to_all | solution.py:163
  (2 other events, 1.5 us)
Sparse Core Ops, SparseCore 0:
  27.0 91.6 reduce-scatter.1

commit v8 on v5

--- a/solution.py
+++ b/solution.py
@@ -14,7 +14,6 @@
 STEP = 2
 HALF = 384
 ORDER = ((0, 192), (192, HALF))
-HOLD = 4 * 10**10
 TIE = 3 * 10**11
 SCALE, FAR = 20, 1
 VMEM = 50 * 2**20
@@ -188,7 +187,7 @@
     (own, *one), (other, *two) = steps
     up, down = second_step(*one)
     one = added(own, up, down)
-    sums = [one, added(tied(other, one, flops=HOLD), *second_step(*two))]
+    sums = [one, added(other, *second_step(*two))]
     sums = [lax.all_to_all(x, "z", split_axis=0, concat_axis=0, tiled=True) for x in sums]
     sums = [jnp.sum(x.astype(F32), axis=0).astype(BF16) for x in sums]
     handed = handed_over((near, jnp.concatenate(sums)), group, y)

time: 190 us -> 186 us (0.979)
  local copies, waits for them, and re-layouts: 14.1 us -> 12 us
    ppermute x12, waiting for transfers between devices: 24.4 us -> 28.8 us  [shifted(): return lax.ppermute(x, axis, [(i, (i + by) % n) for i in range(n)])]
    all_to_all x2, waiting for transfers between devices: 20.7 us -> 16.5 us  [shards(): lax.all_to_all(x, 'z', split_axis=0, concat_axis=0, tiled=True)]
    another operation x1 -> x0, local copies, waits for them, and re-layouts: 2.08 us -> none  [shards(): own, ahead, behind = rest]
  transfers between devices with their start and end apart: 25 -> 25, of which waited for: 12 -> 14; matrix products, arithmetic and copies ran while one was open for 13% -> 12% of each run, Pallas kernels for 13% -> 14%
where the time goes in v8:
time: 186 us; the launch traced here: 183 us
  waiting for transfers between devices  71.6 us (38%)
  starting transfers between devices  45.9 us (25%)
  Pallas kernels  25 us (13%)
  between operations  14.4 us (8%)
  other arithmetic  14 us (8%)
  local copies, waits for them, and re-layouts  12 us (6%)
    ppermute x12, waiting for transfers between devices, shifted(): return lax.ppermute(x, axis, [(i, (i + by) % n) for i in range(n)])  28.8 us
    pallas_call x3, Pallas kernels, product(): pl.pallas_call(functools.partial(product_kernel, first, rows, relative),...  25 us
    ppermute x12, starting transfers between devices, shifted(): return lax.ppermute(x, axis, [(i, (i + by) % n) for i in range(n)])  18.3 us
    all_to_all x2, waiting for transfers between devices, shards(): lax.all_to_all(x, 'z', split_axis=0, concat_axis=0, tiled=True)  16.5 us
    ppermute x7, waiting for transfers between devices, flipped(): return lax.ppermute(x, axes, [(i, n - 1 - i) for i in range(n)])  12.9 us
    all_to_all x2, starting transfers between devices, shards(): lax.all_to_all(x, 'z', split_axis=0, concat_axis=0, tiled=True)  11.9 us
    all_to_all x1, waiting for transfers between devices, shards(): lax.all_to_all(jnp.broadcast_to(squares, (NY * NZ, 768)), ('y', 'z'), spl...  9.41 us
    ppermute x7, starting transfers between devices, flipped(): return lax.ppermute(x, axes, [(i, n - 1 - i) for i in range(n)])  6.21 us
  transfers between devices with their start and end apart: 25, of which 14 were waited for; matrix products, arithmetic and copies ran while one was open for 12% of the time, Pallas kernels for 14%

profile of v8, /device:TPU:2, one launch (start us, length us, event | category | flops | bytes accessed | tf_op | source)
XLA Modules:
  0.0 183.0 jit_solution(3642032766578687503)
XLA Ops:
  7.3 1.7 constant_dynamic-slice_fusion
  10.2 2.6 %fusion.10 = (bf16[2,192,896]{2,1,0:T(8,128)(2,1)}, bf16[2,192,896]{2,1,0:T(8,128)(2,1)}) fusion(bf16[2,384,896]{2,1,0:T(8,128)(2,1)} %bitcast.62), kind=kLoop, calls=%fused_computation.50 | loop fusion | bytes 2752512 | tf_op jit(solution)/shard_map/slice | solution.py:180
  12.8 2.1 %collective-permute-start.6 = (bf16[384,896]{1,0:T(8,128)(2,1)}, bf16[384,896]{1,0:T(8,128)(2,1)S(1)}, u32[]{:S(2)}, u32[]{:S(2)}) collective-permute-start(bf16[384,896]{1,0:T(8,128)(2,1)} %bitcast.13), channel_id=1, source_target_pairs={{0,64},{64,0},{1,65},{65,1},{2,66},{66,2},{3,67},{67,3},{4,68},{68... | collective-permute-start | bytes 2064392 | tf_op jit(solution)/shard_map/ppermute | solution.py:30
  15.9 1.6 pad_maximum_fusion.8
  18.9 9.7 %shard_map.59.refs_1_ = bf16[8,4,384,256]{3,2,1,0:T(8,128)(2,1)} custom-call(s32[1]{0:T(128)} %bitcast.m_ref, bf16[768,896]{1,0:T(8,128)(2,1)S(1)} %bitcast.63, bf16[768,896]{1,0:T(8,128)(2,1)S(1)} %collective-permute-done.h1_ref, bf16[896,2048]{1,0:T(8,128)(2,1)} %bitcast.68, bf16[24,2048]{1,0:T(8,128)(2,1)S(1)} %get-tuple-element.36.r0_ref, ...), custom_call_target="tpu_custom_call" | custom-call | flops 112742891520 | bytes 12713984 | tf_op jit(solution)/shard_map/pallas_call | solution.py:89
  28.7 7.5 %collective-permute-done.7.refs_2_ = bf16[2,24,2048]{2,1,0:T(8,128)(2,1)} collective-permute-done((bf16[2,24,2048]{2,1,0:T(8,128)(2,1)}, bf16[2,24,2048]{2,1,0:T(8,128)(2,1)}, u32[]{:S(2)}, u32[]{:S(2)}) %collective-permute-start.7) | collective-permute-done | bytes 196640 | tf_op jit(solution)/shard_map/ppermute | solution.py:30
  37.1 2.1 %collective-permute-start.13 = (bf16[384,896]{1,0:T(8,128)(2,1)}, bf16[384,896]{1,0:T(8,128)(2,1)S(1)}, u32[]{:S(2)}, u32[]{:S(2)}) collective-permute-start(bf16[384,896]{1,0:T(8,128)(2,1)} %shard_map.62), channel_id=1, source_target_pairs={{0,64},{64,0},{1,65},{65,1},{2,66},{66,2},{3,67},{67,3},{4,68},{68... | collective-permute-start | bytes 2064392 | tf_op jit(solution)/shard_map/ppermute | solution.py:30
  40.2 7.8 %shard_map.61 = (bf16[4,192,256]{2,1,0:T(8,128)(2,1)S(1)}, bf16[4,192,256]{2,1,0:T(8,128)(2,1)S(1)}, bf16[3,8,192,256]{3,2,1,0:T(8,128)(2,1)}) custom-call(s32[1]{0:T(128)} %bitcast.m_ref, bf16[384,896]{1,0:T(8,128)(2,1)S(1)} %copy-done.5, bf16[384,896]{1,0:T(8,128)(2,1)S(1)} %collective-permute-done.8.h1_ref, bf16[896,2048]{1,0:T(8,128)(2,1)} %bitcast.69, ...), custom_call_target="tpu_custom_call" | custom-call | flops 2818572288 | bytes 8192000 | tf_op jit(solution)/shard_map/pallas_call | solution.py:89
  49.4 1.9 %collective-permute-start.11 = (bf16[4,192,256]{2,1,0:T(8,128)(2,1)S(1)}, bf16[4,192,256]{2,1,0:T(8,128)(2,1)S(1)}, u32[]{:S(2)}, u32[]{:S(2)}) collective-permute-start(bf16[4,192,256]{2,1,0:T(8,128)(2,1)S(1)} %get-tuple-element.10), channel_id=1, source_target_pairs={{0,24},{8,0},{16,8},{24,16},{1,25},{9,1},{17,9},{25,17},{2,26},{10... | collective-permute-start | bytes 1179656 | tf_op jit(solution)/shard_map/ppermute | solution.py:25
  51.3 5.4 %collective-permute-done.13.refs_0_ = bf16[384,896]{1,0:T(8,128)(2,1)S(1)} collective-permute-done((bf16[384,896]{1,0:T(8,128)(2,1)}, bf16[384,896]{1,0:T(8,128)(2,1)S(1)}, u32[]{:S(2)}, u32[]{:S(2)}) %collective-permute-start.13) | collective-permute-done | bytes 688160 | tf_op jit(solution)/shard_map/ppermute | solution.py:30
  58.7 1.8 collective-permute-done.9
  61.8 3.0 %collective-permute-start.12 = (bf16[8,192,256]{2,1,0:T(8,128)(2,1)S(1)}, bf16[8,192,256]{2,1,0:T(8,128)(2,1)S(1)}, u32[]{:S(2)}, u32[]{:S(2)}) collective-permute-start(bf16[8,192,256]{2,1,0:T(8,128)(2,1)S(1)} %pad_maximum_fusion.1), channel_id=1, source_target_pairs={{0,24},{8,0},{16,8},{24,16},{1,25},{9,1},{17,9},{25,17},{2,26},{10... | collective-permute-start | bytes 2359304 | tf_op jit(solution)/shard_map/ppermute | solution.py:25
  65.0 7.4 %shard_map.64 = (bf16[4,192,256]{2,1,0:T(8,128)(2,1)S(1)}, bf16[4,192,256]{2,1,0:T(8,128)(2,1)S(1)}, bf16[3,8,192,256]{3,2,1,0:T(8,128)(2,1)}) custom-call(s32[1]{0:T(128)} %bitcast.m_ref, bf16[384,896]{1,0:T(8,128)(2,1)S(1)} %copy-done.2, bf16[384,896]{1,0:T(8,128)(2,1)S(1)} %collective-permute-done.14.h1_ref, bf16[896,2048]{1,0:T(8,128)(2,1)} %bitcast.70, ...), custom_call_target="tpu_custom_call" | custom-call | flops 2818572288 | bytes 8192000 | tf_op jit(solution)/shard_map/pallas_call | solution.py:89
  73.5 2.5 %collective-permute-start.17 = (bf16[4,192,256]{2,1,0:T(8,128)(2,1)S(1)}, bf16[4,192,256]{2,1,0:T(8,128)(2,1)S(1)}, u32[]{:S(2)}, u32[]{:S(2)}) collective-permute-start(bf16[4,192,256]{2,1,0:T(8,128)(2,1)S(1)} %get-tuple-element.13), channel_id=1, source_target_pairs={{0,24},{8,0},{16,8},{24,16},{1,25},{9,1},{17,9},{25,17},{2,26},{10... | collective-permute-start | bytes 1179656 | tf_op jit(solution)/shard_map/ppermute | solution.py:25
  77.1 5.7 %collective-permute-done.12 = bf16[8,192,256]{2,1,0:T(8,128)(2,1)S(1)} collective-permute-done((bf16[8,192,256]{2,1,0:T(8,128)(2,1)S(1)}, bf16[8,192,256]{2,1,0:T(8,128)(2,1)S(1)}, u32[]{:S(2)}, u32[]{:S(2)}) %collective-permute-start.12) | collective-permute-done | bytes 786464 | tf_op jit(solution)/shard_map/ppermute | solution.py:25
  82.8 3.8 %collective-permute-done.10 = bf16[8,192,256]{2,1,0:T(8,128)(2,1)S(1)} collective-permute-done((bf16[8,192,256]{2,1,0:T(8,128)(2,1)S(1)}, bf16[8,192,256]{2,1,0:T(8,128)(2,1)S(1)}, u32[]{:S(2)}, u32[]{:S(2)}) %collective-permute-start.10) | collective-permute-done | bytes 786464 | tf_op jit(solution)/shard_map/ppermute | solution.py:25
  86.7 2.3 %fusion.3 = bf16[8,192,256]{2,1,0:T(8,128)(2,1)} fusion(bf16[8,192,256]{2,1,0:T(8,128)(2,1)S(1)} %collective-permute-done.12, bf16[8,192,256]{2,1,0:T(8,128)(2,1)S(1)} %collective-permute-done.10, bf16[3,8,192,256]{3,2,1,0:T(8,128)(2,1)} %get-tuple-element.8.refs_1_), kind=kLoop, calls=%fused_computation.5 | loop fusion | flops 2359296 | bytes 3145728 | tf_op jit(solution)/shard_map/convert_element_type | solution.py:135
  89.0 8.4 %all-to-all-start = ((bf16[8,192,256]{2,1,0:T(8,128)(2,1)}), bf16[8,192,256]{2,1,0:T(8,128)(2,1)S(1)}, u32[]{:S(2)}, u32[]{:S(2)}) async-start(bf16[8,192,256]{2,1,0:T(8,128)(2,1)} %fusion.3), calls=%async_computation.1 | async-start | bytes 1572864 | tf_op jit(solution)/shard_map/all_to_all | solution.py:191
  98.8 2.1 %collective-permute-start.16 = (bf16[8,192,256]{2,1,0:T(8,128)(2,1)S(1)}, bf16[8,192,256]{2,1,0:T(8,128)(2,1)S(1)}, u32[]{:S(2)}, u32[]{:S(2)}) collective-permute-start(bf16[8,192,256]{2,1,0:T(8,128)(2,1)S(1)} %pad_maximum_fusion.2), channel_id=1, source_target_pairs={{0,8},{8,16},{16,24},{24,0},{1,9},{9,17},{17,25},{25,1},{2,10},{10... | collective-permute-start | bytes 2359304 | tf_op jit(solution)/shard_map/ppermute | solution.py:25
  100.9 12.9 %collective-permute-done.18 = bf16[8,192,256]{2,1,0:T(8,128)(2,1)S(1)} collective-permute-done((bf16[8,192,256]{2,1,0:T(8,128)(2,1)S(1)}, bf16[8,192,256]{2,1,0:T(8,128)(2,1)S(1)}, u32[]{:S(2)}, u32[]{:S(2)}) %collective-permute-start.18) | collective-permute-done | bytes 786464 | tf_op jit(solution)/shard_map/ppermute | solution.py:25
  115.3 2.4 %fusion.1 = bf16[8,192,256]{2,1,0:T(8,128)(2,1)} fusion(bf16[8,192,256]{2,1,0:T(8,128)(2,1)S(1)} %collective-permute-done.18, bf16[8,192,256]{2,1,0:T(8,128)(2,1)S(1)} %collective-permute-done.16, bf16[3,8,192,256]{3,2,1,0:T(8,128)(2,1)} %get-tuple-element.11), kind=kLoop, calls=%fused_computation.2 | loop fusion | flops 2359296 | bytes 3145728 | tf_op jit(solution)/shard_map/convert_element_type | solution.py:135
  117.7 7.2 %all-to-all-done = bf16[8,192,256]{2,1,0:T(8,128)(2,1)S(1)} async-done(((bf16[8,192,256]{2,1,0:T(8,128)(2,1)}), bf16[8,192,256]{2,1,0:T(8,128)(2,1)S(1)}, u32[]{:S(2)}, u32[]{:S(2)}) %all-to-all-start) | async-done | bytes 786464 | tf_op jit(solution)/shard_map/all_to_all | solution.py:191
  124.9 3.5 %all-to-all-start.1 = ((bf16[8,192,256]{2,1,0:T(8,128)(2,1)}), bf16[8,192,256]{2,1,0:T(8,128)(2,1)S(1)}, u32[]{:S(2)}, u32[]{:S(2)}) async-start(bf16[8,192,256]{2,1,0:T(8,128)(2,1)} %fusion.1), calls=%async_computation.2 | async-start | bytes 1572864 | tf_op jit(solution)/shard_map/all_to_all | solution.py:191
  131.1 1.8 collective-permute-start.4
  133.0 2.6 %collective-permute-done.2 = bf16[192,256]{1,0:T(8,128)(2,1)S(1)} collective-permute-done((bf16[192,256]{1,0:T(8,128)(2,1)S(1)}, bf16[192,256]{1,0:T(8,128)(2,1)S(1)}, u32[]{:S(2)}, u32[]{:S(2)}) %collective-permute-start.2) | collective-permute-done | bytes 98336 | tf_op jit(solution)/shard_map/ppermute | solution.py:25
  137.0 2.8 %collective-permute-start.5 = (bf16[384,256]{1,0:T(8,128)(2,1)S(1)}, bf16[384,256]{1,0:T(8,128)(2,1)S(1)}, u32[]{:S(2)}, u32[]{:S(2)}) collective-permute-start(bf16[384,256]{1,0:T(8,128)(2,1)S(1)} %pad_maximum_fusion.7), channel_id=1, source_target_pairs={{0,24},{8,0},{16,8},{24,16},{1,25},{9,1},{17,9},{25,17},{2,26},{10... | collective-permute-start | bytes 589832 | tf_op jit(solution)/shard_map/ppermute | solution.py:25
  140.1 9.3 %all-to-all-done.1 = bf16[8,192,256]{2,1,0:T(8,128)(2,1)S(1)} async-done(((bf16[8,192,256]{2,1,0:T(8,128)(2,1)}), bf16[8,192,256]{2,1,0:T(8,128)(2,1)S(1)}, u32[]{:S(2)}, u32[]{:S(2)}) %all-to-all-start.1) | async-done | bytes 786464 | tf_op jit(solution)/shard_map/all_to_all | solution.py:191
  150.7 1.9 %collective-permute-start.19 = (bf16[384,256]{1,0:T(8,128)(2,1)S(1)}, bf16[384,256]{1,0:T(8,128)(2,1)S(1)}, u32[]{:S(2)}, u32[]{:S(2)}) collective-permute-start(bf16[384,256]{1,0:T(8,128)(2,1)S(1)} %get-tuple-element.14), channel_id=1, source_target_pairs={{0,192},{1,193},{2,194},{3,195},{4,196},{5,197},{6,198},{7,199},{8... | collective-permute-start | bytes 589832 | tf_op jit(solution)/shard_map/ppermute | solution.py:155
  152.6 1.8 collective-permute-start.20
  154.3 3.0 %collective-permute-done.19 = bf16[384,256]{1,0:T(8,128)(2,1)S(1)} collective-permute-done((bf16[384,256]{1,0:T(8,128)(2,1)S(1)}, bf16[384,256]{1,0:T(8,128)(2,1)S(1)}, u32[]{:S(2)}, u32[]{:S(2)}) %collective-permute-start.19) | collective-permute-done | bytes 196640 | tf_op jit(solution)/shard_map/ppermute | solution.py:155
  159.1 5.8 %all-to-all-start.2 = ((f32[32,1,768]{2,1,0:T(1,128)}), f32[32,1,768]{2,1,0:T(1,128)S(1)}, u32[]{:S(2)}, u32[]{:S(2)}) async-start(f32[32,1,768]{2,1,0:T(1,128)} %broadcast_in_dim.9), calls=%async_computation.3 | async-start | bytes 196608 | tf_op jit(solution)/shard_map/all_to_all | solution.py:196
  165.7 9.4 %all-to-all-done.2 = f32[32,1,768]{2,1,0:T(1,128)S(1)} async-done(((f32[32,1,768]{2,1,0:T(1,128)}), f32[32,1,768]{2,1,0:T(1,128)S(1)}, u32[]{:S(2)}, u32[]{:S(2)}) %all-to-all-start.2) | async-done | bytes 98336 | tf_op jit(solution)/shard_map/all_to_all | solution.py:196
  (70 shorter events, 24.5 us)
Async XLA Ops:
  7.2 121.4 %reduce-scatter.2.cloned.1.call-start = ((), (), s32[]{:S(2)}) async-start(), calls=%async_computation.4 | async-start | bytes 7077888 | tf_op jit(solution)/shard_map/reduce_scatter | solution.py:139
  7.2 11.7 %collective-permute-start = (bf16[768,896]{1,0:T(8,128)(2,1)}, bf16[768,896]{1,0:T(8,128)(2,1)S(1)}, u32[]{:S(2)}, u32[]{:S(2)}) collective-permute-start(bf16[768,896]{1,0:T(8,128)(2,1)} %bitcast.61), channel_id=1, source_target_pairs={{0,32},{32,0},{1,33},{33,1},{2,34},{34,2},{3,35},{35,3},{4,36},{36... | collective-permute-start | bytes 4128776 | tf_op jit(solution)/shard_map/ppermute | solution.py:30
  9.7 5.2 %collective-permute-start.1 = (bf16[2,24,2048]{2,1,0:T(8,128)(2,1)}, bf16[2,24,2048]{2,1,0:T(8,128)(2,1)}, u32[]{:S(2)}, u32[]{:S(2)}) collective-permute-start(bf16[2,24,2048]{2,1,0:T(8,128)(2,1)} %pad_maximum_fusion.5), channel_id=1, source_target_pairs={{0,32},{32,0},{1,33},{33,1},{2,34},{34,2},{3,35},{35,3},{4,36},{36... | collective-permute-start | bytes 589832 | tf_op jit(solution)/shard_map/ppermute | solution.py:30
  10.2 8.7 %copy-start = (bf16[1,768,896]{2,1,0:T(8,128)(2,1)S(1)}, bf16[1,768,896]{2,1,0:T(8,128)(2,1)}, u32[]{:S(2)}) copy-start(bf16[1,768,896]{2,1,0:T(8,128)(2,1)} %param.4) | copy-start | bytes 4128772
  12.8 23.4 %collective-permute-start.6 = (bf16[384,896]{1,0:T(8,128)(2,1)}, bf16[384,896]{1,0:T(8,128)(2,1)S(1)}, u32[]{:S(2)}, u32[]{:S(2)}) collective-permute-start(bf16[384,896]{1,0:T(8,128)(2,1)} %bitcast.13), channel_id=1, source_target_pairs={{0,64},{64,0},{1,65},{65,1},{2,66},{66,2},{3,67},{67,3},{4,68},{68... | collective-permute-start | bytes 2064392 | tf_op jit(solution)/shard_map/ppermute | solution.py:30
  15.9 3.0 %copy-start.3 = (bf16[24,2048]{1,0:T(8,128)(2,1)}, bf16[24,2048]{1,0:T(8,128)(2,1)S(1)}, u32[]{:S(2)}) copy-start(bf16[24,2048]{1,0:T(8,128)(2,1)S(1)} %get-tuple-element.41.r1_ref.refs_1_) | copy-start | bytes 294916
  17.5 18.7 %collective-permute-start.7 = (bf16[2,24,2048]{2,1,0:T(8,128)(2,1)}, bf16[2,24,2048]{2,1,0:T(8,128)(2,1)}, u32[]{:S(2)}, u32[]{:S(2)}) collective-permute-start(bf16[2,24,2048]{2,1,0:T(8,128)(2,1)} %pad_maximum_fusion.8), channel_id=1, source_target_pairs={{0,64},{64,0},{1,65},{65,1},{2,66},{66,2},{3,67},{67,3},{4,68},{68... | collective-permute-start | bytes 589832 | tf_op jit(solution)/shard_map/ppermute | solution.py:30
  36.2 0.8 copy-start.4
  37.1 3.1 %copy-start.5 = (bf16[384,896]{1,0:T(8,128)(2,1)S(1)}, bf16[384,896]{1,0:T(8,128)(2,1)}, u32[]{:S(2)}) copy-start(bf16[384,896]{1,0:T(8,128)(2,1)} %shard_map.60.h0_ref) | copy-start | bytes 2064388
  37.1 3.1 %collective-permute-start.8 = (bf16[384,896]{1,0:T(8,128)(2,1)}, bf16[384,896]{1,0:T(8,128)(2,1)S(1)}, u32[]{:S(2)}, u32[]{:S(2)}) collective-permute-start(bf16[384,896]{1,0:T(8,128)(2,1)} %shard_map.60.h0_ref), channel_id=1, source_target_pairs={{0,32},{32,0},{1,33},{33,1},{2,34},{34,2},{3,35},{35,3},{4,36},{36... | collective-permute-start | bytes 2064392 | tf_op jit(solution)/shard_map/ppermute | solution.py:30
  37.1 19.6 %collective-permute-start.13 = (bf16[384,896]{1,0:T(8,128)(2,1)}, bf16[384,896]{1,0:T(8,128)(2,1)S(1)}, u32[]{:S(2)}, u32[]{:S(2)}) collective-permute-start(bf16[384,896]{1,0:T(8,128)(2,1)} %shard_map.62), channel_id=1, source_target_pairs={{0,64},{64,0},{1,65},{65,1},{2,66},{66,2},{3,67},{67,3},{4,68},{68... | collective-permute-start | bytes 2064392 | tf_op jit(solution)/shard_map/ppermute | solution.py:30
  48.0 12.4 %collective-permute-start.9 = (bf16[4,192,256]{2,1,0:T(8,128)(2,1)S(1)}, bf16[4,192,256]{2,1,0:T(8,128)(2,1)S(1)}, u32[]{:S(2)}, u32[]{:S(2)}) collective-permute-start(bf16[4,192,256]{2,1,0:T(8,128)(2,1)S(1)} %get-tuple-element.9), channel_id=1, source_target_pairs={{0,8},{8,16},{16,24},{24,0},{1,9},{9,17},{17,25},{25,1},{2,10},{10... | collective-permute-start | bytes 1179656 | tf_op jit(solution)/shard_map/ppermute | solution.py:25
  49.4 11.1 %collective-permute-start.11 = (bf16[4,192,256]{2,1,0:T(8,128)(2,1)S(1)}, bf16[4,192,256]{2,1,0:T(8,128)(2,1)S(1)}, u32[]{:S(2)}, u32[]{:S(2)}) collective-permute-start(bf16[4,192,256]{2,1,0:T(8,128)(2,1)S(1)} %get-tuple-element.10), channel_id=1, source_target_pairs={{0,24},{8,0},{16,8},{24,16},{1,25},{9,1},{17,9},{25,17},{2,26},{10... | collective-permute-start | bytes 1179656 | tf_op jit(solution)/shard_map/ppermute | solution.py:25
  56.6 0.9 copy-start.1
  57.5 7.5 %collective-permute-start.14 = (bf16[384,896]{1,0:T(8,128)(2,1)}, bf16[384,896]{1,0:T(8,128)(2,1)S(1)}, u32[]{:S(2)}, u32[]{:S(2)}) collective-permute-start(bf16[384,896]{1,0:T(8,128)(2,1)} %shard_map.63.h0_ref), channel_id=1, source_target_pairs={{0,32},{32,0},{1,33},{33,1},{2,34},{34,2},{3,35},{35,3},{4,36},{36... | collective-permute-start | bytes 2064392 | tf_op jit(solution)/shard_map/ppermute | solution.py:30
  61.7 3.3 %copy-start.2 = (bf16[384,896]{1,0:T(8,128)(2,1)S(1)}, bf16[384,896]{1,0:T(8,128)(2,1)}, u32[]{:S(2)}) copy-start(bf16[384,896]{1,0:T(8,128)(2,1)} %shard_map.63.h0_ref) | copy-start | bytes 2064388
  61.8 21.0 %collective-permute-start.12 = (bf16[8,192,256]{2,1,0:T(8,128)(2,1)S(1)}, bf16[8,192,256]{2,1,0:T(8,128)(2,1)S(1)}, u32[]{:S(2)}, u32[]{:S(2)}) collective-permute-start(bf16[8,192,256]{2,1,0:T(8,128)(2,1)S(1)} %pad_maximum_fusion.1), channel_id=1, source_target_pairs={{0,24},{8,0},{16,8},{24,16},{1,25},{9,1},{17,9},{25,17},{2,26},{10... | collective-permute-start | bytes 2359304 | tf_op jit(solution)/shard_map/ppermute | solution.py:25
  64.9 21.8 %collective-permute-start.10 = (bf16[8,192,256]{2,1,0:T(8,128)(2,1)S(1)}, bf16[8,192,256]{2,1,0:T(8,128)(2,1)S(1)}, u32[]{:S(2)}, u32[]{:S(2)}) collective-permute-start(bf16[8,192,256]{2,1,0:T(8,128)(2,1)S(1)} %pad_maximum_fusion), channel_id=1, source_target_pairs={{0,8},{8,16},{16,24},{24,0},{1,9},{9,17},{17,25},{25,1},{2,10},{10... | collective-permute-start | bytes 2359304 | tf_op jit(solution)/shard_map/ppermute | solution.py:25
  72.4 25.0 %collective-permute-start.15 = (bf16[4,192,256]{2,1,0:T(8,128)(2,1)S(1)}, bf16[4,192,256]{2,1,0:T(8,128)(2,1)S(1)}, u32[]{:S(2)}, u32[]{:S(2)}) collective-permute-start(bf16[4,192,256]{2,1,0:T(8,128)(2,1)S(1)} %get-tuple-element.12), channel_id=1, source_target_pairs={{0,8},{8,16},{16,24},{24,0},{1,9},{9,17},{17,25},{25,1},{2,10},{10... | collective-permute-start | bytes 1179656 | tf_op jit(solution)/shard_map/ppermute | solution.py:25
  73.5 23.9 %collective-permute-start.17 = (bf16[4,192,256]{2,1,0:T(8,128)(2,1)S(1)}, bf16[4,192,256]{2,1,0:T(8,128)(2,1)S(1)}, u32[]{:S(2)}, u32[]{:S(2)}) collective-permute-start(bf16[4,192,256]{2,1,0:T(8,128)(2,1)S(1)} %get-tuple-element.13), channel_id=1, source_target_pairs={{0,24},{8,0},{16,8},{24,16},{1,25},{9,1},{17,9},{25,17},{2,26},{10... | collective-permute-start | bytes 1179656 | tf_op jit(solution)/shard_map/ppermute | solution.py:25
  89.0 36.0 %all-to-all-start = ((bf16[8,192,256]{2,1,0:T(8,128)(2,1)}), bf16[8,192,256]{2,1,0:T(8,128)(2,1)S(1)}, u32[]{:S(2)}, u32[]{:S(2)}) async-start(bf16[8,192,256]{2,1,0:T(8,128)(2,1)} %fusion.3), calls=%async_computation.1 | async-start | bytes 1572864 | tf_op jit(solution)/shard_map/all_to_all | solution.py:191
  98.7 15.2 %collective-permute-start.18 = (bf16[8,192,256]{2,1,0:T(8,128)(2,1)S(1)}, bf16[8,192,256]{2,1,0:T(8,128)(2,1)S(1)}, u32[]{:S(2)}, u32[]{:S(2)}) collective-permute-start(bf16[8,192,256]{2,1,0:T(8,128)(2,1)S(1)} %pad_maximum_fusion.3), channel_id=1, source_target_pairs={{0,24},{8,0},{16,8},{24,16},{1,25},{9,1},{17,9},{25,17},{2,26},{10... | collective-permute-start | bytes 2359304 | tf_op jit(solution)/shard_map/ppermute | solution.py:25
  98.8 16.5 %collective-permute-start.16 = (bf16[8,192,256]{2,1,0:T(8,128)(2,1)S(1)}, bf16[8,192,256]{2,1,0:T(8,128)(2,1)S(1)}, u32[]{:S(2)}, u32[]{:S(2)}) collective-permute-start(bf16[8,192,256]{2,1,0:T(8,128)(2,1)S(1)} %pad_maximum_fusion.2), channel_id=1, source_target_pairs={{0,8},{8,16},{16,24},{24,0},{1,9},{9,17},{17,25},{25,1},{2,10},{10... | collective-permute-start | bytes 2359304 | tf_op jit(solution)/shard_map/ppermute | solution.py:25
  124.9 24.5 %all-to-all-start.1 = ((bf16[8,192,256]{2,1,0:T(8,128)(2,1)}), bf16[8,192,256]{2,1,0:T(8,128)(2,1)S(1)}, u32[]{:S(2)}, u32[]{:S(2)}) async-start(bf16[8,192,256]{2,1,0:T(8,128)(2,1)} %fusion.1), calls=%async_computation.2 | async-start | bytes 1572864 | tf_op jit(solution)/shard_map/all_to_all | solution.py:191
  129.7 5.9 %collective-permute-start.2 = (bf16[192,256]{1,0:T(8,128)(2,1)S(1)}, bf16[192,256]{1,0:T(8,128)(2,1)S(1)}, u32[]{:S(2)}, u32[]{:S(2)}) collective-permute-start(bf16[192,256]{1,0:T(8,128)(2,1)S(1)} %get-tuple-element.28), channel_id=1, source_target_pairs={{0,8},{8,16},{16,24},{24,0},{1,9},{9,17},{17,25},{25,1},{2,10},{10... | collective-permute-start | bytes 294920 | tf_op jit(solution)/shard_map/ppermute | solution.py:25
  131.1 4.9 %collective-permute-start.4 = (bf16[192,256]{1,0:T(8,128)(2,1)S(1)}, bf16[192,256]{1,0:T(8,128)(2,1)S(1)}, u32[]{:S(2)}, u32[]{:S(2)}) collective-permute-start(bf16[192,256]{1,0:T(8,128)(2,1)S(1)} %get-tuple-element.30), channel_id=1, source_target_pairs={{0,24},{8,0},{16,8},{24,16},{1,25},{9,1},{17,9},{25,17},{2,26},{10... | collective-permute-start | bytes 294920 | tf_op jit(solution)/shard_map/ppermute | solution.py:25
  137.0 12.5 %collective-permute-start.5 = (bf16[384,256]{1,0:T(8,128)(2,1)S(1)}, bf16[384,256]{1,0:T(8,128)(2,1)S(1)}, u32[]{:S(2)}, u32[]{:S(2)}) collective-permute-start(bf16[384,256]{1,0:T(8,128)(2,1)S(1)} %pad_maximum_fusion.7), channel_id=1, source_target_pairs={{0,24},{8,0},{16,8},{24,16},{1,25},{9,1},{17,9},{25,17},{2,26},{10... | collective-permute-start | bytes 589832 | tf_op jit(solution)/shard_map/ppermute | solution.py:25
  139.9 9.7 %collective-permute-start.3 = (bf16[384,256]{1,0:T(8,128)(2,1)S(1)}, bf16[384,256]{1,0:T(8,128)(2,1)S(1)}, u32[]{:S(2)}, u32[]{:S(2)}) collective-permute-start(bf16[384,256]{1,0:T(8,128)(2,1)S(1)} %pad_maximum_fusion.6), channel_id=1, source_target_pairs={{0,8},{8,16},{16,24},{24,0},{1,9},{9,17},{17,25},{25,1},{2,10},{10... | collective-permute-start | bytes 589832 | tf_op jit(solution)/shard_map/ppermute | solution.py:25
  150.6 24.6 %copy-start.6 = (f32[1,256]{1,0:T(1,128)S(1)}, f32[1,256]{1,0:T(1,128)}, u32[]{:S(2)}) copy-start(f32[1,256]{1,0:T(1,128)} %param.7) | copy-start | bytes 3076
  150.7 6.7 %collective-permute-start.19 = (bf16[384,256]{1,0:T(8,128)(2,1)S(1)}, bf16[384,256]{1,0:T(8,128)(2,1)S(1)}, u32[]{:S(2)}, u32[]{:S(2)}) collective-permute-start(bf16[384,256]{1,0:T(8,128)(2,1)S(1)} %get-tuple-element.14), channel_id=1, source_target_pairs={{0,192},{1,193},{2,194},{3,195},{4,196},{5,197},{6,198},{7,199},{8... | collective-permute-start | bytes 589832 | tf_op jit(solution)/shard_map/ppermute | solution.py:155
  152.6 5.7 %collective-permute-start.20 = (bf16[384,256]{1,0:T(8,128)(2,1)S(1)}, bf16[384,256]{1,0:T(8,128)(2,1)S(1)}, u32[]{:S(2)}, u32[]{:S(2)}) collective-permute-start(bf16[384,256]{1,0:T(8,128)(2,1)S(1)} %broadcast_select_fusion), channel_id=1, source_target_pairs={{0,128},{1,129},{2,130},{3,131},{4,132},{5,133},{6,134},{7,135},{8... | collective-permute-start | bytes 589832 | tf_op jit(solution)/shard_map/ppermute | solution.py:154
  159.1 16.0 %all-to-all-start.2 = ((f32[32,1,768]{2,1,0:T(1,128)}), f32[32,1,768]{2,1,0:T(1,128)S(1)}, u32[]{:S(2)}, u32[]{:S(2)}) async-start(f32[32,1,768]{2,1,0:T(1,128)} %broadcast_in_dim.9), calls=%async_computation.3 | async-start | bytes 196608 | tf_op jit(solution)/shard_map/all_to_all | solution.py:196
Sparse Core Ops, SparseCore 0:
  28.8 91.8 reduce-scatter.1
